TPU v7x, 32 devices: a whole 2x2x4 slice. The times are simulated.
32 devices in a mesh: expert: 8 (over z, x), fsdp: 4 (over y, core).
Axes of the slice: x: 2, y: 2, z: 4, core: 2. Of those that a mesh axis runs over, the one named last changes fastest.
Arguments:
- hidden_in: bfloat16 [2, 2048, 2048], P(None, ('expert', 'fsdp')), may hold values from -6 to 6
- seg_ids: int32 [2, 2048], P(None, ('expert', 'fsdp')), may hold values from 0 to 63, as said below
- routes: int32 [2, 2048, 4], P(None, ('expert', 'fsdp')), may hold values from 0 to 7, all different within a row; in each aligned block of 64 rows (0 to 63, 64 to 127, ..., all dimensions but the last counted through in order) at most 48 rows name the same one
- out_grad: bfloat16 [2, 2048, 2048], P(None, ('expert', 'fsdp')), may hold values from -6 to 6
- norm_gain1: bfloat16 [2048], P(('expert', 'fsdp')), may hold values from 0.5 to 1.5
- w_query: bfloat16 [2048, 2048], P(('expert', 'fsdp')), may hold values from -0.125 to 0.125
- w_key: bfloat16 [2048, 2048], P(('expert', 'fsdp')), may hold values from -0.125 to 0.125
- w_value: bfloat16 [2048, 2048], P(('expert', 'fsdp')), may hold values from -0.125 to 0.125
- b_qkv: bfloat16 [3, 2048], P(None, ('expert', 'fsdp')), may hold values from -3 to 3
- w_out: bfloat16 [2048, 2048], P(('expert', 'fsdp')), may hold values from -0.375 to 0.375
- norm_gain2: bfloat16 [2048], P(('expert', 'fsdp')), may hold values from 0.5 to 1.5
- w_router: bfloat16 [2048, 8], P(('expert', 'fsdp')), may hold values from -0.0625 to 0.0625
- shared_gate: bfloat16 [2048], P(('expert', 'fsdp')), may hold values from -0.125 to 0.125
- sh_gate: bfloat16 [2048, 5632], P(('expert', 'fsdp')), may hold values from -0.125 to 0.125
- sh_up: bfloat16 [2048, 5632], P(('expert', 'fsdp')), may hold values from -0.125 to 0.125
- sh_down: bfloat16 [2048, 5632], P(('expert', 'fsdp')), may hold values from -0.078125 to 0.078125
- ex_gate: bfloat16 [8, 2048, 1408], P('expert', None, 'fsdp'), may hold values from -0.125 to 0.125
- ex_up: bfloat16 [8, 2048, 1408], P('expert', None, 'fsdp'), may hold values from -0.125 to 0.125
- ex_down: bfloat16 [8, 1408, 2048], P('expert', 'fsdp'), may hold values from -0.625 to 0.625
Outputs:
- hidden_out: bfloat16 [2, 2048, 2048], P(None, ('expert', 'fsdp'))
- hidden_in_grad: float32 [2, 2048, 2048], P(None, ('expert', 'fsdp'))
- gain1_grad: float32 [2048], P(('expert', 'fsdp'))
- query_grad: float32 [2048, 2048], P(('expert', 'fsdp'))
- key_grad: float32 [2048, 2048], P(('expert', 'fsdp'))
- value_grad: float32 [2048, 2048], P(('expert', 'fsdp'))
- bias_grad: float32 [3, 2048], P(None, ('expert', 'fsdp'))
- out_proj_grad: float32 [2048, 2048], P(('expert', 'fsdp'))
- gain2_grad: float32 [2048], P(('expert', 'fsdp'))
- router_grad: float32 [2048, 8], P(('expert', 'fsdp'))
- shared_gate_grad: float32 [2048], P(('expert', 'fsdp'))
- sh_gate_grad: float32 [2048, 5632], P(('expert', 'fsdp'))
- sh_up_grad: float32 [2048, 5632], P(('expert', 'fsdp'))
- sh_down_grad: float32 [2048, 5632], P(('expert', 'fsdp'))
- ex_gate_grad: float32 [8, 2048, 1408], P('expert', None, 'fsdp')
- ex_up_grad: float32 [8, 2048, 1408], P('expert', None, 'fsdp')
- ex_down_grad: float32 [8, 1408, 2048], P('expert', 'fsdp')
Inputs may be any that keep to these rules, and one draw needn't show every extreme that they name: `seg_ids`: within each sequence of 256 tokens the ids start at 0 and rise by 0 or 1 from token to token; in each micro-batch one sequence is a single document, and another reaches the largest id. `routes`: each token names 4 different experts; among the 64 tokens of one device in one micro-batch no expert is named more than 48 times, and some device has an expert named exactly 48 times.
All inputs are finite; a program needn't handle non-finite values.
Results may differ from a plain program's by a relative error of at most 0.015.
Values may be sent and summed in bfloat16 or wider, within the bound.
No kernel may reach another device: no remote copies, remote signals or barrier semaphores. Data moves between devices by JAX's collectives and lax.ppermute only.
A program may use at most 720 MiB of HBM per device.

v0:
```python
import jax
import jax.numpy as jnp
from jax import lax
from jax.sharding import PartitionSpec as P

HEADS = 16
HEAD = 128
SHARED_FF = 5632


EPSILON = 1e-06
ROPE_BASE = 1000000.0
MASKED = -1e30


def normalize(values):
    inverse = lax.rsqrt(jnp.mean(values * values, axis=-1, keepdims=True) + EPSILON)
    return (values * inverse, inverse)


def norm_back(grad_normed, scaled, inverse, gain_vec):
    grad_scaled = grad_normed * gain_vec
    return inverse * (grad_scaled - scaled * jnp.mean(grad_scaled * scaled, axis=-1, keepdims=True))


def angle_tables(first_pos, row_count):
    inverse = 1.0 / ROPE_BASE ** (jnp.arange(0, HEAD, 2).astype(jnp.float32) / HEAD)
    angles = (first_pos + jnp.arange(row_count)).astype(jnp.float32)[:, None] * inverse[None, :]
    return (jnp.cos(angles)[:, None, :], jnp.sin(angles)[:, None, :])


def rotate(values, cosine, sine):
    half_size = values.shape[-1] // 2
    first_half = values[..., :half_size]
    second_half = values[..., half_size:]
    return jnp.concatenate(
        [first_half * cosine - second_half * sine, second_half * cosine + first_half * sine],
        axis=-1,
    )


def unrotate(grads, cosine, sine):
    half_size = grads.shape[-1] // 2
    first_half = grads[..., :half_size]
    second_half = grads[..., half_size:]
    return jnp.concatenate(
        [first_half * cosine + second_half * sine, second_half * cosine - first_half * sine],
        axis=-1,
    )


def silu_parts(pre_act):
    logistic = jax.nn.sigmoid(pre_act)
    return (pre_act * logistic, logistic * (1.0 + pre_act * (1.0 - logistic)))


def product(left_op, right_op):
    return jnp.dot(left_op, right_op, preferred_element_type=jnp.float32)


def contract(pattern, left_op, right_op):
    return jnp.einsum(pattern, left_op, right_op, preferred_element_type=jnp.float32)


def scores_of(queries, keys_all, visible, score_scale):
    raw_scores = contract("qhd,khd->hqk", queries, keys_all) * score_scale
    return jnp.where(visible[None], raw_scores, MASKED)


def fetch_dense(
    norm_gain1,
    w_query,
    w_key,
    w_value,
    b_qkv,
    w_out,
    norm_gain2,
    w_router,
    shared_gate,
    sh_gate,
    sh_up,
    sh_down,
):
    return (
        lax.all_gather(norm_gain1, ("expert", "fsdp"), axis=0, tiled=True),
        lax.all_gather(w_query, ("expert", "fsdp"), axis=0, tiled=True),
        lax.all_gather(w_key, ("expert", "fsdp"), axis=0, tiled=True),
        lax.all_gather(w_value, ("expert", "fsdp"), axis=0, tiled=True),
        lax.all_gather(b_qkv, ("expert", "fsdp"), axis=1, tiled=True),
        lax.all_gather(w_out, ("expert", "fsdp"), axis=0, tiled=True),
        lax.all_gather(norm_gain2, ("expert", "fsdp"), axis=0, tiled=True),
        lax.all_gather(w_router, ("expert", "fsdp"), axis=0, tiled=True),
        lax.all_gather(shared_gate, ("expert", "fsdp"), axis=0, tiled=True),
        lax.all_gather(sh_gate, ("expert", "fsdp"), axis=0, tiled=True),
        lax.all_gather(sh_up, ("expert", "fsdp"), axis=0, tiled=True),
        lax.all_gather(sh_down, ("expert", "fsdp"), axis=0, tiled=True),
    )


def reduce_dense(records):
    joined = [
        jnp.concatenate([record[member_idx] for record in records], axis=0)
        for member_idx in range(9)
    ]
    vectors = records[0][9]
    (
        normed_one,
        grad_qkv,
        attended,
        grad_attn,
        normed_two,
        grad_logits,
        grad_gate_up,
        grad_shared,
        shared_hidden,
    ) = joined
    return lax.psum_scatter(
        jnp.concatenate(
            [
                contract("tr,tc->rc", normed_one, grad_qkv),
                contract("tr,tc->rc", attended, grad_attn),
                contract("tr,tc->rc", normed_two, grad_logits),
                contract("tr,tc->rc", normed_two, grad_gate_up),
                contract("tr,tc->rc", grad_shared, shared_hidden),
                vectors.T,
            ],
            axis=1,
        ),
        ("expert", "fsdp"),
        scatter_dimension=0,
        tiled=True,
    )


def on_device(
    hidden_in,
    seg_ids,
    routes,
    out_grad,
    norm_gain1,
    w_query,
    w_key,
    w_value,
    b_qkv,
    w_out,
    norm_gain2,
    w_router,
    shared_gate,
    sh_gate,
    sh_up,
    sh_down,
    ex_gate,
    ex_up,
    ex_down,
):
    micro_count, tokens_dev, model_width = hidden_in.shape
    top_count = routes.shape[2]
    expert_count = w_router.shape[1]
    capacity = 3 * tokens_dev * top_count // (2 * expert_count)
    fsdp_count = lax.axis_size("fsdp")
    score_scale = HEAD ** (-0.5)
    first_pos = lax.axis_index("fsdp") * tokens_dev
    cosine, sine = angle_tables(first_pos, tokens_dev)
    query_pos = first_pos + jnp.arange(tokens_dev)
    key_pos = jnp.arange(tokens_dev * fsdp_count)
    expert_ids = jnp.arange(expert_count)
    source_tok = jnp.arange(tokens_dev * top_count) // top_count
    gate_local, up_local, down_local = (ex_gate[0], ex_up[0], ex_down[0])
    gate_acc = jnp.zeros(gate_local.shape, jnp.float32)
    up_acc = jnp.zeros(up_local.shape, jnp.float32)
    down_acc = jnp.zeros(down_local.shape, jnp.float32)
    outputs = []
    in_grads = []
    totals = None
    for micro_idx in range(micro_count):
        dense = fetch_dense(
            norm_gain1,
            w_query,
            w_key,
            w_value,
            b_qkv,
            w_out,
            norm_gain2,
            w_router,
            shared_gate,
            sh_gate,
            sh_up,
            sh_down,
        )
        (
            gain_one,
            wq_full,
            wk_full,
            wv_full,
            bias_full,
            wo_full,
            gain_two,
            router_w,
            shared_col,
            shgate_w,
            shup_w,
            shdown_w,
        ) = dense
        gain_one_f = gain_one.astype(jnp.float32)
        gain_two_f = gain_two.astype(jnp.float32)
        bias_f = bias_full.astype(jnp.float32)
        seg_local = seg_ids[micro_idx]
        route_local = routes[micro_idx]
        residual = hidden_in[micro_idx].astype(jnp.float32)
        scaled_one, inverse_one = normalize(residual)
        normed_one = (scaled_one * gain_one_f).astype(jnp.bfloat16)
        query_lin = product(normed_one, wq_full) + bias_f[0]
        key_lin = product(normed_one, wk_full) + bias_f[1]
        value_lin = product(normed_one, wv_full) + bias_f[2]
        queries = rotate(query_lin.reshape(tokens_dev, HEADS, HEAD), cosine, sine).astype(
            jnp.bfloat16
        )
        keys_own = (
            rotate(key_lin.reshape(tokens_dev, HEADS, HEAD), cosine, sine)
            .astype(jnp.bfloat16)
            .reshape(tokens_dev, model_width)
        )
        values_own = value_lin.astype(jnp.bfloat16)
        keys_all, values_all, seg_all = (
            lax.all_gather(keys_own, "fsdp", axis=0, tiled=True),
            lax.all_gather(values_own, "fsdp", axis=0, tiled=True),
            lax.all_gather(seg_local, "fsdp", axis=0, tiled=True),
        )
        keys_all = keys_all.reshape(-1, HEADS, HEAD)
        values_all = values_all.reshape(-1, HEADS, HEAD)
        visible = (key_pos[None, :] <= query_pos[:, None]) & (
            seg_all[None, :] == seg_local[:, None]
        )
        scores = scores_of(queries, keys_all, visible, score_scale)
        peak = jnp.max(scores, axis=-1, keepdims=True)
        exp_scores = jnp.exp(scores - peak)
        row_total = jnp.sum(exp_scores, axis=-1, keepdims=True)
        attn_probs = exp_scores / row_total
        log_total = peak + jnp.log(row_total)
        attended = (
            contract("hqk,khd->qhd", attn_probs.astype(jnp.bfloat16), values_all)
            .reshape(tokens_dev, model_width)
            .astype(jnp.bfloat16)
        )
        after_attn = residual + product(attended, wo_full)
        scaled_two, inverse_two = normalize(after_attn)
        normed_two = (scaled_two * gain_two_f).astype(jnp.bfloat16)
        router_cat = jnp.concatenate([router_w, shared_col[:, None]], axis=1)
        logits = product(normed_two, router_cat)
        router_probs = jax.nn.softmax(logits[:, :expert_count], axis=-1)
        shared_scale = jax.nn.sigmoid(logits[:, expert_count])
        gate_lin = product(normed_two, shgate_w)
        up_lin = product(normed_two, shup_w)
        sh_act, sh_slope = silu_parts(gate_lin)
        shared_hidden = (sh_act * up_lin).astype(jnp.bfloat16)
        shared_out = contract("tf,df->td", shared_hidden, shdown_w)
        flat_route = route_local.reshape(-1)
        onehot_int = (flat_route[:, None] == expert_ids[None, :]).astype(jnp.int32)
        earlier = jnp.cumsum(onehot_int, axis=0) - onehot_int
        slot_idx = jnp.sum(earlier * onehot_int, axis=1)
        target = flat_route * capacity + slot_idx
        outgoing = (
            jnp.zeros((expert_count * capacity, model_width), jnp.bfloat16)
            .at[target]
            .set(normed_two[source_tok])
        )
        incoming = lax.all_to_all(
            outgoing.reshape(expert_count, capacity, model_width),
            "expert",
            split_axis=0,
            concat_axis=0,
            tiled=True,
        )
        rows_in = lax.all_gather(incoming, "fsdp", axis=0, tiled=True).reshape(-1, model_width)
        gate_e = product(rows_in, gate_local)
        up_e = product(rows_in, up_local)
        act_e, slope_e = silu_parts(gate_e)
        hidden_e = (act_e * up_e).astype(jnp.bfloat16)
        partial_out = product(hidden_e, down_local)
        summed = lax.psum_scatter(
            partial_out.reshape(-1, capacity, model_width), "fsdp", scatter_dimension=0, tiled=True
        )
        returned = lax.all_to_all(
            summed.astype(jnp.bfloat16), "expert", split_axis=0, concat_axis=0, tiled=True
        ).reshape(-1, model_width)
        results = returned[target].astype(jnp.float32).reshape(tokens_dev, top_count, model_width)
        route_hot = (route_local[:, :, None] == expert_ids[None, None, :]).astype(jnp.float32)
        gates = jnp.sum(route_hot * router_probs[:, None, :], axis=2)
        routed = jnp.sum(gates[:, :, None] * results, axis=1)
        outputs.append(
            (after_attn + shared_scale[:, None] * shared_out + routed).astype(jnp.bfloat16)
        )
        grad_out = out_grad[micro_idx].astype(jnp.float32)
        grad_gates = jnp.sum(grad_out[:, None, :] * results, axis=2)
        grad_results = (
            (gates[:, :, None] * grad_out[:, None, :]).astype(jnp.bfloat16).reshape(-1, model_width)
        )
        grad_outgoing = (
            jnp.zeros((expert_count * capacity, model_width), jnp.bfloat16)
            .at[target]
            .set(grad_results)
        )
        grad_incoming = lax.all_to_all(
            grad_outgoing.reshape(expert_count, capacity, model_width),
            "expert",
            split_axis=0,
            concat_axis=0,
            tiled=True,
        )
        grad_rows = lax.all_gather(grad_incoming, "fsdp", axis=0, tiled=True).reshape(
            -1, model_width
        )
        grad_hidden_e = contract("rd,fd->rf", grad_rows, down_local)
        down_acc = down_acc + contract("rf,rd->fd", hidden_e, grad_rows)
        grad_gate_e = (grad_hidden_e * up_e * slope_e).astype(jnp.bfloat16)
        grad_up_e = (grad_hidden_e * act_e).astype(jnp.bfloat16)
        gate_acc = gate_acc + contract("rd,rf->df", rows_in, grad_gate_e)
        up_acc = up_acc + contract("rd,rf->df", rows_in, grad_up_e)
        row_grads = contract("rf,df->rd", grad_gate_e, gate_local) + contract(
            "rf,df->rd", grad_up_e, up_local
        )
        row_sums = lax.psum_scatter(
            row_grads.reshape(-1, capacity, model_width), "fsdp", scatter_dimension=0, tiled=True
        )
        grad_back = lax.all_to_all(
            row_sums.astype(jnp.bfloat16), "expert", split_axis=0, concat_axis=0, tiled=True
        ).reshape(-1, model_width)
        grad_normed_two = jnp.sum(
            grad_back[target].astype(jnp.float32).reshape(tokens_dev, top_count, model_width),
            axis=1,
        )
        grad_shared = (shared_scale[:, None] * grad_out).astype(jnp.bfloat16)
        grad_sh_hidden = product(grad_shared, shdown_w)
        grad_sh_gate = (grad_sh_hidden * up_lin * sh_slope).astype(jnp.bfloat16)
        grad_sh_up = (grad_sh_hidden * sh_act).astype(jnp.bfloat16)
        grad_probs = jnp.sum(grad_gates[:, :, None] * route_hot, axis=1)
        grad_router = router_probs * (
            grad_probs - jnp.sum(router_probs * grad_probs, axis=-1, keepdims=True)
        )
        grad_scale_lin = (
            jnp.sum(grad_out * shared_out, axis=-1) * shared_scale * (1.0 - shared_scale)
        )
        grad_logits = jnp.concatenate([grad_router, grad_scale_lin[:, None]], axis=1).astype(
            jnp.bfloat16
        )
        grad_normed_two = (
            grad_normed_two
            + contract("tc,dc->td", grad_logits, router_cat)
            + contract("tf,df->td", grad_sh_gate, shgate_w)
            + contract("tf,df->td", grad_sh_up, shup_w)
        )
        grad_after = grad_out + norm_back(grad_normed_two, scaled_two, inverse_two, gain_two_f)
        gain_two_sum = jnp.sum(grad_normed_two * scaled_two, axis=0)
        grad_attn = grad_after.astype(jnp.bfloat16)
        grad_attended = (
            contract("te,de->td", grad_attn, wo_full)
            .astype(jnp.bfloat16)
            .reshape(tokens_dev, HEADS, HEAD)
        )
        again_probs = jnp.exp(scores_of(queries, keys_all, visible, score_scale) - log_total)
        grad_probs_attn = contract("qhd,khd->hqk", grad_attended, values_all)
        grad_values = contract("hqk,qhd->khd", again_probs.astype(jnp.bfloat16), grad_attended)
        grad_scores = (
            again_probs
            * (grad_probs_attn - jnp.sum(again_probs * grad_probs_attn, axis=-1, keepdims=True))
        ).astype(jnp.bfloat16)
        grad_queries = contract("hqk,khd->qhd", grad_scores, keys_all) * score_scale
        grad_keys = contract("hqk,qhd->khd", grad_scores, queries) * score_scale
        grad_keys_own, grad_values_own = (
            lax.psum_scatter(
                grad_keys.reshape(-1, model_width).astype(jnp.bfloat16),
                "fsdp",
                scatter_dimension=0,
                tiled=True,
            ).astype(jnp.float32),
            lax.psum_scatter(
                grad_values.reshape(-1, model_width).astype(jnp.bfloat16),
                "fsdp",
                scatter_dimension=0,
                tiled=True,
            ).astype(jnp.float32),
        )
        grad_query_lin = (
            unrotate(grad_queries, cosine, sine)
            .reshape(tokens_dev, model_width)
            .astype(jnp.bfloat16)
        )
        grad_key_lin = (
            unrotate(grad_keys_own.reshape(tokens_dev, HEADS, HEAD), cosine, sine)
            .reshape(tokens_dev, model_width)
            .astype(jnp.bfloat16)
        )
        grad_value_lin = grad_values_own.astype(jnp.bfloat16)
        grad_normed_one = (
            contract("te,de->td", grad_query_lin, wq_full)
            + contract("te,de->td", grad_key_lin, wk_full)
            + contract("te,de->td", grad_value_lin, wv_full)
        )
        in_grads.append(
            grad_after + norm_back(grad_normed_one, scaled_one, inverse_one, gain_one_f)
        )
        gain_one_sum = jnp.sum(grad_normed_one * scaled_one, axis=0)
        vectors = jnp.stack(
            [
                jnp.sum(grad_query_lin.astype(jnp.float32), axis=0),
                jnp.sum(grad_key_lin.astype(jnp.float32), axis=0),
                jnp.sum(grad_value_lin.astype(jnp.float32), axis=0),
                gain_one_sum,
                gain_two_sum,
            ]
        )
        record = (
            normed_one,
            jnp.concatenate([grad_query_lin, grad_key_lin, grad_value_lin], axis=1),
            attended,
            grad_attn,
            normed_two,
            grad_logits,
            jnp.concatenate([grad_sh_gate, grad_sh_up], axis=1),
            grad_shared,
            shared_hidden,
            vectors,
        )
        panel = reduce_dense([record])
        totals = panel if totals is None else totals + panel
    col_qkv = 3 * model_width
    col_out = col_qkv + model_width
    col_route = col_out + expert_count
    col_gate = col_route + 1
    col_up = col_gate + SHARED_FF
    col_down = col_up + SHARED_FF
    col_vec = col_down + SHARED_FF
    vec_part = totals[:, col_vec : col_vec + 5]
    return (
        jnp.stack(outputs),
        jnp.stack(in_grads),
        vec_part[:, 3],
        totals[:, 0:model_width],
        totals[:, model_width : 2 * model_width],
        totals[:, 2 * model_width : col_qkv],
        vec_part[:, 0:3].T,
        totals[:, col_qkv:col_out],
        vec_part[:, 4],
        totals[:, col_out:col_route],
        totals[:, col_route],
        totals[:, col_gate:col_up],
        totals[:, col_up:col_down],
        totals[:, col_down:col_vec],
        gate_acc[None],
        up_acc[None],
        down_acc[None],
    )


def solution(mesh):
    in_specs = (
        P(None, ("expert", "fsdp"), None),
        P(None, ("expert", "fsdp")),
        P(None, ("expert", "fsdp"), None),
        P(None, ("expert", "fsdp"), None),
        P(("expert", "fsdp")),
        P(("expert", "fsdp"), None),
        P(("expert", "fsdp"), None),
        P(("expert", "fsdp"), None),
        P(None, ("expert", "fsdp")),
        P(("expert", "fsdp"), None),
        P(("expert", "fsdp")),
        P(("expert", "fsdp"), None),
        P(("expert", "fsdp")),
        P(("expert", "fsdp"), None),
        P(("expert", "fsdp"), None),
        P(("expert", "fsdp"), None),
        P("expert", None, "fsdp"),
        P("expert", None, "fsdp"),
        P("expert", "fsdp", None),
    )
    out_specs = (
        P(None, ("expert", "fsdp"), None),
        P(None, ("expert", "fsdp"), None),
        P(("expert", "fsdp")),
        P(("expert", "fsdp"), None),
        P(("expert", "fsdp"), None),
        P(("expert", "fsdp"), None),
        P(None, ("expert", "fsdp")),
        P(("expert", "fsdp"), None),
        P(("expert", "fsdp")),
        P(("expert", "fsdp"), None),
        P(("expert", "fsdp")),
        P(("expert", "fsdp"), None),
        P(("expert", "fsdp"), None),
        P(("expert", "fsdp"), None),
        P("expert", None, "fsdp"),
        P("expert", None, "fsdp"),
        P("expert", "fsdp", None),
    )
    return jax.shard_map(
        on_device, mesh=mesh, in_specs=in_specs, out_specs=out_specs, check_vma=False
    )
```

profile of v0, /device:TPU:0, one launch (start us, length us, event | category | flops | bytes accessed | tf_op | source)
XLA Modules:
  0.0 4738.5 jit_solution(16723372700636690293)
XLA Ops:
  12.0 42.7 all-reduce.6
  54.8 41.1 all-gather.2
  106.1 64.6 %all-gather.24.cloned.1.call-done = bf16[2048,2048]{1,0:T(8,128)(2,1)} async-done(((bf16[64,2048]{1,0:T(8,128)(2,1)}), bf16[2048,2048]{1,0:T(8,128)(2,1)}) %all-gather.24.cloned.1.call-update) | async-done | bytes 8388624 | tf_op jit(solution)/shard_map/all_gather | solution.py:86
  183.4 66.3 %all-gather.20.cloned.1.call-done = bf16[2048,2048]{1,0:T(8,128)(2,1)} async-done(((bf16[64,2048]{1,0:T(8,128)(2,1)}), bf16[2048,2048]{1,0:T(8,128)(2,1)}) %all-gather.20.cloned.1.call-update) | async-done | bytes 8388624 | tf_op jit(solution)/shard_map/all_gather | solution.py:88
  306.4 78.7 %all-gather.30.cloned.1.call-done = bf16[2048,2048]{1,0:T(8,128)(2,1)} async-done(((bf16[64,2048]{1,0:T(8,128)(2,1)}), bf16[2048,2048]{1,0:T(8,128)(2,1)}) %all-gather.30.cloned.1.call-update) | async-done | bytes 8388624 | tf_op jit(solution)/shard_map/all_gather | solution.py:90
  417.3 43.1 all_to_all.40
  460.5 39.9 all-gather.3
  512.8 42.1 all_to_all.41
  563.3 41.3 all_to_all.42
  615.0 40.4 all_to_all.43
  745.5 102.1 %all-gather.32.cloned.1.call-done = bf16[2048,5632]{1,0:T(8,128)(2,1)} async-done(((bf16[64,5632]{1,0:T(8,128)(2,1)}), bf16[2048,5632]{1,0:T(8,128)(2,1)}) %all-gather.32.cloned.1.call-update) | async-done | bytes 23068688 | tf_op jit(solution)/shard_map/all_gather | solution.py:94
  867.0 126.1 %all-gather.34.cloned.1.call-done = bf16[2048,5632]{1,0:T(8,128)(2,1)} async-done(((bf16[64,5632]{1,0:T(8,128)(2,1)}), bf16[2048,5632]{1,0:T(8,128)(2,1)}) %all-gather.34.cloned.1.call-update) | async-done | bytes 23068688 | tf_op jit(solution)/shard_map/all_gather | solution.py:95
  1007.3 85.6 %reduce-scatter.10.cloned.1.call-done = f32[8,48,2048]{2,1,0:T(8,128)} async-done(((f32[32,48,2048]{2,1,0:T(8,128)}), f32[8,48,2048]{2,1,0:T(8,128)}) %reduce-scatter.10.cloned.1.call-update) | async-done | bytes 3145744 | tf_op jit(solution)/shard_map/reduce_scatter | solution.py:280
  1116.1 146.8 %all-gather.36.cloned.1.call-done = bf16[2048,5632]{1,0:T(8,128)(2,1)} async-done(((bf16[64,5632]{1,0:T(8,128)(2,1)}), bf16[2048,5632]{1,0:T(8,128)(2,1)}) %all-gather.36.cloned.1.call-update) | async-done | bytes 23068688 | tf_op jit(solution)/shard_map/all_gather | solution.py:96
  1276.0 86.6 %reduce-scatter.12.cloned.1.call-done = f32[8,48,2048]{2,1,0:T(8,128)} async-done(((f32[32,48,2048]{2,1,0:T(8,128)}), f32[8,48,2048]{2,1,0:T(8,128)}) %reduce-scatter.12.cloned.1.call-update) | async-done | bytes 3145744 | tf_op jit(solution)/shard_map/reduce_scatter | solution.py:280
  1404.7 59.5 %reduce-scatter.20.cloned.1.call-done = f32[8,48,2048]{2,1,0:T(8,128)} async-done(((f32[32,48,2048]{2,1,0:T(8,128)}), f32[8,48,2048]{2,1,0:T(8,128)}) %reduce-scatter.20.cloned.1.call-update) | async-done | bytes 3145744 | tf_op jit(solution)/shard_map/reduce_scatter | solution.py:322
  1473.4 38.6 fusion.4
  1526.5 39.3 reduce-scatter.14.cloned.1.call-done
  1575.0 32.8 fusion.8
  1741.6 19.7 fusion.142
  1859.5 249.0 %concatenate.71 = f32[2048,25102]{1,0:T(8,128)} concatenate(f32[2048,6144]{1,0:T(8,128)} %fusion.70, f32[2048,2048]{1,0:T(8,128)} %fusion.123, f32[2048,9]{1,0:T(8,128)S(1)} %copy-done.53, f32[2048,11264]{1,0:T(8,128)} %fusion.4, f32[2048,5632]{1,0:T(8,128)} %fusion.142, f32[2048,5]{1,0:T(8,128)S(1)} %bitcast.439), dimensions={1} | concatenate | bytes 411271168 | tf_op jit(solution)/shard_map/concatenate | solution.py:118
  2128.0 249.0 %concatenate.74 = f32[2048,25102]{1,0:T(8,128)} concatenate(f32[2048,6144]{1,0:T(8,128)} %fusion.76, f32[2048,2048]{1,0:T(8,128)} %fusion.120, f32[2048,9]{1,0:T(8,128)S(1)} %copy-done.54, f32[2048,11264]{1,0:T(8,128)} %fusion.8, f32[2048,5632]{1,0:T(8,128)} %fusion.144, f32[2048,5]{1,0:T(8,128)S(1)} %bitcast.440), dimensions={1} | concatenate | bytes 411271168 | tf_op jit(solution)/shard_map/concatenate | solution.py:118
  2377.0 194.7 %add.403 = f32[2048,25102]{1,0:T(8,128)} add(f32[2048,25102]{1,0:T(8,128)} %concatenate.71, f32[2048,25102]{1,0:T(8,128)} %concatenate.74) | non-fusion elementwise | flops 51408896 | bytes 616906752 | tf_op jit(solution)/shard_map/add | solution.py:425
  2598.3 2120.2 %reduce-scatter.26.cloned.1.call-done = f32[64,25102]{1,0:T(8,128)} async-done(((f32[2048,25102]{1,0:T(8,128)}), f32[64,25102]{1,0:T(8,128)}) %reduce-scatter.26.cloned.1.call-update) | async-done | bytes 6426128 | tf_op jit(solution)/shard_map/reduce_scatter | solution.py:117
  (644 shorter events, 670.7 us)
Async XLA Ops:
  7.2 90.9 %all-gather.26.cloned.1.call-start = ((), (), s32[]{:S(2)}) async-start(), calls=%async_computation.20 | async-start | bytes 8650752 | tf_op jit(solution)/shard_map/all_gather | solution.py:87
  7.9 162.7 %all-gather.24.cloned.1.call-start = ((), (), s32[]{:S(2)}) async-start(), calls=%async_computation.19 | async-start | bytes 8650752 | tf_op jit(solution)/shard_map/all_gather | solution.py:86
  8.7 241.0 %all-gather.20.cloned.1.call-start = ((), (), s32[]{:S(2)}) async-start(), calls=%async_computation.17 | async-start | bytes 8650752 | tf_op jit(solution)/shard_map/all_gather | solution.py:88
  9.4 263.3 %all-gather.42.cloned.1.call-start = ((), (), s32[]{:S(2)}) async-start(), calls=%async_computation.29 | async-start | bytes 1310720 | tf_op jit(solution)/shard_map/all_gather | solution.py:225
  182.4 103.5 %all-gather.28.cloned.1.call-start = ((), (), s32[]{:S(2)}) async-start(), calls=%async_computation.21 | async-start | bytes 1310720 | tf_op jit(solution)/shard_map/all_gather | solution.py:225
  183.3 121.4 %all-gather.40.cloned.1.call-start = ((), (), s32[]{:S(2)}) async-start(), calls=%async_computation.28 | async-start | bytes 1310720 | tf_op jit(solution)/shard_map/all_gather | solution.py:226
  255.5 129.6 %all-gather.30.cloned.1.call-start = ((), (), s32[]{:S(2)}) async-start(), calls=%async_computation.22 | async-start | bytes 8650752 | tf_op jit(solution)/shard_map/all_gather | solution.py:90
  256.3 146.4 %all-gather.22.cloned.1.call-start = ((), (), s32[]{:S(2)}) async-start(), calls=%async_computation.18 | async-start | bytes 1310720 | tf_op jit(solution)/shard_map/all_gather | solution.py:226
  272.6 384.3 %all-gather.38.cloned.1.call-start = ((), (), s32[]{:S(2)}) async-start(), calls=%async_computation.26 | async-start | bytes 7864320 | tf_op jit(solution)/shard_map/all_gather | solution.py:274
  460.4 207.7 %all-gather.46.cloned.1.call-start = ((), (), s32[]{:S(2)}) async-start(), calls=%async_computation.32 | async-start | bytes 7864320 | tf_op jit(solution)/shard_map/all_gather | solution.py:310
  554.9 133.3 %all-gather.44.cloned.1.call-start = ((), (), s32[]{:S(2)}) async-start(), calls=%async_computation.30 | async-start | bytes 7864320 | tf_op jit(solution)/shard_map/all_gather | solution.py:274
  604.6 95.4 %all-gather.48.cloned.1.call-start = ((), (), s32[]{:S(2)}) async-start(), calls=%async_computation.36 | async-start | bytes 7864320 | tf_op jit(solution)/shard_map/all_gather | solution.py:310
  655.5 192.1 %all-gather.32.cloned.1.call-start = ((), (), s32[]{:S(2)}) async-start(), calls=%async_computation.23 | async-start | bytes 23789568 | tf_op jit(solution)/shard_map/all_gather | solution.py:94
  656.3 336.9 %all-gather.34.cloned.1.call-start = ((), (), s32[]{:S(2)}) async-start(), calls=%async_computation.24 | async-start | bytes 23789568 | tf_op jit(solution)/shard_map/all_gather | solution.py:95
  656.8 436.0 %reduce-scatter.10.cloned.1.call-start = ((), (), s32[]{:S(2)}) async-start(), calls=%async_computation.27 | async-start | bytes 15728640 | tf_op jit(solution)/shard_map/reduce_scatter | solution.py:280
  687.1 575.7 %all-gather.36.cloned.1.call-start = ((), (), s32[]{:S(2)}) async-start(), calls=%async_computation.25 | async-start | bytes 23789568 | tf_op jit(solution)/shard_map/all_gather | solution.py:96
  687.7 674.9 %reduce-scatter.12.cloned.1.call-start = ((), (), s32[]{:S(2)}) async-start(), calls=%async_computation.31 | async-start | bytes 15728640 | tf_op jit(solution)/shard_map/reduce_scatter | solution.py:280
  719.1 745.1 %reduce-scatter.20.cloned.1.call-start = ((), (), s32[]{:S(2)}) async-start(), calls=%async_computation.37 | async-start | bytes 15728640 | tf_op jit(solution)/shard_map/reduce_scatter | solution.py:322
  731.0 834.8 %reduce-scatter.14.cloned.1.call-start = ((), (), s32[]{:S(2)}) async-start(), calls=%async_computation.33 | async-start | bytes 15728640 | tf_op jit(solution)/shard_map/reduce_scatter | solution.py:322
  1096.1 269.7 %all-to-all-start.1 = ((bf16[8,48,2048]{2,1,0:T(8,128)(2,1)}), bf16[8,48,2048]{2,1,0:T(8,128)(2,1)S(1)}, u32[]{:S(2)}, u32[]{:S(2)}) async-start(bf16[8,48,2048]{2,1,0:T(8,128)(2,1)} %convert_element_type.369), calls=%async_computation.2 | async-start | bytes 3145728 | tf_op jit(solution)/shard_map/all_to_all | solution.py:283
  1365.9 101.5 %all-to-all-start.3 = ((bf16[8,48,2048]{2,1,0:T(8,128)(2,1)}), bf16[8,48,2048]{2,1,0:T(8,128)(2,1)}, u32[]{:S(2)}, u32[]{:S(2)}) async-start(bf16[8,48,2048]{2,1,0:T(8,128)(2,1)} %convert_element_type.387), calls=%async_computation.5 | async-start | bytes 3145728 | tf_op jit(solution)/shard_map/all_to_all | solution.py:283
  1467.4 101.7 %all-to-all-start.7 = ((bf16[8,48,2048]{2,1,0:T(8,128)(2,1)}), bf16[8,48,2048]{2,1,0:T(8,128)(2,1)}, u32[]{:S(2)}, u32[]{:S(2)}) async-start(bf16[8,48,2048]{2,1,0:T(8,128)(2,1)} %convert_element_type.421), calls=%async_computation.13 | async-start | bytes 3145728 | tf_op jit(solution)/shard_map/all_to_all | solution.py:325
  1574.7 217.0 %reduce-scatter.16.cloned.1.call-start = ((), (), s32[]{:S(2)}) async-start(), calls=%async_computation.34 | async-start | bytes 1310720 | tf_op jit(solution)/shard_map/reduce_scatter | solution.py:370
  1791.3 2927.1 %reduce-scatter.26.cloned.1.call-start = ((), (), s32[]{:S(2)}) async-start(), calls=%async_computation.40 | async-start | bytes 213024768 | tf_op jit(solution)/shard_map/reduce_scatter | solution.py:117
  (171 other events, 5831.2 us)
Sparse Core Ops, SparseCore 0:
  10.9 80.6 all-gather.25
  94.4 76.1 all-gather.23
  173.5 76.1 all-gather.19
  251.7 15.3 all-gather.41
  269.1 16.7 all-gather.27
  287.9 16.7 all-gather.39
  307.6 77.5 all-gather.29
  387.3 15.3 all-gather.21
  460.5 45.0 all-gather.37
  555.0 44.4 all-gather.45
  604.8 44.4 all-gather.43
  655.6 44.4 all-gather.47
  703.0 144.5 all-gather.31
  850.3 142.7 all-gather.33
  995.6 97.2 reduce-scatter.9
  1095.6 167.2 all-gather.35
  1265.3 97.2 reduce-scatter.11
  1365.1 99.0 reduce-scatter.19
  1466.7 99.0 reduce-scatter.13
  1710.7 25.3 reduce-scatter.15
  1741.6 25.3 reduce-scatter.21
  1770.4 25.2 reduce-scatter.17
  1799.0 24.9 reduce-scatter.23
  2571.9 2146.4 reduce-scatter.25
where the time goes:
time: 4770 us; the launch traced here: 4740 us
  waiting for transfers between devices  3020 us (63%)
  local copies, waits for them, and re-layouts  600 us (13%)
  matrix products  521 us (11%)
  blocking collectives  296 us (6%)
  other arithmetic  260 us (5%)
    reduce_scatter x1, waiting for transfers between devices, reduce_dense(): lax.psum_scatter(jnp.concatenate([contract('tr,tc->rc', normed_one, grad_...  2120 us
    concatenate x2, local copies, waits for them, and re-layouts, reduce_dense(): jnp.concatenate([contract('tr,tc->rc', normed_one, grad_qkv), contract('t...  498 us
    dot_general x50, matrix products, contract(): jnp.einsum(pattern, left_op, right_op, preferred_element_type=jnp.float32)  374 us
    add x1, other arithmetic, on_device(): totals = panel if totals is None else totals + panel  195 us
    reduce_scatter x2, waiting for transfers between devices, on_device(): lax.psum_scatter(partial_out.reshape(-1, capacity, model_width), 'fsdp',...  172 us
    all_gather x1, waiting for transfers between devices, fetch_dense(): lax.all_gather(sh_down, ('expert', 'fsdp'), axis=0, tiled=True)  147 us
    dot_general x22, matrix products, product(): return jnp.dot(left_op, right_op, preferred_element_type=jnp.float32)  146 us
    all_gather x1, waiting for transfers between devices, fetch_dense(): lax.all_gather(sh_up, ('expert', 'fsdp'), axis=0, tiled=True)  126 us
  transfers between devices with their start and end apart: 28, of which 16 were waited for; matrix products, arithmetic and copies ran while one was open for 11% of the time, Pallas kernels for 0%

commit v1 on v0

v1 whole, which is shorter than its diff:
```python
import functools

import jax
import jax.numpy as jnp
from jax import lax
from jax.experimental import pallas as pl
from jax.experimental.pallas import tpu as pltpu
from jax.sharding import PartitionSpec as P

HEADS = 16
HEAD = 128
SHARED_FF = 5632
EPSILON = 1e-06
ROPE_BASE = 1000000.0
MASKED = -1e30
ALL = ("expert", "fsdp")
BF = jnp.bfloat16
F32 = jnp.float32
LANES = 128
TILE = 256


def normalize(values):
    inverse = lax.rsqrt(jnp.mean(values * values, axis=-1, keepdims=True) + EPSILON)
    return (values * inverse, inverse)


def norm_back(grad_normed, scaled, inverse, gain_vec):
    grad_scaled = grad_normed * gain_vec
    return inverse * (grad_scaled - scaled * jnp.mean(grad_scaled * scaled, axis=-1, keepdims=True))


def angle_tables(places):
    inverse = 1.0 / ROPE_BASE ** (jnp.arange(0, HEAD, 2).astype(F32) / HEAD)
    angles = places.astype(F32)[:, None] * inverse[None, :]
    cosine, sine = jnp.cos(angles), jnp.sin(angles)
    return jnp.concatenate([cosine, cosine], axis=1), jnp.concatenate([-sine, sine], axis=1)


def silu_parts(pre_act):
    logistic = 1.0 / (1.0 + jnp.exp(-pre_act))
    return (pre_act * logistic, logistic * (1.0 + pre_act * (1.0 - logistic)))


def contract(pattern, left_op, right_op):
    return jnp.einsum(pattern, left_op, right_op, preferred_element_type=F32)


def dot_nt(left_op, right_op):
    return lax.dot_general(left_op, right_op, (((1,), (1,)), ((), ())), preferred_element_type=F32)


def dot_nn(left_op, right_op):
    return lax.dot_general(left_op, right_op, (((1,), (0,)), ((), ())), preferred_element_type=F32)


def dot_tn(left_op, right_op):
    return lax.dot_general(left_op, right_op, (((0,), (0,)), ((), ())), preferred_element_type=F32)


def after(value, *earlier):
    return lax.optimization_barrier((value, earlier))[0]


def partner_perm(n_exp, n_fsdp, bit):
    return [(e * n_fsdp + f, e * n_fsdp + (f ^ bit)) for e in range(n_exp) for f in range(n_fsdp)]


def expert_perm(n_exp, n_fsdp, move):
    return [(e * n_fsdp + f, move(e) * n_fsdp + f) for e in range(n_exp) for f in range(n_fsdp)]


class Links:
    def __init__(self):
        self.n_exp = lax.axis_size("expert")
        self.n_fsdp = lax.axis_size("fsdp")
        self.my_exp = lax.axis_index("expert")
        self.my_fsdp = lax.axis_index("fsdp")
        self.n_all = self.n_exp * self.n_fsdp
        self.ring = self.n_exp == 8

    def partner(self, value, bit):
        return lax.ppermute(value, ALL, partner_perm(self.n_exp, self.n_fsdp, bit))

    def pair(self, value):
        return lax.ppermute(value, ALL, expert_perm(self.n_exp, self.n_fsdp, lambda e: e ^ 1))

    def forward(self, value):
        return lax.ppermute(value, ALL, expert_perm(self.n_exp, self.n_fsdp, lambda e: (e + 2) % 8))

    def slot(self, step, other):
        z = lax.rem(self.my_exp // 2 + 4 - step, 4)
        x = lax.rem(self.my_exp, 2)
        return z * 2 + (1 - x if other else x)

    def ring_gather(self, value):
        parts, current = [], value
        for step in range(4):
            following = self.forward(current) if step < 3 else None
            parts.append([current, self.pair(current)])
            current = following
        return parts

    def ring_sum(self, parts, kind=BF):
        arriving = None
        for step in (1, 2, 3, 0):
            own, other = parts(step)
            total = own.astype(F32) + self.pair(other.astype(kind)).astype(F32)
            if arriving is not None:
                total = total + arriving.astype(F32)
            arriving = self.forward(total.astype(kind)) if step else None
        return total

    def gather_rows(self, value):
        if not self.ring:
            return lax.all_gather(value, "expert", axis=0)
        parts = self.ring_gather(value)
        full = jnp.zeros((8,) + value.shape, value.dtype)
        for step in range(4):
            for other in range(2):
                full = lax.dynamic_update_index_in_dim(full, parts[step][other], self.slot(step, other), 0)
        return full

    def sum_rows(self, value, kind=BF):
        if not self.ring:
            return lax.psum_scatter(value.astype(kind), "expert", scatter_dimension=0).astype(F32)

        def parts(step):
            return [
                lax.dynamic_index_in_dim(value, self.slot(step, other), 0, keepdims=False) for other in range(2)
            ]

        return self.ring_sum(parts, kind)

    def swap_fsdp(self, value):
        mine = lax.dynamic_index_in_dim(value, self.my_fsdp, 0, keepdims=False)
        result = lax.dynamic_update_index_in_dim(value, mine, self.my_fsdp, 0)
        for bit in range(1, self.n_fsdp):
            other = lax.bitwise_xor(self.my_fsdp, bit)
            block = lax.dynamic_index_in_dim(value, other, 0, keepdims=False)
            result = lax.dynamic_update_index_in_dim(result, self.partner(block, bit), other, 0)
        return result

    def gather_four(self, value):
        far = self.partner(value, 2)
        return [value, self.partner(value, 1), far, self.partner(far, 1)]

    def gather_seq(self, value):
        return jnp.concatenate(self.gather_four(value), axis=1)

    def sum_four(self, parts, kind=BF):
        far = (parts[2].astype(F32) + self.partner(parts[3].astype(kind), 1).astype(F32)).astype(kind)
        near = parts[0].astype(F32) + self.partner(parts[1].astype(kind), 1).astype(F32)
        return near + self.partner(far, 2).astype(F32)

    def gather_small(self, value):
        rows, columns = value.shape
        if not self.ring:
            full = lax.all_gather(value, ALL, axis=0)
        else:
            four = jnp.stack(self.gather_four(value.reshape(rows * columns)))
            parts = self.ring_gather(four)
            blocks = jnp.concatenate([parts[step][other] for step in range(4) for other in range(2)])
            places = jnp.stack([self.slot(step, other) for step in range(4) for other in range(2)])
            inner = lax.bitwise_xor(self.my_fsdp, jnp.arange(4))
            places = (places[:, None] * 4 + inner[None]).reshape(-1)
            choice = (jnp.arange(self.n_all)[:, None] == places[None]).astype(value.dtype)
            full = dot_nn(choice, blocks).astype(value.dtype).reshape(self.n_all, rows, columns)
        return full.transpose(1, 0, 2).reshape(rows, self.n_all * columns)

    def sum_small(self, value):
        rows, columns = value.shape[0], value.shape[1] // self.n_all
        blocks = value.reshape(rows, self.n_all, columns).transpose(1, 0, 2)
        if not self.ring:
            return lax.psum_scatter(blocks.reshape(self.n_all, -1), ALL, scatter_dimension=0).reshape(rows, columns)
        blocks = blocks.reshape(self.n_exp, self.n_fsdp, rows * columns)
        four = self.sum_rows(blocks, F32)
        parts = [
            lax.dynamic_index_in_dim(four, lax.bitwise_xor(self.my_fsdp, k), 0, keepdims=True) for k in range(4)
        ]
        return self.sum_four(parts, F32).reshape(rows, columns)


def attend_kernel(heads, seq, scale, x_ref, w_ref, bias_ref, cos_ref, sin_ref, place_ref, seg_ref,
                  place_row_ref, seg_row_ref, qkv_ref, out_ref):
    lin = dot_nn(x_ref[...], w_ref[...]) + bias_ref[...]
    cosine, sine = cos_ref[...], sin_ref[...]
    span = heads * HEAD
    for micro in range(x_ref.shape[0] // seq):
        low, high = micro * seq, (micro + 1) * seq
        visible = (place_row_ref[...] <= place_ref[...]) & (seg_row_ref[micro : micro + 1, :] == seg_ref[low:high, :])
        for head in range(heads):
            at = head * HEAD
            query = lin[low:high, at : at + HEAD]
            key = lin[low:high, span + at : span + at + HEAD]
            value = lin[low:high, 2 * span + at : 2 * span + at + HEAD].astype(BF)
            query = (query * cosine + pltpu.roll(query, HEAD // 2, 1) * sine).astype(BF)
            key = (key * cosine + pltpu.roll(key, HEAD // 2, 1) * sine).astype(BF)
            scores = jnp.where(visible, dot_nt(query, key) * scale, MASKED)
            exps = jnp.exp(scores - jnp.max(scores, axis=1, keepdims=True))
            probs = exps / jnp.sum(exps, axis=1, keepdims=True)
            out_ref[low:high, at : at + HEAD] = dot_nn(probs.astype(BF), value).astype(BF)
            qkv_ref[low:high, at : at + HEAD] = query
            qkv_ref[low:high, span + at : span + at + HEAD] = key
            qkv_ref[low:high, 2 * span + at : 2 * span + at + HEAD] = value


def attend_back_kernel(heads, seq, scale, grad_ref, wo_ref, qkv_ref, cos_ref, sin_ref, place_ref, seg_ref,
                       place_row_ref, seg_row_ref, lin_ref):
    grad_out = dot_nt(grad_ref[...], wo_ref[...]).astype(BF)
    cosine, sine = cos_ref[...], sin_ref[...]
    span = heads * HEAD
    for micro in range(grad_ref.shape[0] // seq):
        low, high = micro * seq, (micro + 1) * seq
        visible = (place_row_ref[...] <= place_ref[...]) & (seg_row_ref[micro : micro + 1, :] == seg_ref[low:high, :])
        for head in range(heads):
            at = head * HEAD
            query = qkv_ref[low:high, at : at + HEAD]
            key = qkv_ref[low:high, span + at : span + at + HEAD]
            value = qkv_ref[low:high, 2 * span + at : 2 * span + at + HEAD]
            grad = grad_out[low:high, at : at + HEAD]
            scores = jnp.where(visible, dot_nt(query, key) * scale, MASKED)
            exps = jnp.exp(scores - jnp.max(scores, axis=1, keepdims=True))
            probs = exps / jnp.sum(exps, axis=1, keepdims=True)
            grad_probs = dot_nt(grad, value)
            grad_value = dot_tn(probs.astype(BF), grad)
            grad_scores = probs * (grad_probs - jnp.sum(probs * grad_probs, axis=1, keepdims=True))
            grad_scores = grad_scores.astype(BF)
            grad_query = dot_nn(grad_scores, key) * scale
            grad_key = dot_tn(grad_scores, query) * scale
            grad_query = grad_query * cosine - pltpu.roll(grad_query, HEAD // 2, 1) * sine
            grad_key = grad_key * cosine - pltpu.roll(grad_key, HEAD // 2, 1) * sine
            lin_ref[low:high, at : at + HEAD] = grad_query.astype(BF)
            lin_ref[low:high, span + at : span + at + HEAD] = grad_key.astype(BF)
            lin_ref[low:high, 2 * span + at : 2 * span + at + HEAD] = grad_value.astype(BF)


def whole(shape):
    return pl.BlockSpec(shape, lambda *_: (0,) * len(shape))


def attend(normed, wqkv, bias, tables, seq, back=None):
    cosine, sine, place, seg, place_row, seg_row = tables
    rows = normed.shape[0]
    pairs = 2
    wide3 = wqkv.shape[1]
    heads = wide3 // 3 // HEAD // pairs
    span = heads * HEAD
    scale = HEAD ** (-0.5)
    common = (cosine, sine, place, seg, place_row, seg_row)
    common_specs = [whole(item.shape) for item in common]
    params = pltpu.CompilerParams(vmem_limit_bytes=40 * 2**20)
    if back is None:
        return pl.pallas_call(
            functools.partial(attend_kernel, heads, seq, scale),
            grid=(pairs,),
            in_specs=[
                whole(normed.shape),
                pl.BlockSpec((wqkv.shape[0], 3 * span), lambda p: (0, p)),
                pl.BlockSpec((1, 3 * span), lambda p: (0, p)),
            ] + common_specs,
            out_specs=[
                pl.BlockSpec((rows, 3 * span), lambda p: (0, p)),
                pl.BlockSpec((rows, span), lambda p: (0, p)),
            ],
            out_shape=[
                jax.ShapeDtypeStruct((rows, wide3), BF),
                jax.ShapeDtypeStruct((rows, wide3 // 3), BF),
            ],
            compiler_params=params,
            cost_estimate=pl.CostEstimate(flops=5 * 10**9, bytes_accessed=10**7, transcendentals=10**6),
            name="attend",
        )(normed, wqkv, bias, *common)
    grad, wo, qkv = back
    return pl.pallas_call(
        functools.partial(attend_back_kernel, heads, seq, scale),
        grid=(pairs,),
        in_specs=[
            whole(grad.shape),
            pl.BlockSpec((span, wo.shape[1]), lambda p: (p, 0)),
            pl.BlockSpec((rows, 3 * span), lambda p: (0, p)),
        ] + common_specs,
        out_specs=pl.BlockSpec((rows, 3 * span), lambda p: (0, p)),
        out_shape=jax.ShapeDtypeStruct((rows, wide3), BF),
        compiler_params=params,
        cost_estimate=pl.CostEstimate(flops=5 * 10**9, bytes_accessed=10**7, transcendentals=10**6),
        name="attend_back",
    )(grad, wo, qkv, *common)


def feed_kernel(experts, shared, n_tiles, slots_ref, *refs):
    x_refs, g_refs = refs[:4], refs[4:8]
    wg_ref, wu_ref, wd_ref, router_ref = refs[8:12]
    hs_ref, dg_ref, du_ref = refs[12:15]
    gn_refs, out_refs = refs[15:19], refs[19:23]
    scale_shared, scale_expert, named, dot_shared, dot_expert, acc_out, acc_gn = refs[23:]
    width = x_refs[0].shape[-1]
    own = x_refs[0].shape[0]
    rows = 4 * own
    step = pl.program_id(0)
    x = jnp.concatenate([ref[...] for ref in x_refs], axis=0)
    g = jnp.concatenate([ref[0, :, :width] for ref in g_refs], axis=0)
    expert = slots_ref[2]

    @pl.when(step == 0)
    def _():
        logits = dot_nt(x, router_ref[...])
        lane = lax.broadcasted_iota(jnp.int32, logits.shape, 1)
        scores = jnp.where(lane < experts, logits, MASKED)
        exps = jnp.where(lane < experts, jnp.exp(scores - jnp.max(scores, axis=1, keepdims=True)), 0.0)
        probs = exps / jnp.sum(exps, axis=1, keepdims=True)
        mine = jnp.sum(jnp.where(lane == expert, probs, 0.0), axis=1, keepdims=True)
        gate = jnp.sum(jnp.where(lane == experts, logits, 0.0), axis=1, keepdims=True)
        names = jnp.concatenate([ref[0, :, width:] for ref in g_refs], axis=0).astype(F32)
        lane = lax.broadcasted_iota(jnp.int32, names.shape, 1)
        hit = jnp.where((lane < 4) & (names == expert.astype(F32)), 1.0, 0.0)
        hit = jnp.sum(hit, axis=1, keepdims=True)
        scale_shared[...] = jnp.broadcast_to(1.0 / (1.0 + jnp.exp(-gate)), scale_shared.shape)
        scale_expert[...] = jnp.broadcast_to(mine * hit, scale_expert.shape)
        named[...] = jnp.broadcast_to(hit, named.shape)
        dot_shared[...] = jnp.zeros_like(dot_shared)
        dot_expert[...] = jnp.zeros_like(dot_expert)

    wg, wu, wd = wg_ref[...], wu_ref[...], wd_ref[...]
    act, slope = silu_parts(dot_nt(x, wg))
    up = dot_nt(x, wu)
    grad = dot_nt(g, wd)
    unit = lax.broadcasted_iota(jnp.int32, (rows, TILE), 1) + step * TILE
    in_shared = unit < shared
    row_scale = jnp.where(in_shared, scale_shared[:, :1], scale_expert[:, :1])
    hidden = act * up
    dots = hidden * grad
    dot_shared[...] += jnp.sum(jnp.where(in_shared, dots, 0.0), axis=1, keepdims=True)
    dot_expert[...] += jnp.sum(jnp.where(in_shared, 0.0, dots), axis=1, keepdims=True)
    hs = (hidden * row_scale).astype(BF)
    grad = grad * row_scale
    dg = (grad * up * slope).astype(BF)
    du = (grad * act).astype(BF)
    hs_ref[...] = hs
    dg_ref[...] = dg
    du_ref[...] = du
    out_part = dot_nn(hs, wd)
    gn_part = dot_nn(dg, wg) + dot_nn(du, wu)

    @pl.when(step == 0)
    def _():
        acc_out[...] = out_part
        acc_gn[...] = gn_part

    @pl.when((step > 0) & (step < n_tiles - 1))
    def _():
        acc_out[...] += out_part
        acc_gn[...] += gn_part

    @pl.when(step == n_tiles - 1)
    def _():
        lane = lax.broadcasted_iota(jnp.int32, (rows, LANES), 1)
        extra = jnp.where(lane == expert, dot_expert[...] * named[...], 0.0)
        extra = extra + jnp.where(lane == experts, dot_shared[...], 0.0)
        for k in range(4):
            low, high = k * own, (k + 1) * own
            gn_refs[k][:, :width] = (acc_gn[low:high, :] + gn_part[low:high, :]).astype(BF)
            gn_refs[k][:, width:] = extra[low:high, :].astype(BF)
            out_refs[k][...] = (acc_out[low:high, :] + out_part[low:high, :]).astype(BF)


def feed(slots, blocks, near, far, wg, wu, wd, router, experts, shared):
    own, width = blocks[0].shape
    n_tiles = wg.shape[0] // TILE
    rows = 4 * own
    wide = near.shape[2]
    near_spec = [pl.BlockSpec((1, own, wide), lambda i, s, k=k: (s[k], 0, 0)) for k in range(2)]
    tile_rows = pl.BlockSpec((TILE, width), lambda i, s: (i, 0))
    tile_cols = pl.BlockSpec((rows, TILE), lambda i, s: (0, i))
    units = jax.ShapeDtypeStruct((rows, wg.shape[0]), BF)
    return pl.pallas_call(
        functools.partial(feed_kernel, experts, shared, n_tiles),
        grid_spec=pltpu.PrefetchScalarGridSpec(
            num_scalar_prefetch=1,
            grid=(n_tiles,),
            in_specs=[whole((own, width))] * 4 + near_spec + near_spec + [tile_rows] * 3 + [whole(router.shape)],
            out_specs=[tile_cols] * 3 + [whole((own, wide))] * 4 + [whole((own, width))] * 4,
            scratch_shapes=[pltpu.VMEM((rows, LANES), F32)] * 5 + [pltpu.VMEM((rows, width), F32)] * 2,
        ),
        out_shape=[units] * 3
        + [jax.ShapeDtypeStruct((own, wide), BF)] * 4
        + [jax.ShapeDtypeStruct((own, width), BF)] * 4,
        compiler_params=pltpu.CompilerParams(vmem_limit_bytes=56 * 2**20),
        cost_estimate=pl.CostEstimate(flops=16 * 10**9, bytes_accessed=3 * 10**7, transcendentals=10**6),
        name="feed",
    )(slots, *blocks, near, near, far, far, wg, wu, wd, router)


def weights_kernel(slots_ref, *refs):
    x_refs = [refs[4 * k : 4 * k + 4] for k in range(4)]
    near_ref, far_ref = refs[16:18]
    hs_refs, dg_refs, du_refs = refs[18:22], refs[22:26], refs[26:30]
    wg_ref, wu_ref, wd_ref = refs[30:33]
    width = x_refs[0][0].shape[-1]
    for k in range(4):
        x = jnp.concatenate([ref[...] for ref in x_refs[k]], axis=0)
        first, second = slots_ref[2 * k], slots_ref[2 * k + 1]
        g = jnp.concatenate(
            [ref[slot, :, :width] for ref in (near_ref, far_ref) for slot in (first, second)], axis=0
        )
        parts = dot_tn(dg_refs[k][...], x), dot_tn(du_refs[k][...], x), dot_tn(hs_refs[k][...], g)
        for ref, part in zip((wg_ref, wu_ref, wd_ref), parts):
            if k == 0:
                ref[...] = part
            else:
                ref[...] += part


def weight_grads(slots, blocks, near, far, hs, dg, du):
    own, width = blocks[0].shape
    rows, units = hs[0].shape
    n_tiles = units // TILE
    once = pl.Buffered(1)

    def fixed(shape):
        return pl.BlockSpec(shape, lambda *_: (0,) * len(shape), pipeline_mode=once)

    tile_cols = pl.BlockSpec((rows, TILE), lambda i, s: (0, i))
    return pl.pallas_call(
        weights_kernel,
        grid_spec=pltpu.PrefetchScalarGridSpec(
            num_scalar_prefetch=1,
            grid=(n_tiles,),
            in_specs=[fixed((own, width))] * 16 + [fixed(near.shape)] * 2 + [tile_cols] * 12,
            out_specs=[pl.BlockSpec((TILE, width), lambda i, s: (i, 0))] * 3,
        ),
        out_shape=[jax.ShapeDtypeStruct((units, width), F32)] * 3,
        compiler_params=pltpu.CompilerParams(vmem_limit_bytes=56 * 2**20),
        cost_estimate=pl.CostEstimate(flops=32 * 10**9, bytes_accessed=6 * 10**7, transcendentals=0),
        name="weight_grads",
    )(slots, *blocks, near, far, *hs, *dg, *du)


def feed_plain(normed, grad, named, expert, wg, wu, wd, router, experts, shared):
    logits = contract("td,cd->tc", normed, router)
    router_probs = jax.nn.softmax(logits[:, :experts], axis=-1)
    shared_scale = jax.nn.sigmoid(logits[:, experts : experts + 1])
    hot = (jnp.arange(experts) == expert).astype(F32)
    gate_here = jnp.sum(router_probs * hot, axis=1, keepdims=True) * named[:, None]
    is_shared = (jnp.arange(wg.shape[0]) < shared)[None]
    row_scale = jnp.where(is_shared, shared_scale, gate_here)
    act, slope = silu_parts(contract("td,cd->tc", normed, wg))
    up = contract("td,cd->tc", normed, wu)
    hidden = act * up
    hidden_scaled = (hidden * row_scale).astype(BF)
    grad_hidden = contract("td,fd->tf", grad, wd)
    dots = hidden * grad_hidden
    dot_shared = jnp.sum(jnp.where(is_shared, dots, 0.0), axis=1, keepdims=True)
    dot_expert = jnp.sum(jnp.where(is_shared, 0.0, dots), axis=1, keepdims=True) * named[:, None]
    grad_pre = grad_hidden * row_scale
    grad_gate = (grad_pre * up * slope).astype(BF)
    grad_up = (grad_pre * act).astype(BF)
    grad_normed = contract("tc,cd->td", grad_gate, wg) + contract("tc,cd->td", grad_up, wu)
    extra = jnp.concatenate([dot_expert * hot, dot_shared], axis=1)
    extra = jnp.pad(extra, ((0, 0), (0, LANES - extra.shape[1])))
    out = contract("tf,fd->td", hidden_scaled, wd)
    return (
        jnp.concatenate([grad_normed, extra], axis=1),
        out,
        contract("tc,td->cd", grad_gate, normed),
        contract("tc,td->cd", grad_up, normed),
        contract("tf,td->fd", hidden_scaled, grad),
    )


def on_device(
    hidden_in, seg_ids, routes, out_grad, norm_gain1, w_query, w_key, w_value, b_qkv, w_out,
    norm_gain2, w_router, shared_gate, sh_gate, sh_up, sh_down, ex_gate, ex_up, ex_down,
):
    links = Links()
    micro, tok, width = hidden_in.shape
    experts = w_router.shape[1]
    rows_w = w_query.shape[0]
    n_exp, n_fsdp, n_all = links.n_exp, links.n_fsdp, links.n_all
    my_exp, my_fsdp = links.my_exp, links.my_fsdp
    half_f, core_f = my_fsdp // 2, lax.rem(my_fsdp, 2)
    heads_dev = HEADS // n_fsdp
    wide = heads_dev * HEAD
    seq = tok * n_fsdp
    own = micro * tok
    sh_cols = SHARED_FF // n_all
    ex_cols = ex_gate.shape[2]

    def by_fsdp(three):
        rows = three.shape[0]
        split = three.reshape(rows, 3, 2, 2, heads_dev // 2, 2, HEAD)
        return split.transpose(5, 2, 0, 3, 1, 4, 6).reshape(n_fsdp, rows, 3 * wide)

    def from_fsdp(blocks):
        rows = blocks.shape[1]
        split = blocks.reshape(2, 2, rows, 2, 3, heads_dev // 2, HEAD)
        return split.transpose(4, 2, 1, 3, 5, 0, 6).reshape(3, rows, width)

    small = jnp.concatenate([w_router.T, shared_gate[None], norm_gain1[None], norm_gain2[None], b_qkv], axis=0)
    n_small = small.shape[0]
    small = links.gather_small(small)
    router_rows = small[: experts + 1]
    gain_one = small[experts + 1].astype(F32)
    gain_two = small[experts + 2].astype(F32)
    bias = by_fsdp(small[experts + 3 :].astype(F32)[None])
    bias = lax.dynamic_index_in_dim(bias, my_fsdp, 0, keepdims=False)

    x = hidden_in.reshape(own, width).astype(F32)
    scaled_one, inverse_one = normalize(x)
    normed_one = (scaled_one * gain_one).astype(BF)
    normed_seq = links.gather_seq(normed_one.reshape(micro, tok, width)).reshape(micro * seq, width)

    qkv = by_fsdp(jnp.stack([w_query, w_key, w_value], axis=1))
    qkv = links.swap_fsdp(qkv).reshape(n_fsdp * rows_w, 3 * wide)
    wqkv = links.gather_rows(qkv).reshape(width, 3 * wide)
    if links.ring:
        wo_rows = links.gather_rows(after(w_out, wqkv))
        keep = lax.dynamic_slice_in_dim(wo_rows, 4 * core_f, 4, 0)
        give = lax.dynamic_slice_in_dim(wo_rows, 4 * (1 - core_f), 4, 0)
        got = links.partner(give, 1)
        wo = jnp.where(core_f == 0, jnp.stack([keep, got], axis=1), jnp.stack([got, keep], axis=1))
        wo = wo.reshape(wide, width)
    else:
        wo = lax.all_gather(w_out, ALL, axis=0, tiled=True).reshape(2, heads_dev, 2, HEAD, width)
        wo = lax.dynamic_index_in_dim(wo, core_f, 0, keepdims=False)
        wo = lax.dynamic_index_in_dim(wo, half_f, 1, keepdims=False).reshape(wide, width)

    tile_cols = sh_cols // LANES * LANES
    rest_cols = sh_cols - tile_cols

    def by_owner(weight):
        full = weight[:, : n_all * tile_cols].reshape(rows_w, n_all, tile_cols).transpose(1, 0, 2)
        rest = weight[:, n_all * tile_cols :].reshape(rows_w, n_all, rest_cols).transpose(1, 0, 2)
        return full, rest

    def from_owner(full, rest):
        return jnp.concatenate(
            [full.transpose(1, 0, 2).reshape(rows_w, -1), rest.transpose(1, 0, 2).reshape(rows_w, -1)], axis=1
        )

    pieces = [by_owner(weight) for weight in (sh_gate, sh_up, sh_down)]
    shared_w = jnp.concatenate([piece[0] for piece in pieces] + [piece[1] for piece in pieces], axis=2)
    shared_w = lax.all_to_all(shared_w, ALL, split_axis=0, concat_axis=0, tiled=True)
    shared_w = shared_w.reshape(width, 3 * sh_cols).T

    def three(rows):
        return [
            jnp.concatenate(
                [rows[k * tile_cols : (k + 1) * tile_cols],
                 rows[3 * tile_cols + k * rest_cols : 3 * tile_cols + (k + 1) * rest_cols]], axis=0)
            for k in range(3)
        ]

    shared_other = links.partner(shared_w, 2)
    routed_own = [ex_gate[0].T, ex_up[0].T, ex_down[0]]
    routed_other = [links.partner(after(weight, normed_seq), 2) for weight in routed_own]
    units = 2 * (sh_cols + ex_cols)
    pad = jnp.zeros((-units % TILE, width), BF)
    wg, wu, wd = [
        jnp.concatenate([mine, other, routed, routed_far, pad], axis=0)
        for mine, other, routed, routed_far in zip(three(shared_w), three(shared_other), routed_own, routed_other)
    ]
    shared_units = 2 * sh_cols
    router_pad = jnp.pad(router_rows, ((0, -(experts + 1) % 16), (0, 0)))

    grad_own = out_grad.reshape(own, width)
    names = jnp.pad(routes.reshape(own, -1).astype(BF), ((0, 0), (0, LANES - routes.shape[2])))
    grad_near = lax.all_gather(after(jnp.concatenate([grad_own, names], axis=1), wqkv), "expert", axis=0)
    grad_far = links.partner(grad_near, 1)

    order = lax.bitwise_xor(my_fsdp, jnp.arange(n_fsdp))
    places = (order[:, None] * tok + jnp.arange(tok)[None]).reshape(seq)
    seg_seq = links.gather_seq(seg_ids)
    cosine, sine = angle_tables(places)
    tables = (cosine, sine, places[:, None], seg_seq.reshape(micro * seq, 1), places[None], seg_seq)
    qkv_seq, attended = attend(normed_seq, wqkv, bias, tables, seq)
    attn_part = contract("tc,cd->td", attended, wo).reshape(micro, n_fsdp, tok, width)
    attn_sum = links.sum_four([attn_part[:, k] for k in range(4)]).reshape(own, width)
    after_attn = x + attn_sum
    scaled_two, inverse_two = normalize(after_attn)
    normed_two = (scaled_two * gain_two).astype(BF)

    if links.ring:
        gathered = links.ring_gather(normed_two)
        fed, blocks, slots = {}, {}, {}
        for step in (1, 2, 3, 0):
            blocks[step] = gathered[step] + [links.partner(block, 1) for block in gathered[step]]
            slots[step] = [links.slot(step, other) for other in range(2)]
            fed[step] = feed(
                jnp.stack(slots[step] + [my_exp]), blocks[step], grad_near, grad_far,
                wg, wu, wd, router_pad, experts, shared_units,
            )

        def summed(first):
            def parts(step):
                found = fed[step][first : first + 4]
                return [found[k].astype(F32) + links.partner(found[2 + k], 1).astype(F32) for k in range(2)]

            return links.ring_sum(parts)

        grad_sum = summed(3)
        out_sum = summed(7)
        wg_grad, wu_grad, wd_grad = weight_grads(
            jnp.stack([slot for step in range(4) for slot in slots[step]]),
            [block for step in range(4) for block in blocks[step]],
            grad_near, grad_far, *[[fed[step][item] for step in range(4)] for item in range(3)],
        )
    else:
        near = lax.all_gather(normed_two, "expert", axis=0, tiled=True)
        normed_all = jnp.concatenate([near, links.partner(near, 1)], axis=0)
        grad_all = jnp.concatenate([grad_near, grad_far], axis=0).reshape(2 * n_exp * own, -1)
        named = jnp.sum((grad_all[:, width : width + routes.shape[2]] == my_exp.astype(BF)).astype(F32), axis=1)
        grad_part, out_part, wg_grad, wu_grad, wd_grad = feed_plain(
            normed_all, grad_all[:, :width], named, my_exp, wg, wu, wd, router_pad, experts, shared_units
        )

        def summed(part):
            count = n_exp * own
            total = part[:count] + links.partner(part[count:].astype(BF), 1).astype(F32)
            return links.sum_rows(total.reshape(n_exp, own, -1))

        grad_sum, out_sum = summed(grad_part), summed(out_part)
    hidden_out = (after_attn + out_sum).astype(BF)

    own_logits = contract("td,cd->tc", normed_two, router_rows)
    own_probs = jax.nn.softmax(own_logits[:, :experts], axis=-1)
    own_scale = jax.nn.sigmoid(own_logits[:, experts])
    grad_probs = grad_sum[:, width : width + experts]
    grad_router = own_probs * (grad_probs - jnp.sum(own_probs * grad_probs, axis=-1, keepdims=True))
    grad_gate = grad_sum[:, width + experts] * own_scale * (1.0 - own_scale)
    grad_logits = jnp.concatenate([grad_router, grad_gate[:, None]], axis=1).astype(BF)
    grad_normed_two = grad_sum[:, :width] + contract("tc,cd->td", grad_logits, router_rows)
    router_part = contract("tc,td->cd", grad_logits, normed_two)

    grad_after = grad_own.astype(F32) + norm_back(grad_normed_two, scaled_two, inverse_two, gain_two)
    gain_two_part = jnp.sum(grad_normed_two * scaled_two, axis=0)

    grad_attn = links.gather_seq(grad_after.astype(BF).reshape(micro, tok, width)).reshape(micro * seq, width)
    grad_lin = attend(normed_seq, wqkv, bias, tables, seq, (grad_attn, wo, qkv_seq))
    grad_normed_one = contract("tc,dc->td", grad_lin, wqkv).reshape(micro, n_fsdp, tok, width)
    grad_normed_one = links.sum_four([grad_normed_one[:, k] for k in range(4)]).reshape(own, width)
    in_grad = grad_after + norm_back(grad_normed_one, scaled_one, inverse_one, gain_one)
    gain_one_part = jnp.sum(grad_normed_one * scaled_one, axis=0)
    out_grad_part = contract("tc,td->cd", attended, grad_attn).astype(BF)
    qkv_part = contract("td,tc->dc", normed_seq, grad_lin).astype(BF)
    bias_part = jnp.sum(grad_lin.astype(F32), axis=0)

    qkv_sum = links.sum_rows(qkv_part.reshape(n_exp, n_fsdp * rows_w, 3 * wide)).astype(BF)
    qkv_own = from_fsdp(links.swap_fsdp(qkv_sum.reshape(n_fsdp, rows_w, 3 * wide))).astype(F32)
    if links.ring:
        halves = out_grad_part.reshape(heads_dev, 2, HEAD // 2, width)
        keep = lax.dynamic_index_in_dim(halves, core_f, 1, keepdims=False)
        got = links.partner(lax.dynamic_index_in_dim(halves, 1 - core_f, 1, keepdims=False), 1)
        rows = jnp.where(core_f == 0, jnp.concatenate([keep, got]), jnp.concatenate([got, keep]))
        out_own = links.sum_rows(rows)
    else:
        out_place = jnp.zeros((2, heads_dev, 2, HEAD, width), BF)
        out_place = lax.dynamic_update_slice(
            out_place, out_grad_part.reshape(1, heads_dev, 1, HEAD, width), (core_f, 0, half_f, 0, 0)
        )
        out_own = lax.psum_scatter(
            out_place.reshape(width, width), ALL, scatter_dimension=0, tiled=True
        ).astype(F32)
    bias_place = jnp.zeros((n_fsdp, 1, 3 * wide), F32)
    bias_place = from_fsdp(lax.dynamic_update_index_in_dim(bias_place, bias_part[None], my_fsdp, 0))[:, 0]
    small_part = jnp.concatenate([router_part, gain_one_part[None], gain_two_part[None], bias_place], axis=0)
    small_own = links.sum_small(small_part)

    grads = (wg_grad, wu_grad, wd_grad)
    shared_mine = jnp.concatenate(
        [grad[:tile_cols] for grad in grads] + [grad[tile_cols:sh_cols] for grad in grads], axis=0)
    shared_give = jnp.concatenate(
        [grad[sh_cols : sh_cols + tile_cols] for grad in grads]
        + [grad[sh_cols + tile_cols : 2 * sh_cols] for grad in grads], axis=0).astype(BF)
    shared_grads = (shared_mine + links.partner(shared_give, 2).astype(F32)).astype(BF)
    shared_own = lax.all_to_all(
        shared_grads.T.reshape(n_all, rows_w, 3 * sh_cols), ALL, split_axis=0, concat_axis=0, tiled=True
    )
    cut = 3 * tile_cols
    shared_own = [
        from_owner(
            shared_own[:, :, k * tile_cols : (k + 1) * tile_cols],
            shared_own[:, :, cut + k * rest_cols : cut + (k + 1) * rest_cols],
        ).astype(F32)
        for k in range(3)
    ]
    routed_grads = [
        grad[shared_units : shared_units + ex_cols]
        + links.partner(grad[shared_units + ex_cols : units].astype(BF), 2).astype(F32)
        for grad in grads
    ]
    return (
        hidden_out.reshape(micro, tok, width),
        in_grad.reshape(micro, tok, width),
        small_own[experts + 1],
        qkv_own[0],
        qkv_own[1],
        qkv_own[2],
        small_own[experts + 3 :],
        out_own,
        small_own[experts + 2],
        small_own[:experts].T,
        small_own[experts],
        shared_own[0],
        shared_own[1],
        shared_own[2],
        routed_grads[0].T[None],
        routed_grads[1].T[None],
        routed_grads[2][None],
    )


def solution(mesh):
    rows = P(ALL, None)
    tokens = P(None, ALL, None)
    in_specs = (
        tokens, P(None, ALL), tokens, tokens, P(ALL), rows, rows, rows, P(None, ALL), rows,
        P(ALL), rows, P(ALL), rows, rows, rows,
        P("expert", None, "fsdp"), P("expert", None, "fsdp"), P("expert", "fsdp", None),
    )
    out_specs = (
        tokens, tokens, P(ALL), rows, rows, rows, P(None, ALL), rows, P(ALL), rows, P(ALL),
        rows, rows, rows,
        P("expert", None, "fsdp"), P("expert", None, "fsdp"), P("expert", "fsdp", None),
    )
    return jax.shard_map(on_device, mesh=mesh, in_specs=in_specs, out_specs=out_specs, check_vma=False)
```

time: 4770 us -> 1090 us (0.23)
  waiting for transfers between devices: 3020 us -> 547 us
  matrix products: 521 us -> 15.2 us
  local copies, waits for them, and re-layouts: 600 us -> 116 us
  blocking collectives: 296 us -> 0 us
  Pallas kernels: 0 us -> 184 us
  other arithmetic: 260 us -> 83.3 us
  starting transfers between devices: 25.5 us -> 122 us
    reduce_scatter x9 -> x0, waiting for transfers between devices: 2400 us -> none  [the longest x1 2120 us: reduce_dense(): lax.psum_scatter(jnp.concatenate([contract('tr,tc->rc', normed_one, grad_...]
    all_gather x15 -> x1, waiting for transfers between devices: 619 us -> 0.01 us  [on_device(): lax.all_gather(after(jnp.concatenate([grad_own, names], axis=1), wqkv), '...]
    ppermute x0 -> x125, waiting for transfers between devices: none -> 547 us  [the longest x62 246 us: partner(): return lax.ppermute(value, ALL, partner_perm(self.n_exp, self.n_fsdp, bit))]
    dot_general x72 -> x8, matrix products: 521 us -> 15.2 us  [the longest x7 15.1 us: contract(): return jnp.einsum(pattern, left_op, right_op, preferred_element_type=F32)]
    concatenate x3 -> x12, local copies, waits for them, and re-layouts: 498 us -> 12.8 us  [the longest x1 5.27 us: on_device(): jnp.concatenate([piece[0] for piece in pieces] + [piece[1] for piece in p...]
    add x6 -> x11, other arithmetic: 200 us -> 6.43 us  [the longest x1 4.11 us: on_device(): grad_after + norm_back(grad_normed_one, scaled_one, inverse_one, gain_one)]
    pallas_call x0 -> x7, Pallas kernels: none -> 184 us  [the longest x4 125 us: feed(): pl.pallas_call(functools.partial(feed_kernel, experts, shared, n_tiles),...]
    all_to_all x4 -> x0, blocking collectives: 167 us -> none  [the longest x2 84.4 us: on_device(): lax.all_to_all(outgoing.reshape(expert_count, capacity, model_width), 'ex...]
  transfers between devices with their start and end apart: 28 -> 128, of which waited for: 16 -> 45; matrix products, arithmetic and copies ran while one was open for 11% -> 17% of each run, Pallas kernels for 0% -> 10%
where the time goes in v1:
time: 1090 us; the launch traced here: 1080 us
  waiting for transfers between devices  547 us (50%)
  Pallas kernels  184 us (17%)
  starting transfers between devices  122 us (11%)
  local copies, waits for them, and re-layouts  116 us (11%)
  other arithmetic  83.3 us (8%)
  between operations  16.6 us (2%)
  matrix products  15.2 us (1%)
    ppermute x62, waiting for transfers between devices, partner(): return lax.ppermute(value, ALL, partner_perm(self.n_exp, self.n_fsdp, bit))  246 us
    ppermute x27, waiting for transfers between devices, forward(): lax.ppermute(value, ALL, expert_perm(self.n_exp, self.n_fsdp, lambda e: (...  171 us
    ppermute x36, waiting for transfers between devices, pair(): lax.ppermute(value, ALL, expert_perm(self.n_exp, self.n_fsdp, lambda e: e...  130 us
    pallas_call x4, Pallas kernels, feed(): pl.pallas_call(functools.partial(feed_kernel, experts, shared, n_tiles),...  125 us
    unnamed x213, local copies, waits for them, and re-layouts  54.3 us
    pallas_call x1, Pallas kernels, weight_grads(): pl.pallas_call(weights_kernel, grid_spec=pltpu.PrefetchScalarGridSpec(num...  44.5 us
    ppermute x27, starting transfers between devices, forward(): lax.ppermute(value, ALL, expert_perm(self.n_exp, self.n_fsdp, lambda e: (...  41.3 us
    ppermute x36, starting transfers between devices, pair(): lax.ppermute(value, ALL, expert_perm(self.n_exp, self.n_fsdp, lambda e: e...  40.3 us
  transfers between devices with their start and end apart: 128, of which 45 were waited for; matrix products, arithmetic and copies ran while one was open for 17% of the time, Pallas kernels for 10%

profile of v1, /device:TPU:0, one launch (start us, length us, event | category | flops | bytes accessed | tf_op | source)
XLA Modules:
  0.0 1083.9 jit_solution(14729923346659675587)
XLA Ops:
  35.2 39.2 %collective-permute-done.4 = bf16[4,896]{1,0:T(4,128)(2,1)S(1)} collective-permute-done((bf16[4,896]{1,0:T(4,128)(2,1)S(1)}, bf16[4,896]{1,0:T(4,128)(2,1)S(1)}, u32[]{:S(2)}, u32[]{:S(2)}) %collective-permute-start.4) | collective-permute-done | bytes 7200 | tf_op jit(solution)/shard_map/ppermute | solution.py:89
  74.4 11.5 %collective-permute-start.6 = (bf16[4,896]{1,0:T(4,128)(2,1)S(1)}, bf16[4,896]{1,0:T(4,128)(2,1)S(1)}, u32[]{:S(2)}, u32[]{:S(2)}) collective-permute-start(bf16[4,896]{1,0:T(4,128)(2,1)S(1)} %collective-permute-done.4), channel_id=1, source_target_pairs={{0,8},{1,9},{2,10},{3,11},{4,12},{5,13},{6,14},{7,15},{8,16},{9,17... | collective-permute-start | bytes 21512 | tf_op jit(solution)/shard_map/ppermute | solution.py:89
  132.0 18.1 %collective-permute-done.19 = bf16[256,1536]{1,0:T(8,128)(2,1)S(1)} collective-permute-done((bf16[256,1536]{1,0:T(8,128)(2,1)S(1)}, bf16[256,1536]{1,0:T(8,128)(2,1)S(1)}, u32[]{:S(2)}, u32[]{:S(2)}) %collective-permute-start.19) | collective-permute-done | bytes 786464 | tf_op jit(solution)/shard_map/ppermute | solution.py:89
  151.6 18.7 %collective-permute-done.21 = bf16[256,1536]{1,0:T(8,128)(2,1)S(1)} collective-permute-done((bf16[256,1536]{1,0:T(8,128)(2,1)S(1)}, bf16[256,1536]{1,0:T(8,128)(2,1)S(1)}, u32[]{:S(2)}, u32[]{:S(2)}) %collective-permute-start.21) | collective-permute-done | bytes 786464 | tf_op jit(solution)/shard_map/ppermute | solution.py:89
  172.0 15.9 %collective-permute-done.22 = bf16[256,1536]{1,0:T(8,128)(2,1)S(1)} collective-permute-done((bf16[256,1536]{1,0:T(8,128)(2,1)S(1)}, bf16[256,1536]{1,0:T(8,128)(2,1)S(1)}, u32[]{:S(2)}, u32[]{:S(2)}) %collective-permute-start.22) | collective-permute-done | bytes 786464 | tf_op jit(solution)/shard_map/ppermute | solution.py:86
  200.4 12.1 %collective-permute-done.29 = bf16[64,2048]{1,0:T(8,128)(2,1)S(1)} collective-permute-done((bf16[64,2048]{1,0:T(8,128)(2,1)S(1)}, bf16[64,2048]{1,0:T(8,128)(2,1)S(1)}, u32[]{:S(2)}, u32[]{:S(2)}) %collective-permute-start.29) | collective-permute-done | bytes 262176 | tf_op jit(solution)/shard_map/ppermute | solution.py:89
  215.0 11.4 %collective-permute-done.31 = bf16[64,2048]{1,0:T(8,128)(2,1)S(1)} collective-permute-done((bf16[64,2048]{1,0:T(8,128)(2,1)S(1)}, bf16[64,2048]{1,0:T(8,128)(2,1)S(1)}, u32[]{:S(2)}, u32[]{:S(2)}) %collective-permute-start.31) | collective-permute-done | bytes 262176 | tf_op jit(solution)/shard_map/ppermute | solution.py:89
  264.7 114.3 %collective-permute-done.41 = bf16[528,2048]{1,0:T(8,128)(2,1)S(1)} collective-permute-done((bf16[528,2048]{1,0:T(8,128)(2,1)}, bf16[528,2048]{1,0:T(8,128)(2,1)S(1)}, u32[]{:S(2)}, u32[]{:S(2)}) %collective-permute-start.41) | collective-permute-done | bytes 2162720 | tf_op jit(solution)/shard_map/ppermute | solution.py:83
  423.4 13.6 %collective-permute-done.49.refs_0_.refs_8_ = bf16[128,2048]{1,0:T(8,128)(2,1)} collective-permute-done((bf16[128,2048]{1,0:T(8,128)(2,1)S(1)}, bf16[128,2048]{1,0:T(8,128)(2,1)}, u32[]{:S(2)}, u32[]{:S(2)}) %collective-permute-start.49) | collective-permute-done | bytes 524320 | tf_op jit(solution)/shard_map/ppermute | solution.py:89
  452.6 31.1 %feed.7 = (bf16[512,1280]{1,0:T(8,128)(2,1)}, bf16[512,1280]{1,0:T(8,128)(2,1)}, bf16[512,1280]{1,0:T(8,128)(2,1)}, bf16[128,2176]{1,0:T(8,128)(2,1)}, bf16[128,...) custom-call(s32[3]{0:T(128)} %add_add_fusion.3.slots_ref, ...), custom_call_target="tpu_custom_call" | custom-call | flops 16000000000 | bytes 30000000 | tf_op jit(solution)/shard_map/feed/pallas_call | solution.py:376
  485.2 31.6 %feed.6 = (bf16[512,1280]{1,0:T(8,128)(2,1)}, bf16[512,1280]{1,0:T(8,128)(2,1)}, bf16[512,1280]{1,0:T(8,128)(2,1)}, bf16[128,2176]{1,0:T(8,128)(2,1)}, bf16[128,...) custom-call(s32[3]{0:T(128)} %add_add_fusion.2.slots_ref, ...), custom_call_target="tpu_custom_call" | custom-call | flops 16000000000 | bytes 30000000 | tf_op jit(solution)/shard_map/feed/pallas_call | solution.py:376
  518.4 31.3 %feed.5 = (bf16[512,1280]{1,0:T(8,128)(2,1)}, bf16[512,1280]{1,0:T(8,128)(2,1)}, bf16[512,1280]{1,0:T(8,128)(2,1)}, bf16[128,2176]{1,0:T(8,128)(2,1)}, bf16[128,...) custom-call(s32[3]{0:T(128)} %add_add_fusion.1.slots_ref, ...), custom_call_target="tpu_custom_call" | custom-call | flops 16000000000 | bytes 30000000 | tf_op jit(solution)/shard_map/feed/pallas_call | solution.py:376
  551.3 31.3 %feed.4 = (bf16[512,1280]{1,0:T(8,128)(2,1)}, bf16[512,1280]{1,0:T(8,128)(2,1)}, bf16[512,1280]{1,0:T(8,128)(2,1)}, bf16[128,2176]{1,0:T(8,128)(2,1)}, bf16[128,...) custom-call(s32[3]{0:T(128)} %add_add_fusion.slots_ref, ...), custom_call_target="tpu_custom_call" | custom-call | flops 16000000000 | bytes 30000000 | tf_op jit(solution)/shard_map/feed/pallas_call | solution.py:376
  582.6 44.5 %weight_grads.1 = (f32[1280,2048]{1,0:T(8,128)}, f32[1280,2048]{1,0:T(8,128)}, f32[1280,2048]{1,0:T(8,128)}) custom-call(s32[8]{0:T(128)} %copy-done.67, bf16[128,2048]{1,0:T(8,128)(2,1)} %copy-done.32, bf16[128,2048]{1,0:T(8,128)(2,1)} %copy-done.78, bf16[128,2048]{1,0:T(8,128)(2,1)} %copy-done.81, bf16[128,2048]{1,0:T(8,128)(2,1)} %copy-done.82, ...), custom_call_target="tpu_custom_call" | custom-call | flops 32000000000 | bytes 60000000 | tf_op jit(solution)/shard_map/weight_grads/pallas_call | solution.py:424
  680.7 13.7 %collective-permute-done.83 = bf16[128,2176]{1,0:T(8,128)(2,1)S(1)} collective-permute-done((bf16[128,2176]{1,0:T(8,128)(2,1)S(1)}, bf16[128,2176]{1,0:T(8,128)(2,1)S(1)}, u32[]{:S(2)}, u32[]{:S(2)}) %collective-permute-start.83) | collective-permute-done | bytes 557088 | tf_op jit(solution)/shard_map/ppermute | solution.py:86
  697.4 11.9 %collective-permute-done.68 = bf16[128,2048]{1,0:T(8,128)(2,1)S(1)} collective-permute-done((bf16[128,2048]{1,0:T(8,128)(2,1)S(1)}, bf16[128,2048]{1,0:T(8,128)(2,1)S(1)}, u32[]{:S(2)}, u32[]{:S(2)}) %collective-permute-start.68) | collective-permute-done | bytes 524320 | tf_op jit(solution)/shard_map/ppermute | solution.py:86
  710.1 9.5 collective-permute-done.80
  737.1 14.6 %collective-permute-done.123 = bf16[352,2048]{1,0:T(8,128)(2,1)S(1)} collective-permute-done((bf16[352,2048]{1,0:T(8,128)(2,1)S(1)}, bf16[352,2048]{1,0:T(8,128)(2,1)S(1)}, u32[]{:S(2)}, u32[]{:S(2)}) %collective-permute-start.123) | collective-permute-done | bytes 1441824 | tf_op jit(solution)/shard_map/ppermute | solution.py:83
  768.2 22.2 %collective-permute-done.124 = bf16[352,2048]{1,0:T(8,128)(2,1)} collective-permute-done((bf16[352,2048]{1,0:T(8,128)(2,1)}, bf16[352,2048]{1,0:T(8,128)(2,1)}, u32[]{:S(2)}, u32[]{:S(2)}) %collective-permute-start.124) | collective-permute-done | bytes 1441824 | tf_op jit(solution)/shard_map/ppermute | solution.py:83
  798.5 49.0 %collective-permute-done.88 = bf16[2,64,2048]{2,1,0:T(8,128)(2,1)} collective-permute-done((bf16[2,64,2048]{2,1,0:T(8,128)(2,1)}, bf16[2,64,2048]{2,1,0:T(8,128)(2,1)}, u32[]{:S(2)}, u32[]{:S(2)}) %collective-permute-start.88) | collective-permute-done | bytes 524320 | tf_op jit(solution)/shard_map/ppermute | solution.py:83
  892.0 10.1 collective-permute-done.92
  943.1 30.7 %collective-permute-done.117 = bf16[64,2048]{1,0:T(8,128)(2,1)S(1)} collective-permute-done((bf16[64,2048]{1,0:T(8,128)(2,1)}, bf16[64,2048]{1,0:T(8,128)(2,1)S(1)}, u32[]{:S(2)}, u32[]{:S(2)}) %collective-permute-start.117) | collective-permute-done | bytes 262176 | tf_op jit(solution)/shard_map/ppermute | solution.py:86
  992.2 19.7 %collective-permute-done.115 = bf16[64,2048]{1,0:T(8,128)(2,1)S(1)} collective-permute-done((bf16[64,2048]{1,0:T(8,128)(2,1)S(1)}, bf16[64,2048]{1,0:T(8,128)(2,1)S(1)}, u32[]{:S(2)}, u32[]{:S(2)}) %collective-permute-start.115) | collective-permute-done | bytes 262176 | tf_op jit(solution)/shard_map/ppermute | solution.py:86
  1017.4 17.4 %collective-permute-done.120 = bf16[64,2048]{1,0:T(8,128)(2,1)S(1)} collective-permute-done((bf16[64,2048]{1,0:T(8,128)(2,1)}, bf16[64,2048]{1,0:T(8,128)(2,1)S(1)}, u32[]{:S(2)}, u32[]{:S(2)}) %collective-permute-start.120) | collective-permute-done | bytes 262176 | tf_op jit(solution)/shard_map/ppermute | solution.py:89
  (681 shorter events, 444.1 us)
Async XLA Ops:
  11.8 103.0 %collective-permute-start.23 = (s32[2,64]{1,0:T(2,128)}, s32[2,64]{1,0:T(2,128)S(1)}, u32[]{:S(2)}, u32[]{:S(2)}) collective-permute-start(s32[2,64]{1,0:T(2,128)} %param.20), channel_id=1, source_target_pairs={{0,1},{1,0},{2,3},{3,2},{4,5},{5,4},{6,7},{7,6},{8,9},{9,8},{10,11... | collective-permute-start | bytes 1544 | tf_op jit(solution)/shard_map/ppermute | solution.py:83
  22.2 229.3 %all-to-all-start = ((bf16[32,64,528]{2,1,0:T(8,128)(2,1)}), bf16[32,64,528]{2,1,0:T(8,128)(2,1)}, u32[]{:S(2)}, u32[]{:S(2)}) async-start(bf16[32,64,528]{2,1,0:T(8,128)(2,1)} %concatenate.85), calls=%async_computation | async-start | bytes 5242880 | tf_op jit(solution)/shard_map/all_to_all | solution.py:543
  27.2 359.2 %all-gather.3.cloned.1.call-start = ((), (), s32[]{:S(2)}) async-start(), calls=%async_computation.2 | async-start | bytes 5013504 | tf_op jit(solution)/shard_map/all_gather | solution.py:568
  116.1 119.0 %collective-permute-start.10 = (bf16[2,64,2048]{2,1,0:T(8,128)(2,1)S(1)}, bf16[2,64,2048]{2,1,0:T(8,128)(2,1)}, u32[]{:S(2)}, u32[]{:S(2)}) collective-permute-start(bf16[2,64,2048]{2,1,0:T(8,128)(2,1)S(1)} %fusion.25), channel_id=1, source_target_pairs={{0,1},{1,0},{2,3},{3,2},{4,5},{5,4},{6,7},{7,6},{8,9},{9,8},{10,11... | collective-permute-start | bytes 1572872 | tf_op jit(solution)/shard_map/ppermute | solution.py:83
  124.9 110.2 %collective-permute-start.12 = (bf16[2,64,2048]{2,1,0:T(8,128)(2,1)}, bf16[2,64,2048]{2,1,0:T(8,128)(2,1)}, u32[]{:S(2)}, u32[]{:S(2)}) collective-permute-start(bf16[2,64,2048]{2,1,0:T(8,128)(2,1)} %collective-permute-done.11), channel_id=1, source_target_pairs={{0,1},{1,0},{2,3},{3,2},{4,5},{5,4},{6,7},{7,6},{8,9},{9,8},{10,11... | collective-permute-start | bytes 1572872 | tf_op jit(solution)/shard_map/ppermute | solution.py:83
  236.7 169.8 %collective-permute-start.42 = (bf16[352,2048]{1,0:T(8,128)(2,1)}, bf16[352,2048]{1,0:T(8,128)(2,1)}, u32[]{:S(2)}, u32[]{:S(2)}) collective-permute-start(bf16[352,2048]{1,0:T(8,128)(2,1)} %bitcast.67), channel_id=1, source_target_pairs={{0,2},{1,3},{2,0},{3,1},{4,6},{5,7},{6,4},{7,5},{8,10},{9,11},{10,... | collective-permute-start | bytes 4325384 | tf_op jit(solution)/shard_map/ppermute | solution.py:83
  236.7 155.2 %collective-permute-start.43 = (bf16[352,2048]{1,0:T(8,128)(2,1)}, bf16[352,2048]{1,0:T(8,128)(2,1)}, u32[]{:S(2)}, u32[]{:S(2)}) collective-permute-start(bf16[352,2048]{1,0:T(8,128)(2,1)} %bitcast.70), channel_id=1, source_target_pairs={{0,2},{1,3},{2,0},{3,1},{4,6},{5,7},{6,4},{7,5},{8,10},{9,11},{10,... | collective-permute-start | bytes 4325384 | tf_op jit(solution)/shard_map/ppermute | solution.py:83
  238.7 150.3 %collective-permute-start.44 = (bf16[352,2048]{1,0:T(8,128)(2,1)}, bf16[352,2048]{1,0:T(8,128)(2,1)}, u32[]{:S(2)}, u32[]{:S(2)}) collective-permute-start(bf16[352,2048]{1,0:T(8,128)(2,1)} %bitcast.72), channel_id=1, source_target_pairs={{0,2},{1,3},{2,0},{3,1},{4,6},{5,7},{6,4},{7,5},{8,10},{9,11},{10,... | collective-permute-start | bytes 4325384 | tf_op jit(solution)/shard_map/ppermute | solution.py:83
  255.9 123.2 %collective-permute-start.41 = (bf16[528,2048]{1,0:T(8,128)(2,1)}, bf16[528,2048]{1,0:T(8,128)(2,1)S(1)}, u32[]{:S(2)}, u32[]{:S(2)}) collective-permute-start(bf16[528,2048]{1,0:T(8,128)(2,1)} %bitcast.389), channel_id=1, source_target_pairs={{0,2},{1,3},{2,0},{3,1},{4,6},{5,7},{6,4},{7,5},{8,10},{9,11},{10,... | collective-permute-start | bytes 6488072 | tf_op jit(solution)/shard_map/ppermute | solution.py:83
  264.6 131.2 %collective-permute-start.34 = (bf16[2,64,2048]{2,1,0:T(8,128)(2,1)S(1)}, bf16[2,64,2048]{2,1,0:T(8,128)(2,1)S(1)}, u32[]{:S(2)}, u32[]{:S(2)}) collective-permute-start(bf16[2,64,2048]{2,1,0:T(8,128)(2,1)S(1)} %get-tuple-element.164), channel_id=1, source_target_pairs={{0,1},{1,0},{2,3},{3,2},{4,5},{5,4},{6,7},{7,6},{8,9},{9,8},{10,11... | collective-permute-start | bytes 1572872 | tf_op jit(solution)/shard_map/ppermute | solution.py:83
  386.4 64.7 %collective-permute-start.40 = (bf16[8,128,2176]{2,1,0:T(8,128)(2,1)}, bf16[8,128,2176]{2,1,0:T(8,128)(2,1)}, u32[]{:S(2)}, u32[]{:S(2)}) collective-permute-start(bf16[8,128,2176]{2,1,0:T(8,128)(2,1)} %bitcast.430), channel_id=1, source_target_pairs={{0,1},{1,0},{2,3},{3,2},{4,5},{5,4},{6,7},{7,6},{8,9},{9,8},{10,11... | collective-permute-start | bytes 13369352 | tf_op jit(solution)/shard_map/ppermute | solution.py:83
  439.6 110.1 %collective-permute-start.38 = (bf16[128,2048]{1,0:T(8,128)(2,1)S(1)}, bf16[128,2048]{1,0:T(8,128)(2,1)S(1)}, u32[]{:S(2)}, u32[]{:S(2)}) collective-permute-start(bf16[128,2048]{1,0:T(8,128)(2,1)S(1)} %multiply_convert_fusion.1.refs_0_), channel_id=1, source_target_pairs={{0,1},{1,0},{2,3},{3,2},{4,5},{5,4},{6,7},{7,6},{8,9},{9,8},{10,11... | collective-permute-start | bytes 1572872 | tf_op jit(solution)/shard_map/ppermute | solution.py:83
  439.9 109.9 %collective-permute-start.39 = (bf16[128,2048]{1,0:T(8,128)(2,1)}, bf16[128,2048]{1,0:T(8,128)(2,1)S(1)}, u32[]{:S(2)}, u32[]{:S(2)}) collective-permute-start(bf16[128,2048]{1,0:T(8,128)(2,1)} %copy-done.78), channel_id=1, source_target_pairs={{0,1},{1,0},{2,3},{3,2},{4,5},{5,4},{6,7},{7,6},{8,9},{9,8},{10,11... | collective-permute-start | bytes 1572872 | tf_op jit(solution)/shard_map/ppermute | solution.py:83
  757.2 90.4 %collective-permute-start.121 = (bf16[528,2048]{1,0:T(8,128)(2,1)}, bf16[528,2048]{1,0:T(8,128)(2,1)}, u32[]{:S(2)}, u32[]{:S(2)}) collective-permute-start(bf16[528,2048]{1,0:T(8,128)(2,1)} %slice_dynamic-update-slice_fusion.15), channel_id=1, source_target_pairs={{0,2},{1,3},{2,0},{3,1},{4,6},{5,7},{6,4},{7,5},{8,10},{9,11},{10,... | collective-permute-start | bytes 6488072 | tf_op jit(solution)/shard_map/ppermute | solution.py:83
  790.4 57.1 %collective-permute-start.88 = (bf16[2,64,2048]{2,1,0:T(8,128)(2,1)}, bf16[2,64,2048]{2,1,0:T(8,128)(2,1)}, u32[]{:S(2)}, u32[]{:S(2)}) collective-permute-start(bf16[2,64,2048]{2,1,0:T(8,128)(2,1)} %bitcast.75), channel_id=1, source_target_pairs={{0,2},{1,3},{2,0},{3,1},{4,6},{5,7},{6,4},{7,5},{8,10},{9,11},{10,... | collective-permute-start | bytes 1572872 | tf_op jit(solution)/shard_map/ppermute | solution.py:83
  795.2 140.8 %collective-permute-start.45 = (bf16[128,2048]{1,0:T(8,128)(2,1)}, bf16[128,2048]{1,0:T(8,128)(2,1)}, u32[]{:S(2)}, u32[]{:S(2)}) collective-permute-start(bf16[128,2048]{1,0:T(8,128)(2,1)} %get-tuple-element.78), channel_id=1, source_target_pairs={{0,1},{1,0},{2,3},{3,2},{4,5},{5,4},{6,7},{7,6},{8,9},{9,8},{10,11... | collective-permute-start | bytes 1572872 | tf_op jit(solution)/shard_map/ppermute | solution.py:83
  795.2 141.7 %collective-permute-start.47 = (bf16[128,2048]{1,0:T(8,128)(2,1)}, bf16[128,2048]{1,0:T(8,128)(2,1)}, u32[]{:S(2)}, u32[]{:S(2)}) collective-permute-start(bf16[128,2048]{1,0:T(8,128)(2,1)} %add_convert_fusion.15), channel_id=1, source_target_pairs={{0,4},{1,5},{2,6},{3,7},{4,0},{5,1},{6,2},{7,3},{8,12},{9,13},{10,... | collective-permute-start | bytes 1572872 | tf_op jit(solution)/shard_map/ppermute | solution.py:86
  798.3 60.2 %collective-permute-start.87 = (bf16[2,64,2048]{2,1,0:T(8,128)(2,1)}, bf16[2,64,2048]{2,1,0:T(8,128)(2,1)}, u32[]{:S(2)}, u32[]{:S(2)}) collective-permute-start(bf16[2,64,2048]{2,1,0:T(8,128)(2,1)} %bitcast.75), channel_id=1, source_target_pairs={{0,1},{1,0},{2,3},{3,2},{4,5},{5,4},{6,7},{7,6},{8,9},{9,8},{10,11... | collective-permute-start | bytes 1572872 | tf_op jit(solution)/shard_map/ppermute | solution.py:83
  852.6 186.4 %all-to-all-start.1 = ((bf16[32,64,528]{2,1,0:T(8,128)(2,1)}), bf16[32,64,528]{2,1,0:T(8,128)(2,1)}, u32[]{:S(2)}, u32[]{:S(2)}) async-start(bf16[32,64,528]{2,1,0:T(8,128)(2,1)} %bitcast.132), calls=%async_computation.1 | async-start | bytes 5242880 | tf_op jit(solution)/shard_map/all_to_all | solution.py:676
  890.5 47.9 %collective-permute-start.71 = (bf16[128,2048]{1,0:T(8,128)(2,1)}, bf16[128,2048]{1,0:T(8,128)(2,1)}, u32[]{:S(2)}, u32[]{:S(2)}) collective-permute-start(bf16[128,2048]{1,0:T(8,128)(2,1)} %add_convert_fusion.9), channel_id=1, source_target_pairs={{0,8},{1,9},{2,10},{3,11},{4,12},{5,13},{6,14},{7,15},{8,16},{9,17... | collective-permute-start | bytes 1572872 | tf_op jit(solution)/shard_map/ppermute | solution.py:89
  932.4 116.2 %collective-permute-start.103 = (bf16[256,1536]{1,0:T(8,128)(2,1)}, bf16[256,1536]{1,0:T(8,128)(2,1)}, u32[]{:S(2)}, u32[]{:S(2)}) collective-permute-start(bf16[256,1536]{1,0:T(8,128)(2,1)} %get-tuple-element.134), channel_id=1, source_target_pairs={{0,4},{1,5},{2,6},{3,7},{4,0},{5,1},{6,2},{7,3},{8,12},{9,13},{10,... | collective-permute-start | bytes 2359304 | tf_op jit(solution)/shard_map/ppermute | solution.py:86
  935.4 53.3 %collective-permute-start.105 = (bf16[256,1536]{1,0:T(8,128)(2,1)}, bf16[256,1536]{1,0:T(8,128)(2,1)S(1)}, u32[]{:S(2)}, u32[]{:S(2)}) collective-permute-start(bf16[256,1536]{1,0:T(8,128)(2,1)} %get-tuple-element.136), channel_id=1, source_target_pairs={{0,4},{1,5},{2,6},{3,7},{4,0},{5,1},{6,2},{7,3},{8,12},{9,13},{10,... | collective-permute-start | bytes 2359304 | tf_op jit(solution)/shard_map/ppermute | solution.py:86
  936.1 53.2 %collective-permute-start.107 = (bf16[256,1536]{1,0:T(8,128)(2,1)}, bf16[256,1536]{1,0:T(8,128)(2,1)S(1)}, u32[]{:S(2)}, u32[]{:S(2)}) collective-permute-start(bf16[256,1536]{1,0:T(8,128)(2,1)} %fusion.1), channel_id=1, source_target_pairs={{0,8},{1,9},{2,10},{3,11},{4,12},{5,13},{6,14},{7,15},{8,16},{9,17... | collective-permute-start | bytes 2359304 | tf_op jit(solution)/shard_map/ppermute | solution.py:89
  984.1 52.5 %collective-permute-start.104 = (bf16[256,1536]{1,0:T(8,128)(2,1)}, bf16[256,1536]{1,0:T(8,128)(2,1)S(1)}, u32[]{:S(2)}, u32[]{:S(2)}) collective-permute-start(bf16[256,1536]{1,0:T(8,128)(2,1)} %get-tuple-element.137), channel_id=1, source_target_pairs={{0,4},{1,5},{2,6},{3,7},{4,0},{5,1},{6,2},{7,3},{8,12},{9,13},{10,... | collective-permute-start | bytes 2359304 | tf_op jit(solution)/shard_map/ppermute | solution.py:86
  (202 other events, 4137.6 us)
Sparse Core Ops, SparseCore 0:
  192.3 83.1 all-gather.2

commit v2 on v1

v2 whole, which is shorter than its diff:
```python
import functools

import jax
import jax.numpy as jnp
from jax import lax
from jax.experimental import pallas as pl
from jax.experimental.pallas import tpu as pltpu
from jax.sharding import PartitionSpec as P

HEADS = 16
HEAD = 128
SHARED_FF = 5632
EPSILON = 1e-06
ROPE_BASE = 1000000.0
MASKED = -1e30
ALL = ("expert", "fsdp")
BF = jnp.bfloat16
F32 = jnp.float32
LANES = 128
COLS = 1024
GRAD_TILE = 384


def normalize(values):
    inverse = lax.rsqrt(jnp.mean(values * values, axis=-1, keepdims=True) + EPSILON)
    return (values * inverse, inverse)


def norm_back(grad_normed, scaled, inverse, gain_vec):
    grad_scaled = grad_normed * gain_vec
    return inverse * (grad_scaled - scaled * jnp.mean(grad_scaled * scaled, axis=-1, keepdims=True))


def angle_tables(places):
    inverse = 1.0 / ROPE_BASE ** (jnp.arange(0, HEAD, 2).astype(F32) / HEAD)
    angles = places.astype(F32)[:, None] * inverse[None, :]
    cosine, sine = jnp.cos(angles), jnp.sin(angles)
    return jnp.concatenate([cosine, cosine], axis=1), jnp.concatenate([-sine, sine], axis=1)


def silu_parts(pre_act):
    logistic = 1.0 / (1.0 + jnp.exp(-pre_act))
    return (pre_act * logistic, logistic * (1.0 + pre_act * (1.0 - logistic)))


def contract(pattern, left_op, right_op):
    return jnp.einsum(pattern, left_op, right_op, preferred_element_type=F32)


def dot_nt(left_op, right_op):
    return lax.dot_general(left_op, right_op, (((1,), (1,)), ((), ())), preferred_element_type=F32)


def dot_nn(left_op, right_op):
    return lax.dot_general(left_op, right_op, (((1,), (0,)), ((), ())), preferred_element_type=F32)


def dot_tn(left_op, right_op):
    return lax.dot_general(left_op, right_op, (((0,), (0,)), ((), ())), preferred_element_type=F32)


def after(value, *earlier):
    return lax.optimization_barrier((value, earlier))[0]


class Links:
    def __init__(self):
        self.n_exp = lax.axis_size("expert")
        self.n_fsdp = lax.axis_size("fsdp")
        self.my_exp = lax.axis_index("expert")
        self.my_fsdp = lax.axis_index("fsdp")
        self.n_all = self.n_exp * self.n_fsdp

    def partner(self, value, bit):
        pairs = [
            (e * self.n_fsdp + f, e * self.n_fsdp + (f ^ bit)) for e in range(self.n_exp) for f in range(self.n_fsdp)
        ]
        return lax.ppermute(value, ALL, pairs)

    def gather_rows(self, value):
        return lax.all_gather(value, "expert", axis=0)

    def sum_rows(self, value):
        return lax.psum_scatter(value.astype(BF), "expert", scatter_dimension=0).astype(F32)

    def swap_fsdp(self, value):
        result = value
        for bit in range(1, self.n_fsdp):
            other = lax.bitwise_xor(self.my_fsdp, bit)
            block = lax.dynamic_index_in_dim(value, other, 0, keepdims=False)
            result = lax.dynamic_update_index_in_dim(result, self.partner(block, bit), other, 0)
        return result

    def gather_four(self, value):
        far = self.partner(value, 2)
        return [value, self.partner(value, 1), far, self.partner(far, 1)]

    def gather_seq(self, value):
        return jnp.concatenate(self.gather_four(value), axis=1)

    def sum_four(self, parts):
        far = (parts[2].astype(F32) + self.partner(parts[3].astype(BF), 1).astype(F32)).astype(BF)
        near = parts[0].astype(F32) + self.partner(parts[1].astype(BF), 1).astype(F32)
        return near + self.partner(far, 2).astype(F32)


def attend_kernel(heads, seq, scale, x_ref, w_ref, bias_ref, cos_ref, sin_ref, place_ref, seg_ref,
                  place_row_ref, seg_row_ref, qkv_ref, out_ref):
    lin = dot_nn(x_ref[...], w_ref[...]) + bias_ref[...]
    cosine, sine = cos_ref[...], sin_ref[...]
    span = heads * HEAD
    for micro in range(x_ref.shape[0] // seq):
        low, high = micro * seq, (micro + 1) * seq
        visible = (place_row_ref[...] <= place_ref[...]) & (seg_row_ref[micro : micro + 1, :] == seg_ref[low:high, :])
        for head in range(heads):
            at = head * HEAD
            query = lin[low:high, at : at + HEAD]
            key = lin[low:high, span + at : span + at + HEAD]
            value = lin[low:high, 2 * span + at : 2 * span + at + HEAD].astype(BF)
            query = (query * cosine + pltpu.roll(query, HEAD // 2, 1) * sine).astype(BF)
            key = (key * cosine + pltpu.roll(key, HEAD // 2, 1) * sine).astype(BF)
            scores = jnp.where(visible, dot_nt(query, key) * scale, MASKED)
            exps = jnp.exp(scores - jnp.max(scores, axis=1, keepdims=True))
            probs = exps / jnp.sum(exps, axis=1, keepdims=True)
            out_ref[low:high, at : at + HEAD] = dot_nn(probs.astype(BF), value).astype(BF)
            qkv_ref[low:high, at : at + HEAD] = query
            qkv_ref[low:high, span + at : span + at + HEAD] = key
            qkv_ref[low:high, 2 * span + at : 2 * span + at + HEAD] = value


def attend_back_kernel(heads, seq, scale, grad_ref, wo_ref, qkv_ref, cos_ref, sin_ref, place_ref, seg_ref,
                       place_row_ref, seg_row_ref, w_ref, lin_ref, normed_ref):
    grad_out = dot_nt(grad_ref[...], wo_ref[...]).astype(BF)
    cosine, sine = cos_ref[...], sin_ref[...]
    span = heads * HEAD
    for micro in range(grad_ref.shape[0] // seq):
        low, high = micro * seq, (micro + 1) * seq
        visible = (place_row_ref[...] <= place_ref[...]) & (seg_row_ref[micro : micro + 1, :] == seg_ref[low:high, :])
        for head in range(heads):
            at = head * HEAD
            query = qkv_ref[low:high, at : at + HEAD]
            key = qkv_ref[low:high, span + at : span + at + HEAD]
            value = qkv_ref[low:high, 2 * span + at : 2 * span + at + HEAD]
            grad = grad_out[low:high, at : at + HEAD]
            scores = jnp.where(visible, dot_nt(query, key) * scale, MASKED)
            exps = jnp.exp(scores - jnp.max(scores, axis=1, keepdims=True))
            probs = exps / jnp.sum(exps, axis=1, keepdims=True)
            grad_probs = dot_nt(grad, value)
            grad_value = dot_tn(probs.astype(BF), grad)
            grad_scores = probs * (grad_probs - jnp.sum(probs * grad_probs, axis=1, keepdims=True))
            grad_scores = grad_scores.astype(BF)
            grad_query = dot_nn(grad_scores, key) * scale
            grad_key = dot_tn(grad_scores, query) * scale
            grad_query = grad_query * cosine - pltpu.roll(grad_query, HEAD // 2, 1) * sine
            grad_key = grad_key * cosine - pltpu.roll(grad_key, HEAD // 2, 1) * sine
            lin_ref[low:high, at : at + HEAD] = grad_query.astype(BF)
            lin_ref[low:high, span + at : span + at + HEAD] = grad_key.astype(BF)
            lin_ref[low:high, 2 * span + at : 2 * span + at + HEAD] = grad_value.astype(BF)
    part = dot_nt(lin_ref[...], w_ref[...])

    @pl.when(pl.program_id(0) == 0)
    def _():
        normed_ref[...] = part

    @pl.when(pl.program_id(0) > 0)
    def _():
        normed_ref[...] += part


def whole(shape):
    return pl.BlockSpec(shape, lambda *_: (0,) * len(shape))


def attend(normed, wqkv, bias, tables, seq, back=None):
    cosine, sine, place, seg, place_row, seg_row = tables
    rows = normed.shape[0]
    pairs = 2
    wide3 = bias.shape[1]
    heads = wide3 // 3 // HEAD // pairs
    span = heads * HEAD
    scale = HEAD ** (-0.5)
    common = (cosine, sine, place, seg, place_row, seg_row)
    common_specs = [whole(item.shape) for item in common]
    params = pltpu.CompilerParams(vmem_limit_bytes=40 * 2**20)
    if back is None:
        return pl.pallas_call(
            functools.partial(attend_kernel, heads, seq, scale),
            grid=(pairs,),
            in_specs=[
                whole(normed.shape),
                pl.BlockSpec((wqkv.shape[0], 3 * span), lambda p: (0, p)),
                pl.BlockSpec((1, 3 * span), lambda p: (0, p)),
            ] + common_specs,
            out_specs=[
                pl.BlockSpec((rows, 3 * span), lambda p: (0, p)),
                pl.BlockSpec((rows, span), lambda p: (0, p)),
            ],
            out_shape=[
                jax.ShapeDtypeStruct((rows, wide3), BF),
                jax.ShapeDtypeStruct((rows, wide3 // 3), BF),
            ],
            compiler_params=params,
            cost_estimate=pl.CostEstimate(flops=5 * 10**9, bytes_accessed=10**7, transcendentals=10**6),
            name="attend",
        )(normed, wqkv, bias, *common)
    grad, wo, qkv = back
    return pl.pallas_call(
        functools.partial(attend_back_kernel, heads, seq, scale),
        grid=(pairs,),
        in_specs=[
            whole(grad.shape),
            pl.BlockSpec((span, wo.shape[1]), lambda p: (p, 0)),
            pl.BlockSpec((rows, 3 * span), lambda p: (0, p)),
        ] + common_specs + [pl.BlockSpec((wqkv.shape[0], 3 * span), lambda p: (0, p))],
        out_specs=[pl.BlockSpec((rows, 3 * span), lambda p: (0, p)), whole((rows, wqkv.shape[0]))],
        out_shape=[jax.ShapeDtypeStruct((rows, wide3), BF), jax.ShapeDtypeStruct((rows, wqkv.shape[0]), F32)],
        compiler_params=params,
        cost_estimate=pl.CostEstimate(flops=5 * 10**9, bytes_accessed=10**7, transcendentals=10**6),
        name="attend_back",
    )(grad, wo, qkv, *common, wqkv)


def feed_kernel(experts, shared, expert_ref, *refs):
    x_refs, g_refs = refs[:4], refs[4:8]
    weights = (refs[8:11], refs[11:14])
    unit_refs, gn_refs, out_refs = refs[14:20], refs[20:24], refs[24:28]
    x_all, g_all = refs[28:30]
    units = (refs[30:33], refs[33:36])
    gn, out, sems = refs[36:]
    own, width = x_refs[0].shape
    rows = 4 * own
    expert = expert_ref[0]

    def block(k):
        return pl.ds(k * own, own)

    def start(number, source, target):
        copy = pltpu.make_async_copy(source, target, sems.at[number])
        copy.start()
        return copy

    x_copies = [start(k, x_refs[k], x_all.at[block(k), :]) for k in range(4)]
    g_copies = [start(4 + k, g_refs[k], g_all.at[block(k), :]) for k in range(4)]
    for copy in x_copies:
        copy.wait()
    gates = [dot_nt(x_all[...], weights[k][0][...]) for k in range(2)]
    for copy in g_copies:
        copy.wait()
    names = g_all[:, width:].astype(F32)
    lane = lax.broadcasted_iota(jnp.int32, names.shape, 1)
    hit = jnp.where((lane < 4) & (names == expert.astype(F32)), 1.0, 0.0)
    hit = jnp.sum(hit, axis=1, keepdims=True)
    first = shared // LANES * LANES
    logits = gates[0][:, first : first + LANES]
    lane = lane - (shared - first)
    is_expert = (lane >= 0) & (lane < experts)
    scores = jnp.where(is_expert, logits, MASKED)
    exps = jnp.where(is_expert, jnp.exp(scores - jnp.max(scores, axis=1, keepdims=True)), 0.0)
    mine = jnp.sum(jnp.where(lane == expert, exps, 0.0), axis=1, keepdims=True)
    mine = mine / jnp.sum(exps, axis=1, keepdims=True)
    last = jnp.sum(jnp.where(lane == experts, logits, 0.0), axis=1, keepdims=True)
    scales = (1.0 / (1.0 + jnp.exp(-last)), mine * hit)
    dots, copies = [], []
    for k in range(2):
        hs, dg, du = units[k]
        act, slope = silu_parts(gates[k])
        up = dot_nt(x_all[...], weights[k][1][...])
        grad = dot_nt(g_all[:, :width], weights[k][2][...])
        hidden = act * up
        dots.append(jnp.sum(hidden * grad, axis=1, keepdims=True))
        grad = grad * scales[k]
        hs[...] = (hidden * scales[k]).astype(BF)
        dg[...] = (grad * up * slope).astype(BF)
        du[...] = (grad * act).astype(BF)
        copies += [
            start(3 * k + j, source, target) for j, (source, target) in enumerate(zip((hs, dg, du), unit_refs[3 * k :]))
        ]
    lane = lax.broadcasted_iota(jnp.int32, (rows, LANES), 1)
    extra = jnp.where(lane == expert, dots[1] * hit, 0.0) + jnp.where(lane == experts, dots[0], 0.0)
    gn[:, width:] = extra.astype(BF)
    total = dot_nn(units[0][1][...], weights[0][0][...]) + dot_nn(units[0][2][...], weights[0][1][...])
    total += dot_nn(units[1][1][...], weights[1][0][...]) + dot_nn(units[1][2][...], weights[1][1][...])
    gn[:, :width] = total.astype(BF)
    copies += [start(6 + k, gn.at[block(k), :], gn_refs[k]) for k in range(4)]
    total = dot_nn(units[0][0][...], weights[0][2][...]) + dot_nn(units[1][0][...], weights[1][2][...])
    out[...] = total.astype(BF)
    copies += [start(10 + k, out.at[block(k), :], out_refs[k]) for k in range(4)]
    for copy in copies:
        copy.wait()


def feed(expert, x_blocks, g_blocks, shared_w, routed_w, experts, shared):
    own, width = x_blocks[0].shape
    rows = 4 * own
    wide = g_blocks[0].shape[1]
    counts = (shared_w[0].shape[0], routed_w[0].shape[0])
    anywhere = pl.BlockSpec(memory_space=pl.ANY)
    weights = [pltpu.with_memory_space_constraint(weight, pltpu.VMEM) for weight in (*shared_w, *routed_w)]
    found = pl.pallas_call(
        functools.partial(feed_kernel, experts, shared),
        in_specs=[pl.BlockSpec(memory_space=pltpu.SMEM)]
        + [anywhere] * 8
        + [pl.BlockSpec(memory_space=pltpu.VMEM)] * 6,
        out_specs=[anywhere] * 14,
        scratch_shapes=[pltpu.VMEM((rows, width), BF), pltpu.VMEM((rows, wide), BF)]
        + [pltpu.VMEM((rows, count), BF) for count in counts for _ in range(3)]
        + [pltpu.VMEM((rows, wide), BF), pltpu.VMEM((rows, width), BF), pltpu.SemaphoreType.DMA((14,))],
        out_shape=[jax.ShapeDtypeStruct((rows, count), BF) for count in counts for _ in range(3)]
        + [jax.ShapeDtypeStruct((own, wide), BF)] * 4
        + [jax.ShapeDtypeStruct((own, width), BF)] * 4,
        compiler_params=pltpu.CompilerParams(vmem_limit_bytes=42 * 2**20),
        cost_estimate=pl.CostEstimate(flops=16 * 10**9, bytes_accessed=3 * 10**7, transcendentals=10**6),
        name="feed",
    )(expert, *x_blocks, *g_blocks, *weights)
    return found[:3], found[3:6], found[6:10], found[10:14]


def join_kernel(cuts, y_ref, mine_ref, low_ref, high_ref, behind_ref, *out_refs):
    half = low_ref.shape[0]
    for k, pieces in enumerate(cuts):
        at = 0
        for low, count in pieces:
            for block in range(mine_ref.shape[1] // LANES):
                columns = slice(block * LANES, (block + 1) * LANES)
                target = pl.ds(pl.multiple_of((2 * block + y_ref[0]) * LANES, LANES), LANES)
                out_refs[k][at : at + count, target] = mine_ref[low : low + count, columns]
                target = pl.ds(pl.multiple_of((2 * block + 1 - y_ref[0]) * LANES, LANES), LANES)
                middle = min(max(half - low, 0), count)
                if middle:
                    out_refs[k][at : at + middle, target] = low_ref[low : low + middle, columns]
                if middle < count:
                    begin = low + middle - half
                    out_refs[k][at + middle : at + count, target] = high_ref[begin : begin + count - middle, columns]
            at += count
        rest = out_refs[k].shape[0] - at
        out_refs[k][at:, :] = behind_ref[...] if k == 0 else jnp.zeros((rest, out_refs[k].shape[1]), BF)


def join_shared(y, mine, low, high, behind, cuts):
    rows = sum(count for _, count in cuts[0]) + behind.shape[0]
    vmem = pl.BlockSpec(memory_space=pltpu.VMEM)
    return pl.pallas_call(
        functools.partial(join_kernel, cuts),
        in_specs=[pl.BlockSpec(memory_space=pltpu.SMEM)] + [vmem] * 4,
        out_specs=[vmem] * 3,
        out_shape=[jax.ShapeDtypeStruct((rows, 2 * mine.shape[1]), BF)] * 3,
        compiler_params=pltpu.CompilerParams(vmem_limit_bytes=24 * 2**20),
        cost_estimate=pl.CostEstimate(flops=0, bytes_accessed=10**7, transcendentals=0),
        name="join_shared",
    )(y, mine, low, high, behind)


def weights_kernel(n_sets, split, y_ref, *refs):
    sources, lhs_refs = refs[:16], refs[16 : 16 + 4 * n_sets]
    out_refs, (held, sems) = refs[16 + 4 * n_sets : -2], refs[-2:]
    rows, width = held.shape
    own = rows // 16

    @pl.when(pl.program_id(0) == 0)
    def _():
        copies = [
            pltpu.make_async_copy(
                sources[k].at[:, pl.ds(0, width)], held.at[pl.ds(k * own, own), :], sems.at[k])
            for k in range(16)
        ]
        for copy in copies:
            copy.start()
        for copy in copies:
            copy.wait()

    for k in range(n_sets):
        lhs = jnp.concatenate([ref[...] for ref in lhs_refs[4 * k : 4 * k + 4]], axis=0)
        total = dot_tn(lhs, held[...])
        if not split:
            out_refs[k][...] = total.astype(BF)
            continue
        for block in range(width // LANES // 2):
            even = total[:, 2 * block * LANES : (2 * block + 1) * LANES]
            odd = total[:, (2 * block + 1) * LANES : (2 * block + 2) * LANES]
            columns = slice(block * LANES, (block + 1) * LANES)
            out_refs[2 * k][:, columns] = jnp.where(y_ref[0] == 0, even, odd).astype(BF)
            out_refs[2 * k + 1][:, columns] = jnp.where(y_ref[0] == 0, odd, even).astype(BF)


def weight_grads(y, sources, lhs_sets, width, split=False):
    rows, units = lhs_sets[0][0].shape
    n_sets = len(lhs_sets)
    n_tiles = units // GRAD_TILE
    columns = width // 2 if split else width
    n_outs = 2 * n_sets if split else n_sets
    return pl.pallas_call(
        functools.partial(weights_kernel, n_sets, split),
        grid=(n_tiles,),
        in_specs=[pl.BlockSpec(memory_space=pltpu.SMEM)]
        + [pl.BlockSpec(memory_space=pl.ANY)] * 16
        + [pl.BlockSpec((rows, GRAD_TILE), lambda i: (0, i))] * (4 * n_sets),
        out_specs=[pl.BlockSpec((GRAD_TILE, columns), lambda i: (i, 0))] * n_outs,
        scratch_shapes=[pltpu.VMEM((4 * rows, width), BF), pltpu.SemaphoreType.DMA((16,))],
        out_shape=[jax.ShapeDtypeStruct((units, columns), BF)] * n_outs,
        compiler_params=pltpu.CompilerParams(vmem_limit_bytes=36 * 2**20),
        cost_estimate=pl.CostEstimate(
            flops=4 * 10**9 * n_sets * n_tiles, bytes_accessed=2 * 10**7, transcendentals=0),
        name="weight_grads",
    )(y, *sources, *[item for lhs in lhs_sets for item in lhs])


def feed_plain(normed, grad, named, expert, wg, wu, wd, router, experts, shared):
    logits = contract("td,cd->tc", normed, router)
    router_probs = jax.nn.softmax(logits[:, :experts], axis=-1)
    shared_scale = jax.nn.sigmoid(logits[:, experts : experts + 1])
    hot = (jnp.arange(experts) == expert).astype(F32)
    gate_here = jnp.sum(router_probs * hot, axis=1, keepdims=True) * named[:, None]
    is_shared = (jnp.arange(wg.shape[0]) < shared)[None]
    row_scale = jnp.where(is_shared, shared_scale, gate_here)
    act, slope = silu_parts(contract("td,cd->tc", normed, wg))
    up = contract("td,cd->tc", normed, wu)
    hidden = act * up
    hidden_scaled = (hidden * row_scale).astype(BF)
    grad_hidden = contract("td,fd->tf", grad, wd)
    dots = hidden * grad_hidden
    dot_shared = jnp.sum(jnp.where(is_shared, dots, 0.0), axis=1, keepdims=True)
    dot_expert = jnp.sum(jnp.where(is_shared, 0.0, dots), axis=1, keepdims=True) * named[:, None]
    grad_pre = grad_hidden * row_scale
    grad_gate = (grad_pre * up * slope).astype(BF)
    grad_up = (grad_pre * act).astype(BF)
    grad_normed = contract("tc,cd->td", grad_gate, wg) + contract("tc,cd->td", grad_up, wu)
    extra = jnp.concatenate([dot_expert * hot, dot_shared], axis=1)
    extra = jnp.pad(extra, ((0, 0), (0, LANES - extra.shape[1])))
    out = contract("tf,fd->td", hidden_scaled, wd)
    return (
        jnp.concatenate([grad_normed, extra], axis=1),
        out,
        contract("tc,td->cd", grad_gate, normed),
        contract("tc,td->cd", grad_up, normed),
        contract("tf,td->fd", hidden_scaled, grad),
    )


def ring_perm(move):
    pairs = []
    for me in range(32):
        z, x, y, c = me // 8, me // 4 % 2, me // 2 % 2, me % 2
        z, x, y, c = move(z, x, y, c)
        pairs.append((me, ((z * 2 + x) * 2 + y) * 2 + c))
    return pairs


MOVES = {
    "core": lambda z, x, y, c: (z, x, y, 1 - c),
    "y": lambda z, x, y, c: (z, x, 1 - y, c),
    "yc": lambda z, x, y, c: (z, x, 1 - y, 1 - c),
    "x": lambda z, x, y, c: (z, 1 - x, y, c),
    "z1": lambda z, x, y, c: ((z + 1) % 4, x, y, c),
    "z2": lambda z, x, y, c: ((z + 2) % 4, x, y, c),
    "z3": lambda z, x, y, c: ((z + 3) % 4, x, y, c),
}


def send(value, link):
    return lax.ppermute(value, ALL, ring_perm(MOVES[link]))


def sync(*values):
    return lax.optimization_barrier(values)


def pick(value, place, axis=0):
    return lax.dynamic_index_in_dim(value, place, axis, keepdims=False)


def put(value, block, place, axis=0):
    return lax.dynamic_update_index_in_dim(value, block, place, axis)


def in_order(mine, other, bit, axis):
    return jnp.where(bit == 0, jnp.stack([mine, other], axis=axis), jnp.stack([other, mine], axis=axis))


def on_device_ring(
    hidden_in, seg_ids, routes, out_grad, norm_gain1, w_query, w_key, w_value, b_qkv, w_out,
    norm_gain2, w_router, shared_gate, sh_gate, sh_up, sh_down, ex_gate, ex_up, ex_down,
):
    micro, tok, width = hidden_in.shape
    experts = w_router.shape[1]
    rows_w = w_query.shape[0]
    top_count = routes.shape[2]
    my_exp, my_fsdp = lax.axis_index("expert"), lax.axis_index("fsdp")
    z, x, y, c = my_exp // 2, lax.rem(my_exp, 2), my_fsdp // 2, lax.rem(my_fsdp, 2)
    n_exp, n_fsdp, n_all = 8, 4, 32
    heads_dev = HEADS // n_fsdp
    wide = heads_dev * HEAD
    seq, own = tok * n_fsdp, micro * tok
    ex_cols = ex_gate.shape[2]
    sh_cols = SHARED_FF // 16
    full_cols = sh_cols // LANES * LANES
    rest_cols = sh_cols - full_cols
    unit_cols = 3 * sh_cols

    def slot(step, other):
        return lax.rem(z + 4 - step, 4) * 2 + (1 - x if other else x)

    def by_fsdp(three):
        rows = three.shape[0]
        split = three.reshape(rows, 3, 2, 2, heads_dev // 2, 2, HEAD)
        return split.transpose(5, 2, 0, 3, 1, 4, 6).reshape(n_fsdp, rows, 3 * wide)

    def from_fsdp(blocks):
        rows = blocks.shape[1]
        split = blocks.reshape(2, 2, rows, 2, 3, heads_dev // 2, HEAD)
        return split.transpose(4, 2, 1, 3, 5, 0, 6).reshape(3, rows, width)

    small = jnp.concatenate([w_router.T, shared_gate[None], norm_gain1[None], norm_gain2[None], b_qkv], axis=0)
    n_small = small.shape[0]
    small = [small.reshape(1, n_small * rows_w)]
    for _ in range(3):
        small.append(send(small[-1], "z1"))
    small = jnp.concatenate(small)
    qkv = by_fsdp(jnp.stack([w_query, w_key, w_value], axis=1))
    arrived = [send(pick(qkv, lax.bitwise_xor(my_fsdp, k)), link) for k, link in ((1, "core"), (2, "y"), (3, "yc"))]
    seg_near, seg_far = send(seg_ids, "core"), send(seg_ids, "y")
    grad_own = out_grad.reshape(own, width)
    names = jnp.pad(routes.reshape(own, top_count).astype(BF), ((0, 0), (0, LANES - top_count)))
    g_own = [jnp.concatenate([grad_own, names], axis=1)]
    g_pair = []
    routed_mine = jnp.concatenate([ex_gate[0].T, ex_up[0].T, ex_down[0]], axis=0)
    small, arrived, g_own[0], seg_near, seg_far, routed_mine = sync(
        small, arrived, g_own[0], seg_near, seg_far, routed_mine)
    for k in range(3):
        qkv = put(qkv, arrived[k], lax.bitwise_xor(my_fsdp, k + 1))
    block = jnp.concatenate(
        [qkv.reshape(n_fsdp * rows_w, 3 * wide), w_out.reshape(rows_w, n_fsdp, wide).reshape(-1, wide)], axis=1)

    following = send(block, "z1")
    small = jnp.concatenate([small, send(small, "x")])
    at_pair = send(sync(block, small)[0], "x")
    small = jnp.concatenate([small, send(small, "y")])
    small = jnp.concatenate([small, send(small, "core")])
    places = jnp.stack(
        [slot(step, other) * 4 + lax.bitwise_xor(my_fsdp, k) for k in (0, 2, 1, 3) for other in range(2) for step in range(4)])
    choice = (jnp.arange(n_all)[:, None] == places[None]).astype(BF)
    small = dot_nn(choice, small).astype(BF).reshape(n_all, n_small, rows_w).transpose(1, 0, 2).reshape(n_small, width)
    router_rows = small[: experts + 1]
    gain_one = small[experts + 1].astype(F32)
    gain_two = small[experts + 2].astype(F32)
    bias = pick(by_fsdp(small[experts + 3 :].astype(F32)[None]), my_fsdp)
    hidden = hidden_in.reshape(own, width).astype(F32)
    scaled_one, inverse_one = normalize(hidden)
    normed_one = (scaled_one * gain_one).astype(BF).reshape(micro, tok, width)
    seq_far, seq_near = send(normed_one, "y"), send(normed_one, "core")
    seg_last = send(seg_far, "core")
    weights = jnp.zeros((n_exp,) + block.shape, BF)
    weights = put(weights, block, slot(0, 0))

    def ring_put(weights, step, mine, other):
        return put(put(weights, mine, slot(step, 0)), other, slot(step, 1))

    a_blocks = [routed_mine[k * 264 : (k + 1) * 264] for k in range(4)]
    got_blocks = []
    current = following
    (current, at_pair, seq_far, seq_near, seg_last, normed_one, a_blocks, bias, router_rows) = sync(
        current, at_pair, seq_far, seq_near, seg_last, normed_one, a_blocks, bias, router_rows)
    weights = put(weights, at_pair, slot(0, 1))
    seq_last = send(seq_far, "core")

    def by_owner(weight):
        full = weight[:, : 16 * full_cols].reshape(rows_w, 16, full_cols).transpose(1, 0, 2)
        rest = weight[:, 16 * full_cols :].reshape(rows_w, 16, rest_cols).transpose(1, 0, 2)
        return full, rest

    pieces = [by_owner(weight) for weight in (sh_gate, sh_up, sh_down)]
    shared_w = jnp.concatenate([piece[0] for piece in pieces] + [piece[1] for piece in pieces], axis=2)
    shared_w = shared_w.reshape(4, 2, 2, rows_w, unit_cols)

    def swap_core(blocks):
        mine, give = pick(blocks, c, 2), pick(blocks, 1 - c, 2)
        return in_order(mine, send(give, "core"), c, 2)

    def swap_z(blocks, k):
        return send(pick(blocks, lax.rem(z + k, 4)), f"z{k}")

    def swap_x(blocks):
        mine, give = pick(blocks, x, 1), pick(blocks, 1 - x, 1)
        return in_order(mine, send(give, "x"), x, 1)

    for step in (1, 2):
        at_pair = send(current, "x")
        following = send(current, "z1")
        got = send(a_blocks[step - 1], "y")
        if step == 2:
            shared_w = swap_core(shared_w)
        mine = current
        current, at_pair, got, mine, a_blocks, shared_w, seq_last = sync(
            following, at_pair, got, mine, a_blocks, shared_w, seq_last)
        got_blocks.append(got)
        weights = ring_put(weights, step, mine, at_pair)

    at_pair = send(current, "x")
    got = send(a_blocks[2], "y")
    shared_z = {1: swap_z(shared_w, 1), 3: swap_z(shared_w, 3)}
    current, at_pair, got, shared_z, shared_w, a_blocks, weights = sync(
        current, at_pair, got, shared_z, shared_w, a_blocks, weights)
    got_blocks.append(got)
    weights = ring_put(weights, 3, current, at_pair)

    got = send(a_blocks[3], "y")
    shared_z[2] = swap_z(shared_w, 2)
    wo_rows = weights[:, :, 3 * wide :].reshape(n_exp, rows_w, width)
    keep = lax.dynamic_slice_in_dim(wo_rows, 4 * c, 4, 0)
    arrived = send(lax.dynamic_slice_in_dim(wo_rows, 4 * (1 - c), 4, 0), "core")
    wo = in_order(keep, arrived, c, 1).reshape(wide, width)
    weights = weights.reshape(width, 4 * wide)
    order = lax.bitwise_xor(my_fsdp, jnp.arange(n_fsdp))
    places = (order[:, None] * tok + jnp.arange(tok)[None]).reshape(seq)
    seg_seq = jnp.concatenate([seg_ids, seg_near, seg_far, seg_last], axis=1)
    normed_seq = jnp.concatenate([normed_one, seq_near, seq_far, seq_last], axis=1).reshape(micro * seq, width)
    cosine, sine = angle_tables(places)
    tables = (cosine, sine, places[:, None], seg_seq.reshape(micro * seq, 1), places[None], seg_seq)
    weights, wo, tables, normed_seq, got, shared_z, shared_w, g_own[0] = sync(
        weights, wo, tables, normed_seq, got, shared_z, shared_w, g_own[0])
    got_blocks.append(got)
    for k in (1, 2, 3):
        shared_w = put(shared_w, shared_z[k], lax.rem(z + 4 - k, 4))
    shared_w = swap_x(shared_w)
    g_own.append(send(g_own[0], "z1"))
    qkv_seq, attended = attend(normed_seq, weights, bias, tables, seq)
    attn_part = contract("tc,cd->td", attended, wo).reshape(micro, n_fsdp, tok, width)
    last = (attn_part[:, 2] + send(attn_part[:, 3].astype(BF), "core").astype(F32)).astype(BF)
    near = attn_part[:, 0] + send(attn_part[:, 1].astype(BF), "core").astype(F32)
    last, near, shared_w, g_own, got_blocks = sync(last, near, shared_w, g_own, got_blocks)

    last = send(last, "y")
    g_pair.append(send(g_own[0], "x"))
    g_own.append(send(g_own[1], "z1"))
    shared_w = shared_w.reshape(16 * rows_w, unit_cols).T
    after_attn = hidden + near.reshape(own, width) + last.astype(F32).reshape(own, width)
    scaled_two, inverse_two = normalize(after_attn)
    normed_two = (scaled_two * gain_two).astype(BF)
    x_own, x_pair = [normed_two], []
    shared_w, x_own, after_attn, scaled_two, g_own, g_pair, got_blocks = sync(
        shared_w, x_own, after_attn, scaled_two, g_own, g_pair, got_blocks)

    half = unit_cols // 2
    arrived = [send(shared_w[:half], "y")]
    x_pair.append(send(x_own[0], "x"))
    g_pair.append(send(g_own[1], "x"))
    x_own.append(send(x_own[0], "z1"))
    g_own.append(send(g_own[2], "z1"))
    routed_other = jnp.concatenate(got_blocks, axis=0)
    pad = jnp.zeros((2 * GRAD_TILE - 2 * ex_cols, width), BF)
    routed_w = [
        jnp.concatenate(
            [routed_mine[k * ex_cols : (k + 1) * ex_cols], routed_other[k * ex_cols : (k + 1) * ex_cols], pad], axis=0)
        for k in range(3)
    ]

    def four(mine, other):
        return [mine, other, send(mine, "core"), send(other, "core")]

    arrived, shared_w, x_own, g_own, x_pair, g_pair, routed_w = sync(
        arrived, shared_w, x_own, g_own, x_pair, g_pair, routed_w)
    arrived.append(send(shared_w[half:], "y"))
    x_pair.append(send(x_own[1], "x"))
    g_pair.append(send(g_own[2], "x"))
    x_own.append(send(x_own[1], "z1"))
    x_four, g_four = [four(x_own[0], x_pair[0])], [four(g_own[k], g_pair[k]) for k in range(2)]
    behind = jnp.pad(router_rows, ((0, GRAD_TILE - sh_cols - experts - 1), (0, 0)))
    arrived, shared_w, x_four, g_four, x_own, g_own, x_pair, g_pair, routed_w, behind = sync(
        arrived, shared_w, x_four, g_four, x_own, g_own, x_pair, g_pair, routed_w, behind)
    rest_at = 3 * full_cols
    cuts = [
        [(k * full_cols, full_cols), (rest_at + k * rest_cols, rest_cols)] for k in range(3)
    ]
    y_place = y.reshape(1)
    shared_w = join_shared(y_place, shared_w, arrived[0], arrived[1], behind, cuts)
    g_pair.append(send(g_own[3], "x"))
    x_four.append(four(x_own[1], x_pair[1]))
    g_four.append(four(g_own[2], g_pair[2]))

    expert = my_exp.reshape(1)
    fed, near_sums, sums = [], [], []

    def core_sums(found):
        return [found[k].astype(F32) + send(found[2 + k], "core").astype(F32) for k in range(2)]

    def pair_sums(parts):
        return parts[0] + send(parts[1].astype(BF), "x").astype(F32)

    for step in range(4):
        shared_w, routed_w, x_four, g_four, x_own, x_pair, g_pair, near_sums, sums, fed = sync(
            shared_w, routed_w, x_four, g_four, x_own, x_pair, g_pair, near_sums, sums, fed)
        if step == 0:
            x_pair.append(send(x_own[2], "x"))
            x_own.append(send(x_own[2], "z1"))
            g_four.append(four(g_own[3], g_pair[3]))
        if step == 1:
            x_pair.append(send(x_own[3], "x"))
            x_four.append(four(x_own[2], x_pair[2]))
        if step == 2:
            x_four.append(four(x_own[3], x_pair[3]))
        if step >= 1:
            near_sums.append(core_sums(fed[step - 1][2]))
        if step >= 2:
            sums.append(pair_sums(near_sums[step - 2]))
        fed.append(feed(expert, x_four[step], g_four[step], shared_w, routed_w, experts, sh_cols))
    near_sums, sums, fed, x_four, g_four = sync(near_sums, sums, fed, x_four, g_four)

    x_blocks = [item for four_of in x_four for item in four_of]
    g_blocks = [item for four_of in g_four for item in four_of]
    shared_sets = [[fed[step][0][item] for step in range(4)] for item in range(3)]
    routed_sets = [[fed[step][1][item] for step in range(4)] for item in range(3)]
    flying = send(sums[1].astype(BF), "z1")
    sums.append(pair_sums(near_sums[2]))
    near_sums.append(core_sums(fed[3][2]))
    sg_mine, sg_give, su_mine, su_give = weight_grads(y_place, x_blocks, [shared_sets[1], shared_sets[2]], width, True)
    sums, near_sums, flying, sg_mine, sg_give, su_mine, su_give, x_blocks, g_blocks, shared_sets, routed_sets = sync(
        sums, near_sums, flying, sg_mine, sg_give, su_mine, su_give, x_blocks, g_blocks, shared_sets, routed_sets)
    sums.append(pair_sums(near_sums[3]))
    flying = send((sums[2] + flying.astype(F32)).astype(BF), "z1")
    sg_got = send(sg_give, "y")
    sd_mine, sd_give = weight_grads(y_place, g_blocks, [shared_sets[0]], width, True)
    (ed_grad,) = weight_grads(y_place, g_blocks, [routed_sets[0]], width)
    sums, flying, sg_got, su_give, sd_mine, sd_give, ed_grad, x_blocks, routed_sets, fed = sync(
        sums, flying, sg_got, su_give, sd_mine, sd_give, ed_grad, x_blocks, routed_sets, fed)
    flying = send((sums[3] + flying.astype(F32)).astype(BF), "z1")
    su_got = send(su_give, "y")
    out_near = [core_sums(fed[step][3]) for step in range(4)]
    grad_sum, out_near, su_got, sd_give, x_blocks, routed_sets, ed_grad = sync(
        sums[0] + flying.astype(F32), out_near, su_got, sd_give, x_blocks, routed_sets, ed_grad)

    own_logits = contract("td,cd->tc", normed_two, router_rows)
    own_probs = jax.nn.softmax(own_logits[:, :experts], axis=-1)
    own_scale = jax.nn.sigmoid(own_logits[:, experts])
    grad_probs = grad_sum[:, width : width + experts]
    grad_router = own_probs * (grad_probs - jnp.sum(own_probs * grad_probs, axis=-1, keepdims=True))
    grad_gate = grad_sum[:, width + experts] * own_scale * (1.0 - own_scale)
    grad_logits = jnp.concatenate([grad_router, grad_gate[:, None]], axis=1).astype(BF)
    grad_normed_two = grad_sum[:, :width] + contract("tc,cd->td", grad_logits, router_rows)
    router_part = contract("tc,td->cd", grad_logits, normed_two)
    grad_after = grad_own.astype(F32) + norm_back(grad_normed_two, scaled_two, inverse_two, gain_two)
    gain_two_part = jnp.sum(grad_normed_two * scaled_two, axis=0)
    low = grad_after.astype(BF).reshape(micro, tok, width)
    sd_got = send(sd_give, "y")
    out_sums = [pair_sums(out_near[0])]
    low, grad_after, out_sums, out_near, sd_got, x_blocks, routed_sets, ed_grad = sync(
        low, grad_after, out_sums, out_near, sd_got, x_blocks, routed_sets, ed_grad)
    far, near = send(low, "y"), send(low, "core")
    out_sums.append(pair_sums(out_near[1]))
    eg_grad, eu_grad = weight_grads(y_place, x_blocks, [routed_sets[1], routed_sets[2]], width)
    shared_grads = [
        (mine.astype(F32) + got.astype(F32)).astype(BF)
        for mine, got in ((sg_mine, sg_got), (su_mine, su_got), (sd_mine, sd_got))
    ]
    shared_grads = jnp.concatenate(
        [grad[:full_cols] for grad in shared_grads] + [grad[full_cols:sh_cols] for grad in shared_grads], axis=0)
    shared_grads = shared_grads.T.reshape(4, 2, 2, rows_w, unit_cols)
    far, near, low, grad_after, out_sums, out_near, eg_grad, eu_grad, ed_grad, shared_grads = sync(
        far, near, low, grad_after, out_sums, out_near, eg_grad, eu_grad, ed_grad, shared_grads)

    e_grads = (eg_grad, eu_grad, ed_grad)
    e_give = jnp.concatenate([grad[ex_cols : 2 * ex_cols] for grad in e_grads], axis=0)
    e_got = []
    shared_grads = swap_core(shared_grads)
    grad_attn = jnp.concatenate([low, near, far, send(far, "core")], axis=1).reshape(micro * seq, width)
    grad_lin, grad_normed_one = attend(normed_seq, weights, bias, tables, seq, (grad_attn, wo, qkv_seq))
    gain_one_part = jnp.sum(grad_normed_one * normed_seq.astype(F32), axis=0) / gain_one
    parts = grad_normed_one.reshape(micro, n_fsdp, tok, width)
    last = (parts[:, 2] + send(parts[:, 3].astype(BF), "core").astype(F32)).astype(BF)
    near = parts[:, 0] + send(parts[:, 1].astype(BF), "core").astype(F32)
    out_sums.append(pair_sums(out_near[2]))
    flying = send(out_sums[1].astype(BF), "z1")
    out_grad_part = contract("tc,td->cd", attended, grad_attn).astype(BF)
    split = out_grad_part.reshape(heads_dev, 2, HEAD // 2, width)
    keep = pick(split, c, 1)
    arrived = send(pick(split, 1 - c, 1), "core")
    wo_part = jnp.where(c == 0, jnp.concatenate([keep, arrived]), jnp.concatenate([arrived, keep]))
    grad_lin, gain_one_part, last, near, out_sums, out_near, flying, shared_grads, e_give, wo_part = sync(
        grad_lin, gain_one_part, last, near, out_sums, out_near, flying, shared_grads, e_give, wo_part)

    def panel_sum(panel, step):
        return pick(panel, slot(step, 0)).astype(F32) + send(pick(panel, slot(step, 1)), "x").astype(F32)

    far = send(last, "y")
    shared_z = {1: swap_z(shared_grads, 1), 3: swap_z(shared_grads, 3)}
    out_sums.append(pair_sums(out_near[3]))
    wo_sums = {step: panel_sum(wo_part, step) for step in (1, 2)}
    qkv_part = contract("td,tc->dc", normed_seq, grad_lin).astype(BF)
    bias_place = put(jnp.zeros((n_fsdp, 1, 3 * wide), F32), jnp.sum(grad_lin.astype(F32), axis=0)[None], my_fsdp)
    bias_place = from_fsdp(bias_place)[:, 0]
    small_part = jnp.concatenate([router_part, gain_one_part[None], gain_two_part[None], bias_place], axis=0)
    small_part = small_part.astype(BF).reshape(n_small, n_exp, n_fsdp, rows_w).transpose(1, 2, 0, 3)
    small_part = small_part.reshape(n_exp, n_fsdp * n_small * rows_w)
    behind_rows = 8
    small_part = jnp.pad(small_part, ((0, 0), (0, behind_rows * 3 * wide - small_part.shape[1])))
    panel = qkv_part.reshape(n_exp, n_fsdp * rows_w, 3 * wide)
    panel = jnp.concatenate([panel, small_part.reshape(n_exp, behind_rows, 3 * wide)], axis=1)
    far, out_sums, flying, panel, near, shared_z, shared_grads, wo_sums, wo_part, e_give = sync(
        far, out_sums, flying, panel, near, shared_z, shared_grads, wo_sums, wo_part, e_give)
    grad_normed_one = (near + far.astype(F32)).reshape(own, width)
    in_grad = grad_after + norm_back(grad_normed_one, scaled_one, inverse_one, gain_one)

    sums = {}
    for turn, step in enumerate((1, 2, 3, 0)):
        sums[step] = panel_sum(panel, step)
        e_got.append(send(e_give[turn * 264 : (turn + 1) * 264], "y"))
        if turn == 0:
            shared_z[2] = swap_z(shared_grads, 2)
            flying_out = send((out_sums[2] + flying.astype(F32)).astype(BF), "z1")
        elif turn == 1:
            for k in (1, 2, 3):
                shared_grads = put(shared_grads, shared_z[k], lax.rem(z + 4 - k, 4))
            flying = send(sums[1].astype(BF), "z1")
            flying_out = send((out_sums[3] + flying_out.astype(F32)).astype(BF), "z1")
            flying_wo = send(wo_sums[1].astype(BF), "z1")
            wo_sums[3] = panel_sum(wo_part, 3)
            shared_x = [send(pick(shared_grads, 1 - x, 1)[:2], "x")]
        elif turn == 2:
            flying = send((sums[2] + flying.astype(F32)).astype(BF), "z1")
            flying_wo = send((wo_sums[2] + flying_wo.astype(F32)).astype(BF), "z1")
            wo_sums[0] = panel_sum(wo_part, 0)
            shared_x.append(send(pick(shared_grads, 1 - x, 1)[2:], "x"))
        else:
            flying = send((sums[3] + flying.astype(F32)).astype(BF), "z1")
            flying_wo = send((wo_sums[3] + flying_wo.astype(F32)).astype(BF), "z1")
            shared_grads = in_order(pick(shared_grads, x, 1), jnp.concatenate(shared_x), x, 1)
        if turn == 0:
            sums, e_got, shared_z, shared_grads, e_give, panel, flying_out, wo_part = sync(
                sums, e_got, shared_z, shared_grads, e_give, panel, flying_out, wo_part)
        elif turn < 3:
            sums, e_got, shared_x, shared_grads, flying, e_give, panel, flying_out, flying_wo, wo_sums, wo_part = sync(
                sums, e_got, shared_x, shared_grads, flying, e_give, panel, flying_out, flying_wo, wo_sums, wo_part)
    hidden_out = (after_attn + out_sums[0] + flying_out.astype(F32)).astype(BF)
    out_own = wo_sums[0] + flying_wo.astype(F32)
    total = (sums[0] + flying.astype(F32)).astype(BF)

    total, shared_grads, e_got = sync(total, shared_grads, e_got)
    count = n_fsdp * rows_w
    small_sum = total[count:].reshape(-1)[: n_fsdp * n_small * rows_w].reshape(n_fsdp, n_small * rows_w)
    small_sum = jnp.pad(small_sum, ((0, 0), (0, 3 * wide - n_small * rows_w)))
    blocks = jnp.concatenate([total[:count, : 3 * wide].reshape(n_fsdp, rows_w, 3 * wide), small_sum[:, None]], axis=1)
    qkv_own = blocks
    for k, link in ((1, "core"), (2, "y"), (3, "yc")):
        place = lax.bitwise_xor(my_fsdp, k)
        qkv_own = put(qkv_own, send(pick(blocks, place), link), place)
    small_own = jnp.sum(qkv_own[:, rows_w, : n_small * rows_w].astype(F32), axis=0).reshape(n_small, rows_w)
    qkv_own = from_fsdp(qkv_own[:, :rows_w]).astype(F32)
    shared_grads = shared_grads.reshape(16, rows_w, unit_cols)

    def from_owner(k):
        full = shared_grads[:, :, k * full_cols : (k + 1) * full_cols]
        rest = shared_grads[:, :, rest_at + k * rest_cols : rest_at + (k + 1) * rest_cols]
        return jnp.concatenate(
            [full.transpose(1, 0, 2).reshape(rows_w, -1), rest.transpose(1, 0, 2).reshape(rows_w, -1)], axis=1
        ).astype(F32)

    e_got = jnp.concatenate(e_got, axis=0)
    routed_grads = [
        grad[:ex_cols].astype(F32) + e_got[k * ex_cols : (k + 1) * ex_cols].astype(F32)
        for k, grad in enumerate(e_grads)
    ]
    return (
        hidden_out.reshape(micro, tok, width),
        in_grad.reshape(micro, tok, width),
        small_own[experts + 1],
        qkv_own[0],
        qkv_own[1],
        qkv_own[2],
        small_own[experts + 3 :],
        out_own,
        small_own[experts + 2],
        small_own[:experts].T,
        small_own[experts],
        from_owner(0),
        from_owner(1),
        from_owner(2),
        routed_grads[0].T[None],
        routed_grads[1].T[None],
        routed_grads[2][None],
    )


def on_device_any(
    hidden_in, seg_ids, routes, out_grad, norm_gain1, w_query, w_key, w_value, b_qkv, w_out,
    norm_gain2, w_router, shared_gate, sh_gate, sh_up, sh_down, ex_gate, ex_up, ex_down,
):
    links = Links()
    micro, tok, width = hidden_in.shape
    experts = w_router.shape[1]
    rows_w = w_query.shape[0]
    n_exp, n_fsdp, n_all = links.n_exp, links.n_fsdp, links.n_all
    my_exp, my_fsdp = links.my_exp, links.my_fsdp
    half_f, core_f = my_fsdp // 2, lax.rem(my_fsdp, 2)
    heads_dev = HEADS // n_fsdp
    wide = heads_dev * HEAD
    seq = tok * n_fsdp
    own = micro * tok
    sh_cols = SHARED_FF // n_all
    ex_cols = ex_gate.shape[2]

    def by_fsdp(three):
        rows = three.shape[0]
        split = three.reshape(rows, 3, 2, 2, heads_dev // 2, 2, HEAD)
        return split.transpose(5, 2, 0, 3, 1, 4, 6).reshape(n_fsdp, rows, 3 * wide)

    def from_fsdp(blocks):
        rows = blocks.shape[1]
        split = blocks.reshape(2, 2, rows, 2, 3, heads_dev // 2, HEAD)
        return split.transpose(4, 2, 1, 3, 5, 0, 6).reshape(3, rows, width)

    small = jnp.concatenate([w_router.T, shared_gate[None], norm_gain1[None], norm_gain2[None], b_qkv], axis=0)
    n_small = small.shape[0]
    small = lax.all_gather(small, ALL, axis=1, tiled=True)
    router_rows = small[: experts + 1]
    gain_one = small[experts + 1].astype(F32)
    gain_two = small[experts + 2].astype(F32)
    bias = by_fsdp(small[experts + 3 :].astype(F32)[None])
    bias = lax.dynamic_index_in_dim(bias, my_fsdp, 0, keepdims=False)

    x = hidden_in.reshape(own, width).astype(F32)
    scaled_one, inverse_one = normalize(x)
    normed_one = (scaled_one * gain_one).astype(BF)
    normed_seq = links.gather_seq(normed_one.reshape(micro, tok, width)).reshape(micro * seq, width)

    qkv = by_fsdp(jnp.stack([w_query, w_key, w_value], axis=1))
    qkv = links.swap_fsdp(qkv).reshape(n_fsdp * rows_w, 3 * wide)
    wqkv = links.gather_rows(qkv).reshape(width, 3 * wide)
    wo = lax.all_gather(w_out, ALL, axis=0, tiled=True).reshape(2, heads_dev, 2, HEAD, width)
    wo = lax.dynamic_index_in_dim(wo, core_f, 0, keepdims=False)
    wo = lax.dynamic_index_in_dim(wo, half_f, 1, keepdims=False).reshape(wide, width)

    tile_cols = sh_cols // LANES * LANES
    rest_cols = sh_cols - tile_cols

    def by_owner(weight):
        full = weight[:, : n_all * tile_cols].reshape(rows_w, n_all, tile_cols).transpose(1, 0, 2)
        rest = weight[:, n_all * tile_cols :].reshape(rows_w, n_all, rest_cols).transpose(1, 0, 2)
        return full, rest

    def from_owner(full, rest):
        return jnp.concatenate(
            [full.transpose(1, 0, 2).reshape(rows_w, -1), rest.transpose(1, 0, 2).reshape(rows_w, -1)], axis=1
        )

    pieces = [by_owner(weight) for weight in (sh_gate, sh_up, sh_down)]
    shared_w = jnp.concatenate([piece[0] for piece in pieces] + [piece[1] for piece in pieces], axis=2)
    shared_w = lax.all_to_all(shared_w, ALL, split_axis=0, concat_axis=0, tiled=True)
    shared_w = shared_w.reshape(width, 3 * sh_cols).T

    def three(rows):
        return [
            jnp.concatenate(
                [rows[k * tile_cols : (k + 1) * tile_cols],
                 rows[3 * tile_cols + k * rest_cols : 3 * tile_cols + (k + 1) * rest_cols]], axis=0)
            for k in range(3)
        ]

    shared_other = links.partner(shared_w, 2)
    routed_w = jnp.concatenate([ex_gate[0].T, ex_up[0].T, ex_down[0]], axis=0)
    halves = [[0, 2], [1, 3]]
    routed_w = lax.all_gather(routed_w, "fsdp", axis=0, axis_index_groups=halves)
    routed_w = [routed_w[:, k * ex_cols : (k + 1) * ex_cols].reshape(2 * ex_cols, width) for k in range(3)]
    units = 2 * (sh_cols + ex_cols)
    pad_rows = -(units + experts + 1) % LANES
    pad = jnp.zeros((pad_rows + experts + 1, width), BF)
    behind = (jnp.pad(router_rows, ((0, pad_rows), (0, 0))), pad, pad)
    wg, wu, wd = [
        jnp.concatenate(pieces, axis=0)
        for pieces in zip(three(shared_w), three(shared_other), routed_w, behind)
    ]
    shared_units = 2 * sh_cols

    grad_own = out_grad.reshape(own, width)
    names = jnp.pad(routes.reshape(own, -1).astype(BF), ((0, 0), (0, LANES - routes.shape[2])))
    grad_near = lax.all_gather(jnp.concatenate([grad_own, names], axis=1), "expert", axis=0)
    grad_far = links.partner(grad_near, 1)

    order = lax.bitwise_xor(my_fsdp, jnp.arange(n_fsdp))
    places = (order[:, None] * tok + jnp.arange(tok)[None]).reshape(seq)
    seg_seq = links.gather_seq(seg_ids)
    cosine, sine = angle_tables(places)
    tables = (cosine, sine, places[:, None], seg_seq.reshape(micro * seq, 1), places[None], seg_seq)
    qkv_seq, attended = attend(normed_seq, wqkv, bias, tables, seq)
    attn_part = contract("tc,cd->td", attended, wo).reshape(micro, n_fsdp, tok, width)
    attn_sum = links.sum_four([attn_part[:, k] for k in range(4)]).reshape(own, width)
    after_attn = x + attn_sum
    scaled_two, inverse_two = normalize(after_attn)
    normed_two = (scaled_two * gain_two).astype(BF)

    near = lax.all_gather(normed_two, "expert", axis=0, tiled=True)
    normed_all = jnp.concatenate([near, links.partner(near, 1)], axis=0)
    grad_all = jnp.concatenate([grad_near, grad_far], axis=0).reshape(2 * n_exp * own, -1)
    named = jnp.sum((grad_all[:, width : width + routes.shape[2]] == my_exp.astype(BF)).astype(F32), axis=1)
    grad_part, out_part, wg_grad, wu_grad, wd_grad = feed_plain(
        normed_all, grad_all[:, :width], named, my_exp, wg, wu, wd, router_rows, experts, shared_units
    )

    def summed(part):
        count = n_exp * own
        total = part[:count] + links.partner(part[count:].astype(BF), 1).astype(F32)
        return links.sum_rows(total.reshape(n_exp, own, -1))

    grad_sum, out_sum = summed(grad_part), summed(out_part)
    wg_grad, wu_grad, wd_grad = [item.astype(BF) for item in (wg_grad, wu_grad, wd_grad)]
    hidden_out = (after_attn + out_sum).astype(BF)

    own_logits = contract("td,cd->tc", normed_two, router_rows)
    own_probs = jax.nn.softmax(own_logits[:, :experts], axis=-1)
    own_scale = jax.nn.sigmoid(own_logits[:, experts])
    grad_probs = grad_sum[:, width : width + experts]
    grad_router = own_probs * (grad_probs - jnp.sum(own_probs * grad_probs, axis=-1, keepdims=True))
    grad_gate = grad_sum[:, width + experts] * own_scale * (1.0 - own_scale)
    grad_logits = jnp.concatenate([grad_router, grad_gate[:, None]], axis=1).astype(BF)
    grad_normed_two = grad_sum[:, :width] + contract("tc,cd->td", grad_logits, router_rows)
    router_part = contract("tc,td->cd", grad_logits, normed_two)

    grad_after = grad_own.astype(F32) + norm_back(grad_normed_two, scaled_two, inverse_two, gain_two)
    gain_two_part = jnp.sum(grad_normed_two * scaled_two, axis=0)

    grad_attn = links.gather_seq(grad_after.astype(BF).reshape(micro, tok, width)).reshape(micro * seq, width)
    grad_lin, grad_normed_one = attend(normed_seq, wqkv, bias, tables, seq, (grad_attn, wo, qkv_seq))
    gain_one_part = jnp.sum(grad_normed_one * normed_seq.astype(F32), axis=0) / gain_one
    grad_normed_one = grad_normed_one.reshape(micro, n_fsdp, tok, width)
    grad_normed_one = links.sum_four([grad_normed_one[:, k] for k in range(4)]).reshape(own, width)
    in_grad = grad_after + norm_back(grad_normed_one, scaled_one, inverse_one, gain_one)
    out_grad_part = contract("tc,td->cd", attended, grad_attn).astype(BF)
    qkv_part = contract("td,tc->dc", normed_seq, grad_lin).astype(BF)
    bias_part = jnp.sum(grad_lin.astype(F32), axis=0)

    out_place = jnp.zeros((2, heads_dev, 2, HEAD, width), BF)
    out_place = lax.dynamic_update_slice(
        out_place, out_grad_part.reshape(1, heads_dev, 1, HEAD, width), (core_f, 0, half_f, 0, 0)
    )
    out_own = lax.psum_scatter(
        out_place.reshape(width, width), ALL, scatter_dimension=0, tiled=True
    ).astype(F32)
    bias_place = jnp.zeros((n_fsdp, 1, 3 * wide), F32)
    bias_place = from_fsdp(lax.dynamic_update_index_in_dim(bias_place, bias_part[None], my_fsdp, 0))[:, 0]
    small_part = jnp.concatenate([router_part, gain_one_part[None], gain_two_part[None], bias_place], axis=0)
    small_part = small_part.astype(BF).reshape(n_small, n_exp, n_fsdp, rows_w).transpose(1, 2, 0, 3)
    behind_rows = -(-n_fsdp * n_small * rows_w // (3 * wide) // 8) * 8
    room = behind_rows * 3 * wide
    small_part = small_part.reshape(n_exp, n_fsdp * n_small * rows_w)
    small_part = jnp.pad(small_part, ((0, 0), (0, room - small_part.shape[1])))
    qkv_part = jnp.concatenate(
        [qkv_part.reshape(n_exp, n_fsdp * rows_w, 3 * wide), small_part.reshape(n_exp, behind_rows, 3 * wide)], axis=1
    )
    qkv_sum = links.sum_rows(qkv_part).astype(BF)
    small_sum = qkv_sum[n_fsdp * rows_w :].reshape(-1)[: n_fsdp * n_small * rows_w].reshape(n_fsdp, n_small * rows_w)
    small_sum = jnp.pad(small_sum, ((0, 0), (0, 3 * wide - n_small * rows_w)))
    qkv_sum = qkv_sum[: n_fsdp * rows_w].reshape(n_fsdp, rows_w, 3 * wide)
    qkv_own = links.swap_fsdp(jnp.concatenate([qkv_sum, small_sum[:, None]], axis=1))
    small_own = jnp.sum(qkv_own[:, rows_w, : n_small * rows_w].astype(F32), axis=0).reshape(n_small, rows_w)
    qkv_own = from_fsdp(qkv_own[:, :rows_w]).astype(F32)

    grads = (wg_grad, wu_grad, wd_grad)
    shared_mine = jnp.concatenate(
        [grad[:tile_cols] for grad in grads] + [grad[tile_cols:sh_cols] for grad in grads], axis=0)
    shared_give = jnp.concatenate(
        [grad[sh_cols : sh_cols + tile_cols] for grad in grads]
        + [grad[sh_cols + tile_cols : 2 * sh_cols] for grad in grads], axis=0)
    shared_got = links.partner(shared_give, 2)
    shared_grads = (shared_mine.astype(F32) + shared_got.astype(F32)).astype(BF)
    shared_own = lax.all_to_all(
        shared_grads.T.reshape(n_all, rows_w, 3 * sh_cols), ALL, split_axis=0, concat_axis=0, tiled=True
    )
    cut = 3 * tile_cols
    shared_own = [
        from_owner(
            shared_own[:, :, k * tile_cols : (k + 1) * tile_cols],
            shared_own[:, :, cut + k * rest_cols : cut + (k + 1) * rest_cols],
        ).astype(F32)
        for k in range(3)
    ]
    routed_grads = jnp.stack(
        [
            jnp.concatenate([grad[low : low + ex_cols] for grad in grads], axis=0)
            for low in (shared_units, shared_units + ex_cols)
        ]
    )
    routed_grads = lax.psum_scatter(routed_grads, "fsdp", scatter_dimension=0, axis_index_groups=halves).astype(F32)
    routed_grads = [routed_grads[k * ex_cols : (k + 1) * ex_cols] for k in range(3)]
    return (
        hidden_out.reshape(micro, tok, width),
        in_grad.reshape(micro, tok, width),
        small_own[experts + 1],
        qkv_own[0],
        qkv_own[1],
        qkv_own[2],
        small_own[experts + 3 :],
        out_own,
        small_own[experts + 2],
        small_own[:experts].T,
        small_own[experts],
        shared_own[0],
        shared_own[1],
        shared_own[2],
        routed_grads[0].T[None],
        routed_grads[1].T[None],
        routed_grads[2][None],
    )


def solution(mesh):
    rows = P(ALL, None)
    tokens = P(None, ALL, None)
    in_specs = (
        tokens, P(None, ALL), tokens, tokens, P(ALL), rows, rows, rows, P(None, ALL), rows,
        P(ALL), rows, P(ALL), rows, rows, rows,
        P("expert", None, "fsdp"), P("expert", None, "fsdp"), P("expert", "fsdp", None),
    )
    out_specs = (
        tokens, tokens, P(ALL), rows, rows, rows, P(None, ALL), rows, P(ALL), rows, P(ALL),
        rows, rows, rows,
        P("expert", None, "fsdp"), P("expert", None, "fsdp"), P("expert", "fsdp", None),
    )
    on_device = on_device_ring if mesh.shape["expert"] == 8 and mesh.shape["fsdp"] == 4 else on_device_any
    return jax.shard_map(on_device, mesh=mesh, in_specs=in_specs, out_specs=out_specs, check_vma=False)
```

time: 1090 us -> 861 us (0.79)
  waiting for transfers between devices: 547 us -> 340 us
  Pallas kernels: 184 us -> 154 us
  starting transfers between devices: 122 us -> 93.2 us
  local copies, waits for them, and re-layouts: 116 us -> 140 us
  other arithmetic: 83.3 us -> 106 us
  between operations: 16.6 us -> 4.7 us
    ppermute x125 -> x134, waiting for transfers between devices: 547 us -> 340 us  [send(): return lax.ppermute(value, ALL, ring_perm(MOVES[link]))]
    pallas_call x5 -> x9, Pallas kernels: 170 us -> 133 us  [the longest x4 88.4 us: feed(): pl.pallas_call(functools.partial(feed_kernel, experts, shared), in_specs=...]
    add x11 -> x37, other arithmetic: 6.43 us -> 34.9 us  [the longest x16 11.5 us: core_sums(): found[k].astype(F32) + send(found[2 + k], 'core').astype(F32)]
    concatenate x5 -> x13, other arithmetic: 4.33 us -> 29.2 us  [the longest x1 15.1 us: on_device_ring(): jnp.concatenate([routed_mine[k * ex_cols:(k + 1) * ex_cols], routed_other...]
    another operation x10 -> x3, other arithmetic: 20 us -> 0.17 us  [the longest x1 0.14 us: in_order(): jnp.stack([mine, other], axis=axis)]
    ppermute x125 -> x134, starting transfers between devices: 112 us -> 93.2 us  [send(): return lax.ppermute(value, ALL, ring_perm(MOVES[link]))]
    slice x22 -> x43, local copies, waits for them, and re-layouts: 9.29 us -> 26.4 us  [the longest x1 4.46 us: on_device_ring(): a_blocks = [routed_mine[k * 264:(k + 1) * 264] for k in range(4)]]
    convert_element_type x32 -> x22, other arithmetic: 26.9 us -> 18.1 us  [the longest x3 3.58 us: from_owner(): return jnp.concatenate([full.transpose(1, 0, 2).reshape(rows_w, -1), rest...]
  transfers between devices with their start and end apart: 128 -> 134, of which waited for: 45 -> 44; matrix products, arithmetic and copies ran while one was open for 17% -> 20% of each run, Pallas kernels for 10% -> 17%
where the time goes in v2:
time: 861 us; the launch traced here: 851 us
  waiting for transfers between devices  340 us (39%)
  Pallas kernels  154 us (18%)
  local copies, waits for them, and re-layouts  140 us (16%)
  other arithmetic  106 us (12%)
  starting transfers between devices  93.2 us (11%)
  matrix products  12.6 us (1%)
    ppermute x134, waiting for transfers between devices, send(): return lax.ppermute(value, ALL, ring_perm(MOVES[link]))  340 us
    ppermute x134, starting transfers between devices, send(): return lax.ppermute(value, ALL, ring_perm(MOVES[link]))  93.2 us
    pallas_call x4, Pallas kernels, feed(): pl.pallas_call(functools.partial(feed_kernel, experts, shared), in_specs=...  88.4 us
    unnamed x454, local copies, waits for them, and re-layouts  50.4 us
    pallas_call x4, Pallas kernels, weight_grads(): pl.pallas_call(functools.partial(weights_kernel, n_sets, split), grid=(n_...  42.6 us
  transfers between devices with their start and end apart: 134, of which 44 were waited for; matrix products, arithmetic and copies ran while one was open for 20% of the time, Pallas kernels for 17%

profile of v2, /device:TPU:0, one launch (start us, length us, event | category | flops | bytes accessed | tf_op | source)
XLA Modules:
  0.0 850.6 jit_solution(3448929326033477836)
XLA Ops:
  57.2 11.1 %collective-permute-done.8 = bf16[256,2048]{1,0:T(8,128)(2,1)} collective-permute-done((bf16[256,2048]{1,0:T(8,128)(2,1)}, bf16[256,2048]{1,0:T(8,128)(2,1)}, u32[]{:S(2)}, u32[]{:S(2)}) %collective-permute-start.8) | collective-permute-done | bytes 1048608 | tf_op jit(solution)/shard_map/ppermute | solution.py:460
  103.4 22.3 %collective-permute-done.20 = bf16[256,2048]{1,0:T(8,128)(2,1)S(1)} collective-permute-done((bf16[256,2048]{1,0:T(8,128)(2,1)}, bf16[256,2048]{1,0:T(8,128)(2,1)S(1)}, u32[]{:S(2)}, u32[]{:S(2)}) %collective-permute-start.20) | collective-permute-done | bytes 1048608 | tf_op jit(solution)/shard_map/ppermute | solution.py:460
  133.4 12.6 %collective-permute-done.26 = bf16[2,2,64,1056]{3,2,1,0:T(8,128)(2,1)S(1)} collective-permute-done((bf16[2,2,64,1056]{3,2,1,0:T(8,128)(2,1)S(1)}, bf16[2,2,64,1056]{3,2,1,0:T(8,128)(2,1)S(1)}, u32[]{:S(2)}, u32[]{:S(2)}) %collective-permute-start.26) | collective-permute-done | bytes 540704 | tf_op jit(solution)/shard_map/ppermute | solution.py:460
  146.1 9.1 %collective-permute-done.27 = bf16[2,2,64,1056]{3,2,1,0:T(8,128)(2,1)S(1)} collective-permute-done((bf16[2,2,64,1056]{3,2,1,0:T(8,128)(2,1)S(1)}, bf16[2,2,64,1056]{3,2,1,0:T(8,128)(2,1)S(1)}, u32[]{:S(2)}, u32[]{:S(2)}) %collective-permute-start.27) | collective-permute-done | bytes 540704 | tf_op jit(solution)/shard_map/ppermute | solution.py:460
  179.9 21.2 %collective-permute-done.30 = bf16[2,2,64,1056]{3,2,1,0:T(8,128)(2,1)S(1)} collective-permute-done((bf16[2,2,64,1056]{3,2,1,0:T(8,128)(2,1)S(1)}, bf16[2,2,64,1056]{3,2,1,0:T(8,128)(2,1)S(1)}, u32[]{:S(2)}, u32[]{:S(2)}) %collective-permute-start.30) | collective-permute-done | bytes 540704 | tf_op jit(solution)/shard_map/ppermute | solution.py:460
  225.9 23.7 %collective-permute-done.33 = bf16[4,2,64,1056]{3,2,1,0:T(8,128)(2,1)} collective-permute-done((bf16[4,2,64,1056]{3,2,1,0:T(8,128)(2,1)S(1)}, bf16[4,2,64,1056]{3,2,1,0:T(8,128)(2,1)}, u32[]{:S(2)}, u32[]{:S(2)}) %collective-permute-start.33) | collective-permute-done | bytes 1081376 | tf_op jit(solution)/shard_map/ppermute | solution.py:460
  278.3 15.1 %fusion.2 = (bf16[768,2048]{1,0:T(8,128)(2,1)}, bf16[768,2048]{1,0:T(8,128)(2,1)}, bf16[768,2048]{1,0:T(8,128)(2,1)}) fusion(bf16[264,2048]{1,0:T(8,128)(2,1)} %collective-permute-done.29, bf16[264,2048]{1,0:T(8,128)(2,1)S(1)} %copy-done.148, bf16[352,2048]{1,0:T(8,128)(2,1)S(1)} %copy-done.119, bf16[768]{0:T(1024)(128)(2,1)S(1)} %pad.75.clone, ...), kind=kLoop, calls=%fused_computation.10 | loop fusion | flops 45613056 | bytes 18089472 | tf_op jit(solution)/shard_map/concatenate | solution.py:651
  303.2 13.1 %collective-permute-done.50.refs_0_.refs_8_ = bf16[128,2048]{1,0:T(8,128)(2,1)S(1)} collective-permute-done((bf16[128,2048]{1,0:T(8,128)(2,1)S(1)}, bf16[128,2048]{1,0:T(8,128)(2,1)S(1)}, u32[]{:S(2)}, u32[]{:S(2)}) %collective-permute-start.50) | collective-permute-done | bytes 524320 | tf_op jit(solution)/shard_map/ppermute | solution.py:460
  320.8 12.5 %collective-permute-done.52.refs_5_.refs_9_ = bf16[128,2176]{1,0:T(8,128)(2,1)} collective-permute-done((bf16[128,2176]{1,0:T(8,128)(2,1)}, bf16[128,2176]{1,0:T(8,128)(2,1)}, u32[]{:S(2)}, u32[]{:S(2)}) %collective-permute-start.52) | collective-permute-done | bytes 557088 | tf_op jit(solution)/shard_map/ppermute | solution.py:460
  353.2 22.0 %feed.4 = (bf16[512,384]{1,0:T(8,128)(2,1)}, bf16[512,384]{1,0:T(8,128)(2,1)}, bf16[512,384]{1,0:T(8,128)(2,1)}, bf16[512,768]{1,0:T(8,128)(2,1)}, bf16[512,768]...) custom-call(s32[1]{0:T(128)} %bitcast.98.expert_ref, ...), custom_call_target="tpu_custom_call" | custom-call | flops 16000000000 | bytes 30000000 | tf_op jit(solution)/shard_map/feed/pallas_call | solution.py:299
  378.2 22.0 %feed.5 = (bf16[512,384]{1,0:T(8,128)(2,1)}, bf16[512,384]{1,0:T(8,128)(2,1)}, bf16[512,384]{1,0:T(8,128)(2,1)}, bf16[512,768]{1,0:T(8,128)(2,1)}, bf16[512,768]...) custom-call(s32[1]{0:T(128)} %bitcast.98.expert_ref, ...), custom_call_target="tpu_custom_call" | custom-call | flops 16000000000 | bytes 30000000 | tf_op jit(solution)/shard_map/feed/pallas_call | solution.py:299
  403.1 22.2 %feed.6 = (bf16[512,384]{1,0:T(8,128)(2,1)}, bf16[512,384]{1,0:T(8,128)(2,1)}, bf16[512,384]{1,0:T(8,128)(2,1)}, bf16[512,768]{1,0:T(8,128)(2,1)}, bf16[512,768]...) custom-call(s32[1]{0:T(128)} %bitcast.98.expert_ref, ...), custom_call_target="tpu_custom_call" | custom-call | flops 16000000000 | bytes 30000000 | tf_op jit(solution)/shard_map/feed/pallas_call | solution.py:299
  429.6 22.2 %feed.7 = (bf16[512,384]{1,0:T(8,128)(2,1)}, bf16[512,384]{1,0:T(8,128)(2,1)}, bf16[512,384]{1,0:T(8,128)(2,1)}, bf16[512,768]{1,0:T(8,128)(2,1)}, bf16[512,768]...) custom-call(s32[1]{0:T(128)} %bitcast.98.expert_ref, ...), custom_call_target="tpu_custom_call" | custom-call | flops 16000000000 | bytes 30000000 | tf_op jit(solution)/shard_map/feed/pallas_call | solution.py:299
  475.7 10.1 %weight_grads.6 = bf16[768,2048]{1,0:T(8,128)(2,1)S(1)} custom-call(s32[1]{0:T(128)} %bitcast.97.y_ref, bf16[128,2176]{1,0:T(8,128)(2,1)S(1)} %copy-done.17, bf16[128,2176]{1,0:T(8,128)(2,1)} %collective-permute-done.37.refs_5_.refs_1_, bf16[128,2176]{1,0:T(8,128)(2,1)S(1)} %copy-done.34, bf16[128,2176]{1,0:T(8,128)(2,1)} %collective-permute-done.47.refs_7_.refs_3_, ...), custom_call_target="tpu_custom_call" | custom-call | flops 8000000000 | bytes 20000000 | tf_op jit(solution)/shard_map/weight_grads/pallas_call | solution.py:391
  509.5 9.0 %collective-permute-done.82 = bf16[128,2176]{1,0:T(8,128)(2,1)S(1)} collective-permute-done((bf16[128,2176]{1,0:T(8,128)(2,1)S(1)}, bf16[128,2176]{1,0:T(8,128)(2,1)S(1)}, u32[]{:S(2)}, u32[]{:S(2)}) %collective-permute-start.82) | collective-permute-done | bytes 557088 | tf_op jit(solution)/shard_map/ppermute | solution.py:460
  559.7 16.9 %weight_grads.7 = (bf16[768,2048]{1,0:T(8,128)(2,1)S(1)}, bf16[768,2048]{1,0:T(8,128)(2,1)}) custom-call(s32[1]{0:T(128)} %bitcast.97.y_ref, bf16[128,2048]{1,0:T(8,128)(2,1)S(1)} %copy-done.7, bf16[128,2048]{1,0:T(8,128)(2,1)S(1)} %copy-done.44, bf16[128,2048]{1,0:T(8,128)(2,1)S(1)} %copy-done.47, bf16[128,2048]{1,0:T(8,128)(2,1)S(1)} %copy-done.50, ...), custom_call_target="tpu_custom_call" | custom-call | flops 16000000000 | bytes 20000000 | tf_op jit(solution)/shard_map/weight_grads/pallas_call | solution.py:391
  596.0 13.3 %attend_back.1 = (bf16[512,1536]{1,0:T(8,128)(2,1)S(1)}, f32[512,2048]{1,0:T(8,128)S(1)}) custom-call(bf16[512,2048]{1,0:T(8,128)(2,1)S(1)} %bitcast.351, bf16[512,2048]{1,0:T(8,128)(2,1)S(1)} %bitcast.349, bf16[512,1536]{1,0:T(8,128)(2,1)S(1)} %copy-done.80, f32[256,128]{1,0:T(8,128)S(1)} %copy-done.21, f32[256,128]{1,0:T(8,128)S(1)} %copy-done.23, ...), custom_call_target="tpu_custom_call" | custom-call | flops 5000000000 | bytes 10000000 | tf_op jit(solution)/shard_map/attend_back/pallas_call | solution.py:207
  650.3 8.3 collective-permute-done.107
  685.1 22.3 %collective-permute-done.112 = bf16[2,2,64,1056]{3,2,1,0:T(8,128)(2,1)S(1)} collective-permute-done((bf16[2,2,64,1056]{3,2,1,0:T(8,128)(2,1)}, bf16[2,2,64,1056]{3,2,1,0:T(8,128)(2,1)S(1)}, u32[]{:S(2)}, u32[]{:S(2)}) %collective-permute-start.112) | collective-permute-done | bytes 540704 | tf_op jit(solution)/shard_map/ppermute | solution.py:460
  716.8 29.0 %collective-permute-done.114 = bf16[264,1536]{1,0:T(8,128)(2,1)S(1)} collective-permute-done((bf16[264,1536]{1,0:T(8,128)(2,1)S(1)}, bf16[264,1536]{1,0:T(8,128)(2,1)S(1)}, u32[]{:S(2)}, u32[]{:S(2)}) %collective-permute-start.114) | collective-permute-done | bytes 811040 | tf_op jit(solution)/shard_map/ppermute | solution.py:460
  746.0 14.5 %collective-permute-done.118 = bf16[128,2048]{1,0:T(8,128)(2,1)S(1)} collective-permute-done((bf16[128,2048]{1,0:T(8,128)(2,1)S(1)}, bf16[128,2048]{1,0:T(8,128)(2,1)S(1)}, u32[]{:S(2)}, u32[]{:S(2)}) %collective-permute-start.118) | collective-permute-done | bytes 524320 | tf_op jit(solution)/shard_map/ppermute | solution.py:460
  771.0 16.3 %collective-permute-done.121 = bf16[264,1536]{1,0:T(8,128)(2,1)S(1)} collective-permute-done((bf16[264,1536]{1,0:T(8,128)(2,1)S(1)}, bf16[264,1536]{1,0:T(8,128)(2,1)S(1)}, u32[]{:S(2)}, u32[]{:S(2)}) %collective-permute-start.121) | collective-permute-done | bytes 811040 | tf_op jit(solution)/shard_map/ppermute | solution.py:460
  787.6 9.6 %collective-permute-done.123 = bf16[2,2,64,1056]{3,2,1,0:T(8,128)(2,1)S(1)} collective-permute-done((bf16[2,2,64,1056]{3,2,1,0:T(8,128)(2,1)S(1)}, bf16[2,2,64,1056]{3,2,1,0:T(8,128)(2,1)S(1)}, u32[]{:S(2)}, u32[]{:S(2)}) %collective-permute-start.123) | collective-permute-done | bytes 540704 | tf_op jit(solution)/shard_map/ppermute | solution.py:460
  802.3 20.0 %collective-permute-done.133 = bf16[64,2048]{1,0:T(8,128)(2,1)S(1)} collective-permute-done((bf16[64,2048]{1,0:T(8,128)(2,1)S(1)}, bf16[64,2048]{1,0:T(8,128)(2,1)S(1)}, u32[]{:S(2)}, u32[]{:S(2)}) %collective-permute-start.133) | collective-permute-done | bytes 262176 | tf_op jit(solution)/shard_map/ppermute | solution.py:460
  (985 shorter events, 447.4 us)
Async XLA Ops:
  40.6 27.7 %collective-permute-start.8 = (bf16[256,2048]{1,0:T(8,128)(2,1)}, bf16[256,2048]{1,0:T(8,128)(2,1)}, u32[]{:S(2)}, u32[]{:S(2)}) collective-permute-start(bf16[256,2048]{1,0:T(8,128)(2,1)} %pad_maximum_fusion.10), channel_id=1, source_target_pairs={{0,8},{1,9},{2,10},{3,11},{4,12},{5,13},{6,14},{7,15},{8,16},{9,17... | collective-permute-start | bytes 3145736 | tf_op jit(solution)/shard_map/ppermute | solution.py:460
  40.6 27.7 %collective-permute-start.10 = (bf16[256,2048]{1,0:T(8,128)(2,1)}, bf16[256,2048]{1,0:T(8,128)(2,1)}, u32[]{:S(2)}, u32[]{:S(2)}) collective-permute-start(bf16[256,2048]{1,0:T(8,128)(2,1)} %pad_maximum_fusion.10), channel_id=1, source_target_pairs={{0,4},{1,5},{2,6},{3,7},{4,0},{5,1},{6,2},{7,3},{8,12},{9,13},{10,... | collective-permute-start | bytes 3145736 | tf_op jit(solution)/shard_map/ppermute | solution.py:460
  68.3 28.1 %collective-permute-start.18 = (bf16[264,2048]{1,0:T(8,128)(2,1)}, bf16[264,2048]{1,0:T(8,128)(2,1)}, u32[]{:S(2)}, u32[]{:S(2)}) collective-permute-start(bf16[264,2048]{1,0:T(8,128)(2,1)} %get-tuple-element.768), channel_id=1, source_target_pairs={{0,2},{1,3},{2,0},{3,1},{4,6},{5,7},{6,4},{7,5},{8,10},{9,11},{10,... | collective-permute-start | bytes 3244040 | tf_op jit(solution)/shard_map/ppermute | solution.py:460
  98.2 27.6 %collective-permute-start.20 = (bf16[256,2048]{1,0:T(8,128)(2,1)}, bf16[256,2048]{1,0:T(8,128)(2,1)S(1)}, u32[]{:S(2)}, u32[]{:S(2)}) collective-permute-start(bf16[256,2048]{1,0:T(8,128)(2,1)} %collective-permute-done.16), channel_id=1, source_target_pairs={{0,8},{1,9},{2,10},{3,11},{4,12},{5,13},{6,14},{7,15},{8,16},{9,17... | collective-permute-start | bytes 3145736 | tf_op jit(solution)/shard_map/ppermute | solution.py:460
  125.8 29.4 %collective-permute-start.25 = (bf16[264,2048]{1,0:T(8,128)(2,1)S(1)}, bf16[264,2048]{1,0:T(8,128)(2,1)S(1)}, u32[]{:S(2)}, u32[]{:S(2)}) collective-permute-start(bf16[264,2048]{1,0:T(8,128)(2,1)S(1)} %copy-done.146), channel_id=1, source_target_pairs={{0,2},{1,3},{2,0},{3,1},{4,6},{5,7},{6,4},{7,5},{8,10},{9,11},{10,... | collective-permute-start | bytes 3244040 | tf_op jit(solution)/shard_map/ppermute | solution.py:460
  126.3 28.8 %collective-permute-start.24 = (bf16[256,2048]{1,0:T(8,128)(2,1)S(1)}, bf16[256,2048]{1,0:T(8,128)(2,1)S(1)}, u32[]{:S(2)}, u32[]{:S(2)}) collective-permute-start(bf16[256,2048]{1,0:T(8,128)(2,1)S(1)} %collective-permute-done.20), channel_id=1, source_target_pairs={{0,4},{1,5},{2,6},{3,7},{4,0},{5,1},{6,2},{7,3},{8,12},{9,13},{10,... | collective-permute-start | bytes 3145736 | tf_op jit(solution)/shard_map/ppermute | solution.py:460
  169.2 31.9 %collective-permute-start.29 = (bf16[264,2048]{1,0:T(8,128)(2,1)}, bf16[264,2048]{1,0:T(8,128)(2,1)}, u32[]{:S(2)}, u32[]{:S(2)}) collective-permute-start(bf16[264,2048]{1,0:T(8,128)(2,1)} %get-tuple-element.796), channel_id=1, source_target_pairs={{0,2},{1,3},{2,0},{3,1},{4,6},{5,7},{6,4},{7,5},{8,10},{9,11},{10,... | collective-permute-start | bytes 3244040 | tf_op jit(solution)/shard_map/ppermute | solution.py:460
  172.1 29.1 %collective-permute-start.30 = (bf16[2,2,64,1056]{3,2,1,0:T(8,128)(2,1)S(1)}, bf16[2,2,64,1056]{3,2,1,0:T(8,128)(2,1)S(1)}, u32[]{:S(2)}, u32[]{:S(2)}) collective-permute-start(bf16[2,2,64,1056]{3,2,1,0:T(8,128)(2,1)S(1)} %dynamic-slice_bitcast_fusion.15), channel_id=1, source_target_pairs={{0,16},{1,17},{2,18},{3,19},{4,20},{5,21},{6,22},{7,23},{8,24},{9,... | collective-permute-start | bytes 1622024 | tf_op jit(solution)/shard_map/ppermute | solution.py:460
  221.8 27.8 %collective-permute-start.33 = (bf16[4,2,64,1056]{3,2,1,0:T(8,128)(2,1)S(1)}, bf16[4,2,64,1056]{3,2,1,0:T(8,128)(2,1)}, u32[]{:S(2)}, u32[]{:S(2)}) collective-permute-start(bf16[4,2,64,1056]{3,2,1,0:T(8,128)(2,1)S(1)} %get-tuple-element.1534), channel_id=1, source_target_pairs={{0,4},{1,5},{2,6},{3,7},{4,0},{5,1},{6,2},{7,3},{8,12},{9,13},{10,... | collective-permute-start | bytes 3244040 | tf_op jit(solution)/shard_map/ppermute | solution.py:460
  222.5 30.8 %collective-permute-start.34 = (bf16[128,2176]{1,0:T(8,128)(2,1)S(1)}, bf16[128,2176]{1,0:T(8,128)(2,1)}, u32[]{:S(2)}, u32[]{:S(2)}) collective-permute-start(bf16[128,2176]{1,0:T(8,128)(2,1)S(1)} %fusion.30.refs_4_.refs_0_), channel_id=1, source_target_pairs={{0,8},{1,9},{2,10},{3,11},{4,12},{5,13},{6,14},{7,15},{8,16},{9,17... | collective-permute-start | bytes 1671176 | tf_op jit(solution)/shard_map/ppermute | solution.py:460
  301.6 31.7 %collective-permute-start.43 = (bf16[528,1024]{1,0:T(8,128)(2,1)}, bf16[528,1024]{1,0:T(8,128)(2,1)}, u32[]{:S(2)}, u32[]{:S(2)}) collective-permute-start(bf16[528,1024]{1,0:T(8,128)(2,1)} %slice.305), channel_id=1, source_target_pairs={{0,2},{1,3},{2,0},{3,1},{4,6},{5,7},{6,4},{7,5},{8,10},{9,11},{10,... | collective-permute-start | bytes 3244040 | tf_op jit(solution)/shard_map/ppermute | solution.py:460
  340.6 34.6 %collective-permute-start.58 = (bf16[128,2176]{1,0:T(8,128)(2,1)S(1)}, bf16[128,2176]{1,0:T(8,128)(2,1)S(1)}, u32[]{:S(2)}, u32[]{:S(2)}) collective-permute-start(bf16[128,2176]{1,0:T(8,128)(2,1)S(1)} %copy-done.31), channel_id=1, source_target_pairs={{0,1},{1,0},{2,3},{3,2},{4,5},{5,4},{6,7},{7,6},{8,9},{9,8},{10,11... | collective-permute-start | bytes 1671176 | tf_op jit(solution)/shard_map/ppermute | solution.py:460
  546.7 37.9 %collective-permute-start.94 = (bf16[2,64,2048]{2,1,0:T(8,128)(2,1)}, bf16[2,64,2048]{2,1,0:T(8,128)(2,1)}, u32[]{:S(2)}, u32[]{:S(2)}) collective-permute-start(bf16[2,64,2048]{2,1,0:T(8,128)(2,1)} %bitcast.386), channel_id=1, source_target_pairs={{0,2},{1,3},{2,0},{3,1},{4,6},{5,7},{6,4},{7,5},{8,10},{9,11},{10,... | collective-permute-start | bytes 1572872 | tf_op jit(solution)/shard_map/ppermute | solution.py:460
  547.2 37.4 %collective-permute-start.95 = (bf16[2,64,2048]{2,1,0:T(8,128)(2,1)}, bf16[2,64,2048]{2,1,0:T(8,128)(2,1)}, u32[]{:S(2)}, u32[]{:S(2)}) collective-permute-start(bf16[2,64,2048]{2,1,0:T(8,128)(2,1)} %bitcast.387), channel_id=1, source_target_pairs={{0,1},{1,0},{2,3},{3,2},{4,5},{5,4},{6,7},{7,6},{8,9},{9,8},{10,11... | collective-permute-start | bytes 1572872 | tf_op jit(solution)/shard_map/ppermute | solution.py:460
  547.2 35.4 %collective-permute-start.96 = (bf16[128,2048]{1,0:T(8,128)(2,1)}, bf16[128,2048]{1,0:T(8,128)(2,1)}, u32[]{:S(2)}, u32[]{:S(2)}) collective-permute-start(bf16[128,2048]{1,0:T(8,128)(2,1)} %convert_add_fusion.27), channel_id=1, source_target_pairs={{0,4},{1,5},{2,6},{3,7},{4,0},{5,1},{6,2},{7,3},{8,12},{9,13},{10,... | collective-permute-start | bytes 1572872 | tf_op jit(solution)/shard_map/ppermute | solution.py:460
  662.2 45.2 %collective-permute-start.112 = (bf16[2,2,64,1056]{3,2,1,0:T(8,128)(2,1)}, bf16[2,2,64,1056]{3,2,1,0:T(8,128)(2,1)S(1)}, u32[]{:S(2)}, u32[]{:S(2)}) collective-permute-start(bf16[2,2,64,1056]{3,2,1,0:T(8,128)(2,1)} %dynamic-slice_bitcast_fusion.12), channel_id=1, source_target_pairs={{0,16},{1,17},{2,18},{3,19},{4,20},{5,21},{6,22},{7,23},{8,24},{9,... | collective-permute-start | bytes 1622024 | tf_op jit(solution)/shard_map/ppermute | solution.py:460
  668.5 39.0 %collective-permute-start.111 = (bf16[264,2048]{1,0:T(8,128)(2,1)}, bf16[264,2048]{1,0:T(8,128)(2,1)}, u32[]{:S(2)}, u32[]{:S(2)}) collective-permute-start(bf16[264,2048]{1,0:T(8,128)(2,1)} %slice.324), channel_id=1, source_target_pairs={{0,2},{1,3},{2,0},{3,1},{4,6},{5,7},{6,4},{7,5},{8,10},{9,11},{10,... | collective-permute-start | bytes 3244040 | tf_op jit(solution)/shard_map/ppermute | solution.py:460
  670.0 76.0 %collective-permute-start.119 = (bf16[64,2048]{1,0:T(8,128)(2,1)}, bf16[64,2048]{1,0:T(8,128)(2,1)}, u32[]{:S(2)}, u32[]{:S(2)}) collective-permute-start(bf16[64,2048]{1,0:T(8,128)(2,1)} %convert_add_fusion.34), channel_id=1, source_target_pairs={{0,8},{1,9},{2,10},{3,11},{4,12},{5,13},{6,14},{7,15},{8,16},{9,17... | collective-permute-start | bytes 786440 | tf_op jit(solution)/shard_map/ppermute | solution.py:460
  708.8 51.7 %collective-permute-start.116 = (bf16[2,2,64,1056]{3,2,1,0:T(8,128)(2,1)S(1)}, bf16[2,2,64,1056]{3,2,1,0:T(8,128)(2,1)S(1)}, u32[]{:S(2)}, u32[]{:S(2)}) collective-permute-start(bf16[2,2,64,1056]{3,2,1,0:T(8,128)(2,1)S(1)} %dynamic-slice_bitcast_fusion.11), channel_id=1, source_target_pairs={{0,4},{1,5},{2,6},{3,7},{4,0},{5,1},{6,2},{7,3},{8,12},{9,13},{10,... | collective-permute-start | bytes 1622024 | tf_op jit(solution)/shard_map/ppermute | solution.py:460
  710.0 35.8 %collective-permute-start.114 = (bf16[264,1536]{1,0:T(8,128)(2,1)S(1)}, bf16[264,1536]{1,0:T(8,128)(2,1)S(1)}, u32[]{:S(2)}, u32[]{:S(2)}) collective-permute-start(bf16[264,1536]{1,0:T(8,128)(2,1)S(1)} %dynamic-slice_bitcast_fusion.8), channel_id=1, source_target_pairs={{0,4},{1,5},{2,6},{3,7},{4,0},{5,1},{6,2},{7,3},{8,12},{9,13},{10,... | collective-permute-start | bytes 2433032 | tf_op jit(solution)/shard_map/ppermute | solution.py:460
  712.6 48.0 %collective-permute-start.115 = (bf16[264,2048]{1,0:T(8,128)(2,1)S(1)}, bf16[264,2048]{1,0:T(8,128)(2,1)S(1)}, u32[]{:S(2)}, u32[]{:S(2)}) collective-permute-start(bf16[264,2048]{1,0:T(8,128)(2,1)S(1)} %slice.325), channel_id=1, source_target_pairs={{0,2},{1,3},{2,0},{3,1},{4,6},{5,7},{6,4},{7,5},{8,10},{9,11},{10,... | collective-permute-start | bytes 3244040 | tf_op jit(solution)/shard_map/ppermute | solution.py:460
  716.7 43.9 %collective-permute-start.117 = (bf16[264,1536]{1,0:T(8,128)(2,1)S(1)}, bf16[264,1536]{1,0:T(8,128)(2,1)S(1)}, u32[]{:S(2)}, u32[]{:S(2)}) collective-permute-start(bf16[264,1536]{1,0:T(8,128)(2,1)S(1)} %convert_add_fusion.3), channel_id=1, source_target_pairs={{0,8},{1,9},{2,10},{3,11},{4,12},{5,13},{6,14},{7,15},{8,16},{9,17... | collective-permute-start | bytes 2433032 | tf_op jit(solution)/shard_map/ppermute | solution.py:460
  764.2 33.0 %collective-permute-start.124 = (bf16[264,1536]{1,0:T(8,128)(2,1)S(1)}, bf16[264,1536]{1,0:T(8,128)(2,1)S(1)}, u32[]{:S(2)}, u32[]{:S(2)}) collective-permute-start(bf16[264,1536]{1,0:T(8,128)(2,1)S(1)} %add_convert_fusion.1), channel_id=1, source_target_pairs={{0,8},{1,9},{2,10},{3,11},{4,12},{5,13},{6,14},{7,15},{8,16},{9,17... | collective-permute-start | bytes 2433032 | tf_op jit(solution)/shard_map/ppermute | solution.py:460
  764.3 32.8 %collective-permute-start.122 = (bf16[264,2048]{1,0:T(8,128)(2,1)S(1)}, bf16[264,2048]{1,0:T(8,128)(2,1)}, u32[]{:S(2)}, u32[]{:S(2)}) collective-permute-start(bf16[264,2048]{1,0:T(8,128)(2,1)S(1)} %slice.328), channel_id=1, source_target_pairs={{0,2},{1,3},{2,0},{3,1},{4,6},{5,7},{6,4},{7,5},{8,10},{9,11},{10,... | collective-permute-start | bytes 3244040 | tf_op jit(solution)/shard_map/ppermute | solution.py:460
  (338 other events, 4504.6 us)

commit v3 on v2

--- a/solution.py
+++ b/solution.py
@@ -104,14 +104,15 @@
         return near + self.partner(far, 2).astype(F32)
 
 
-def attend_kernel(heads, seq, scale, x_ref, w_ref, bias_ref, cos_ref, sin_ref, place_ref, seg_ref,
-                  place_row_ref, seg_row_ref, qkv_ref, out_ref):
+def attend_kernel(heads, seq, scale, split, x_ref, w_ref, bias_ref, cos_ref, sin_ref, place_ref, seg_ref,
+                  place_row_ref, seg_row_ref, core_ref, qkv_ref, *out_refs):
     lin = dot_nn(x_ref[...], w_ref[...]) + bias_ref[...]
     cosine, sine = cos_ref[...], sin_ref[...]
     span = heads * HEAD
     for micro in range(x_ref.shape[0] // seq):
         low, high = micro * seq, (micro + 1) * seq
         visible = (place_row_ref[...] <= place_ref[...]) & (seg_row_ref[micro : micro + 1, :] == seg_ref[low:high, :])
+        found = []
         for head in range(heads):
             at = head * HEAD
             query = lin[low:high, at : at + HEAD]
@@ -122,17 +123,31 @@
             scores = jnp.where(visible, dot_nt(query, key) * scale, MASKED)
             exps = jnp.exp(scores - jnp.max(scores, axis=1, keepdims=True))
             probs = exps / jnp.sum(exps, axis=1, keepdims=True)
-            out_ref[low:high, at : at + HEAD] = dot_nn(probs.astype(BF), value).astype(BF)
+            found.append(dot_nn(probs.astype(BF), value))
             qkv_ref[low:high, at : at + HEAD] = query
             qkv_ref[low:high, span + at : span + at + HEAD] = key
             qkv_ref[low:high, 2 * span + at : 2 * span + at + HEAD] = value
-
-
-def attend_back_kernel(heads, seq, scale, grad_ref, wo_ref, qkv_ref, cos_ref, sin_ref, place_ref, seg_ref,
-                       place_row_ref, seg_row_ref, w_ref, lin_ref, normed_ref):
-    grad_out = dot_nt(grad_ref[...], wo_ref[...]).astype(BF)
+        if not split:
+            out_refs[0][low:high, :] = jnp.concatenate(found, axis=1).astype(BF)
+            continue
+        first = jnp.concatenate([item[:, : HEAD // 2] for item in found], axis=1)
+        second = jnp.concatenate([item[:, HEAD // 2 :] for item in found], axis=1)
+        out_refs[0][low:high, :] = jnp.where(core_ref[0] == 0, first, second).astype(BF)
+        out_refs[1][low:high, :] = jnp.where(core_ref[0] == 0, second, first).astype(BF)
+
+
+def attend_back_kernel(heads, seq, scale, split, grad_ref, other_ref, qkv_ref, cos_ref, sin_ref, place_ref, seg_ref,
+                       place_row_ref, seg_row_ref, core_ref, w_ref, x_ref, lin_ref, normed_ref, *panel_refs):
     cosine, sine = cos_ref[...], sin_ref[...]
     span = heads * HEAD
+    if split:
+        first = jnp.where(core_ref[0] == 0, grad_ref[...], other_ref[...])
+        second = jnp.where(core_ref[0] == 0, other_ref[...], grad_ref[...])
+        half = HEAD // 2
+        grad_out = jnp.concatenate(
+            [part[:, k * half : (k + 1) * half] for k in range(heads) for part in (first, second)], axis=1)
+    else:
+        grad_out = dot_nt(grad_ref[...], other_ref[...]).astype(BF)
     for micro in range(grad_ref.shape[0] // seq):
         low, high = micro * seq, (micro + 1) * seq
         visible = (place_row_ref[...] <= place_ref[...]) & (seg_row_ref[micro : micro + 1, :] == seg_ref[low:high, :])
@@ -156,6 +171,14 @@
             lin_ref[low:high, at : at + HEAD] = grad_query.astype(BF)
             lin_ref[low:high, span + at : span + at + HEAD] = grad_key.astype(BF)
             lin_ref[low:high, 2 * span + at : 2 * span + at + HEAD] = grad_value.astype(BF)
+    if split:
+        panel_ref = panel_refs[0]
+        count, rows = panel_ref.shape[0], x_ref.shape[1] // panel_ref.shape[0]
+        grad_w = dot_tn(x_ref[...], lin_ref[...]).astype(BF)
+        for k in range(count):
+            panel_ref[k, :rows, :] = grad_w[k * rows : (k + 1) * rows, :]
+        behind = panel_ref.shape[1] - rows
+        panel_ref[:, rows:, :] = jnp.zeros((count, behind, panel_ref.shape[2]), BF)
     part = dot_nt(lin_ref[...], w_ref[...])
 
     @pl.when(pl.program_id(0) == 0)
@@ -171,7 +194,7 @@
     return pl.BlockSpec(shape, lambda *_: (0,) * len(shape))
 
 
-def attend(normed, wqkv, bias, tables, seq, back=None):
+def attend(normed, wqkv, bias, tables, seq, back=None, core=None, panel=None):
     cosine, sine, place, seg, place_row, seg_row = tables
     rows = normed.shape[0]
     pairs = 2
@@ -179,68 +202,68 @@
     heads = wide3 // 3 // HEAD // pairs
     span = heads * HEAD
     scale = HEAD ** (-0.5)
-    common = (cosine, sine, place, seg, place_row, seg_row)
-    common_specs = [whole(item.shape) for item in common]
-    params = pltpu.CompilerParams(vmem_limit_bytes=40 * 2**20)
+    split = core is not None
+    common = (cosine, sine, place, seg, place_row, seg_row, core if split else jnp.zeros((1,), jnp.int32))
+    common_specs = [whole(item.shape) for item in common[:-1]] + [pl.BlockSpec(memory_space=pltpu.SMEM)]
+    params = pltpu.CompilerParams(vmem_limit_bytes=48 * 2**20)
+    cost = pl.CostEstimate(flops=10**8, bytes_accessed=10**6, transcendentals=10**5)
+    columns, count = (span // 2, 2) if split else (span, 1)
+    kept = pl.BlockSpec((rows, columns), lambda p: (0, p))
     if back is None:
         return pl.pallas_call(
-            functools.partial(attend_kernel, heads, seq, scale),
+            functools.partial(attend_kernel, heads, seq, scale, split),
             grid=(pairs,),
             in_specs=[
                 whole(normed.shape),
                 pl.BlockSpec((wqkv.shape[0], 3 * span), lambda p: (0, p)),
                 pl.BlockSpec((1, 3 * span), lambda p: (0, p)),
             ] + common_specs,
-            out_specs=[
-                pl.BlockSpec((rows, 3 * span), lambda p: (0, p)),
-                pl.BlockSpec((rows, span), lambda p: (0, p)),
-            ],
-            out_shape=[
-                jax.ShapeDtypeStruct((rows, wide3), BF),
-                jax.ShapeDtypeStruct((rows, wide3 // 3), BF),
-            ],
+            out_specs=[pl.BlockSpec((rows, 3 * span), lambda p: (0, p))] + [kept] * count,
+            out_shape=[jax.ShapeDtypeStruct((rows, wide3), BF)]
+            + [jax.ShapeDtypeStruct((rows, pairs * columns), BF)] * count,
             compiler_params=params,
-            cost_estimate=pl.CostEstimate(flops=5 * 10**9, bytes_accessed=10**7, transcendentals=10**6),
+            cost_estimate=cost,
             name="attend",
         )(normed, wqkv, bias, *common)
-    grad, wo, qkv = back
+    grad, other, qkv = back
     return pl.pallas_call(
-        functools.partial(attend_back_kernel, heads, seq, scale),
+        functools.partial(attend_back_kernel, heads, seq, scale, split),
         grid=(pairs,),
-        in_specs=[
-            whole(grad.shape),
-            pl.BlockSpec((span, wo.shape[1]), lambda p: (p, 0)),
-            pl.BlockSpec((rows, 3 * span), lambda p: (0, p)),
-        ] + common_specs + [pl.BlockSpec((wqkv.shape[0], 3 * span), lambda p: (0, p))],
-        out_specs=[pl.BlockSpec((rows, 3 * span), lambda p: (0, p)), whole((rows, wqkv.shape[0]))],
-        out_shape=[jax.ShapeDtypeStruct((rows, wide3), BF), jax.ShapeDtypeStruct((rows, wqkv.shape[0]), F32)],
+        in_specs=([kept, kept] if split else [whole(grad.shape), pl.BlockSpec((span, other.shape[1]), lambda p: (p, 0))])
+        + [pl.BlockSpec((rows, 3 * span), lambda p: (0, p))]
+        + common_specs
+        + [pl.BlockSpec((wqkv.shape[0], 3 * span), lambda p: (0, p)), whole(normed.shape)],
+        out_specs=[pl.BlockSpec((rows, 3 * span), lambda p: (0, p)), whole((rows, wqkv.shape[0]))]
+        + ([pl.BlockSpec(panel[:2] + (3 * span,), lambda p: (0, 0, p))] if split else []),
+        out_shape=[jax.ShapeDtypeStruct((rows, wide3), BF), jax.ShapeDtypeStruct((rows, wqkv.shape[0]), F32)]
+        + ([jax.ShapeDtypeStruct(panel, BF)] if split else []),
         compiler_params=params,
-        cost_estimate=pl.CostEstimate(flops=5 * 10**9, bytes_accessed=10**7, transcendentals=10**6),
+        cost_estimate=cost,
         name="attend_back",
-    )(grad, wo, qkv, *common, wqkv)
+    )(grad, other, qkv, *common, wqkv, normed)
 
 
 def feed_kernel(experts, shared, expert_ref, *refs):
-    x_refs, g_refs = refs[:4], refs[4:8]
-    weights = (refs[8:11], refs[11:14])
-    unit_refs, gn_refs, out_refs = refs[14:20], refs[20:24], refs[24:28]
-    x_all, g_all = refs[28:30]
-    units = (refs[30:33], refs[33:36])
-    gn, out, sems = refs[36:]
+    x_refs, g_refs = refs[:3], refs[3:6]
+    weights = (refs[6:9], refs[9:12])
+    unit_refs, gn_refs, out_refs = refs[12:18], refs[18:21], refs[21:24]
+    x_all, g_all = refs[24:26]
+    units = (refs[26:29], refs[29:32])
+    gn, out, sems = refs[32:]
     own, width = x_refs[0].shape
     rows = 4 * own
     expert = expert_ref[0]
 
     def block(k):
-        return pl.ds(k * own, own)
+        return pl.ds(k * own, 2 * own if k == 2 else own)
 
     def start(number, source, target):
         copy = pltpu.make_async_copy(source, target, sems.at[number])
         copy.start()
         return copy
 
-    x_copies = [start(k, x_refs[k], x_all.at[block(k), :]) for k in range(4)]
-    g_copies = [start(4 + k, g_refs[k], g_all.at[block(k), :]) for k in range(4)]
+    x_copies = [start(k, x_refs[k], x_all.at[block(k), :]) for k in range(3)]
+    g_copies = [start(3 + k, g_refs[k], g_all.at[block(k), :]) for k in range(3)]
     for copy in x_copies:
         copy.wait()
     gates = [dot_nt(x_all[...], weights[k][0][...]) for k in range(2)]
@@ -281,10 +304,10 @@
     total = dot_nn(units[0][1][...], weights[0][0][...]) + dot_nn(units[0][2][...], weights[0][1][...])
     total += dot_nn(units[1][1][...], weights[1][0][...]) + dot_nn(units[1][2][...], weights[1][1][...])
     gn[:, :width] = total.astype(BF)
-    copies += [start(6 + k, gn.at[block(k), :], gn_refs[k]) for k in range(4)]
+    copies += [start(6 + k, gn.at[block(k), :], gn_refs[k]) for k in range(3)]
     total = dot_nn(units[0][0][...], weights[0][2][...]) + dot_nn(units[1][0][...], weights[1][2][...])
     out[...] = total.astype(BF)
-    copies += [start(10 + k, out.at[block(k), :], out_refs[k]) for k in range(4)]
+    copies += [start(9 + k, out.at[block(k), :], out_refs[k]) for k in range(3)]
     for copy in copies:
         copy.wait()
 
@@ -299,20 +322,94 @@
     found = pl.pallas_call(
         functools.partial(feed_kernel, experts, shared),
         in_specs=[pl.BlockSpec(memory_space=pltpu.SMEM)]
-        + [anywhere] * 8
+        + [anywhere] * 6
         + [pl.BlockSpec(memory_space=pltpu.VMEM)] * 6,
-        out_specs=[anywhere] * 14,
+        out_specs=[anywhere] * 12,
         scratch_shapes=[pltpu.VMEM((rows, width), BF), pltpu.VMEM((rows, wide), BF)]
         + [pltpu.VMEM((rows, count), BF) for count in counts for _ in range(3)]
-        + [pltpu.VMEM((rows, wide), BF), pltpu.VMEM((rows, width), BF), pltpu.SemaphoreType.DMA((14,))],
+        + [pltpu.VMEM((rows, wide), BF), pltpu.VMEM((rows, width), BF), pltpu.SemaphoreType.DMA((12,))],
         out_shape=[jax.ShapeDtypeStruct((rows, count), BF) for count in counts for _ in range(3)]
-        + [jax.ShapeDtypeStruct((own, wide), BF)] * 4
-        + [jax.ShapeDtypeStruct((own, width), BF)] * 4,
+        + [jax.ShapeDtypeStruct((count, columns), BF) for columns in (wide, width) for count in (own, own, 2 * own)],
         compiler_params=pltpu.CompilerParams(vmem_limit_bytes=42 * 2**20),
         cost_estimate=pl.CostEstimate(flops=16 * 10**9, bytes_accessed=3 * 10**7, transcendentals=10**6),
         name="feed",
     )(expert, *x_blocks, *g_blocks, *weights)
-    return found[:3], found[3:6], found[6:10], found[10:14]
+    return found[:3], found[3:6], found[6:9], found[9:12]
+
+
+SMALL_COST = pl.CostEstimate(flops=0, bytes_accessed=10**6, transcendentals=0)
+
+
+def pack_kernel(full, rest, gate_ref, up_ref, down_ref, out_ref):
+    count = out_ref.shape[0]
+    refs = (gate_ref, up_ref, down_ref)
+    for j in range(count):
+        for k in range(3):
+            out_ref[j, :, k * full : (k + 1) * full] = refs[k][:, j * full : (j + 1) * full]
+        low = count * full + j * rest
+        out_ref[j, :, 3 * full :] = jnp.concatenate([ref[:, low : low + rest] for ref in refs], axis=1)
+
+
+def pack_shared(gate, up, down, count, full, rest):
+    vmem = pl.BlockSpec(memory_space=pltpu.VMEM)
+    return pl.pallas_call(
+        functools.partial(pack_kernel, full, rest),
+        in_specs=[vmem] * 3,
+        out_specs=vmem,
+        out_shape=jax.ShapeDtypeStruct((count, gate.shape[0], 3 * (full + rest)), BF),
+        compiler_params=pltpu.CompilerParams(vmem_limit_bytes=16 * 2**20),
+        cost_estimate=SMALL_COST,
+        name="pack_shared",
+    )(gate, up, down)
+
+
+def unpack_kernel(full, rest, in_ref, *out_refs):
+    count = in_ref.shape[0]
+    for k in range(3):
+        for j in range(count):
+            out_refs[k][:, j * full : (j + 1) * full] = in_ref[j, :, k * full : (k + 1) * full].astype(F32)
+        low = 3 * full + k * rest
+        for j in range(0, count, 4):
+            at = count * full + j * rest
+            piece = jnp.concatenate([in_ref[j + i, :, low : low + rest] for i in range(4)], axis=1)
+            out_refs[k][:, at : at + 4 * rest] = piece.astype(F32)
+
+
+def unpack_shared(blocks, full, rest):
+    count, rows, _ = blocks.shape
+    vmem = pl.BlockSpec(memory_space=pltpu.VMEM)
+    return pl.pallas_call(
+        functools.partial(unpack_kernel, full, rest),
+        in_specs=[vmem],
+        out_specs=[vmem] * 3,
+        out_shape=[jax.ShapeDtypeStruct((rows, count * (full + rest)), F32)] * 3,
+        compiler_params=pltpu.CompilerParams(vmem_limit_bytes=16 * 2**20),
+        cost_estimate=SMALL_COST,
+        name="unpack_shared",
+    )(blocks)
+
+
+def fold_kernel(full, rest, *refs):
+    out_ref, rests = refs[6], []
+    for k in range(3):
+        total = refs[2 * k][...].astype(F32) + refs[2 * k + 1][...].astype(F32)
+        total = total.T.astype(BF)
+        out_ref[:, k * full : (k + 1) * full] = total[:, :full]
+        rests.append(total[:, full : full + rest])
+    out_ref[:, 3 * full :] = jnp.concatenate(rests, axis=1)
+
+
+def fold_shared(pairs, full, rest):
+    vmem = pl.BlockSpec(memory_space=pltpu.VMEM)
+    return pl.pallas_call(
+        functools.partial(fold_kernel, full, rest),
+        in_specs=[vmem] * 6,
+        out_specs=vmem,
+        out_shape=jax.ShapeDtypeStruct((pairs[0][0].shape[1], 3 * (full + rest)), BF),
+        compiler_params=pltpu.CompilerParams(vmem_limit_bytes=24 * 2**20),
+        cost_estimate=SMALL_COST,
+        name="fold_shared",
+    )(*[item for pair in pairs for item in pair])
 
 
 def join_kernel(cuts, y_ref, mine_ref, low_ref, high_ref, behind_ref, *out_refs):
@@ -351,18 +448,18 @@
 
 
 def weights_kernel(n_sets, split, y_ref, *refs):
-    sources, lhs_refs = refs[:16], refs[16 : 16 + 4 * n_sets]
-    out_refs, (held, sems) = refs[16 + 4 * n_sets : -2], refs[-2:]
+    sources, lhs_refs = refs[:12], refs[12 : 12 + 4 * n_sets]
+    out_refs, (held, sems) = refs[12 + 4 * n_sets : -2], refs[-2:]
     rows, width = held.shape
     own = rows // 16
 
     @pl.when(pl.program_id(0) == 0)
     def _():
-        copies = [
-            pltpu.make_async_copy(
-                sources[k].at[:, pl.ds(0, width)], held.at[pl.ds(k * own, own), :], sems.at[k])
-            for k in range(16)
-        ]
+        copies = []
+        for k in range(12):
+            at, count = (k // 3 * 4 + k % 3) * own, 2 * own if k % 3 == 2 else own
+            copies.append(
+                pltpu.make_async_copy(sources[k].at[:, pl.ds(0, width)], held.at[pl.ds(at, count), :], sems.at[k]))
         for copy in copies:
             copy.start()
         for copy in copies:
@@ -372,7 +469,18 @@
         lhs = jnp.concatenate([ref[...] for ref in lhs_refs[4 * k : 4 * k + 4]], axis=0)
         total = dot_tn(lhs, held[...])
         if not split:
-            out_refs[k][...] = total.astype(BF)
+            for tile in range(2):
+                at = 0
+                for out_ref in out_refs:
+                    low, high = max(at, tile * GRAD_TILE), min(at + out_ref.shape[0], (tile + 1) * GRAD_TILE)
+                    if low < high:
+
+                        @pl.when(pl.program_id(0) == tile)
+                        def _(out_ref=out_ref, low=low, high=high, at=at, tile=tile):
+                            out_ref[low - at : high - at, :] = total[
+                                low - tile * GRAD_TILE : high - tile * GRAD_TILE, :].astype(BF)
+
+                    at += out_ref.shape[0]
             continue
         for block in range(width // LANES // 2):
             even = total[:, 2 * block * LANES : (2 * block + 1) * LANES]
@@ -382,21 +490,24 @@
             out_refs[2 * k + 1][:, columns] = jnp.where(y_ref[0] == 0, odd, even).astype(BF)
 
 
-def weight_grads(y, sources, lhs_sets, width, split=False):
+def weight_grads(y, sources, lhs_sets, width, parts=None):
     rows, units = lhs_sets[0][0].shape
     n_sets = len(lhs_sets)
     n_tiles = units // GRAD_TILE
-    columns = width // 2 if split else width
-    n_outs = 2 * n_sets if split else n_sets
+    split = parts is None
+    if split:
+        shapes = [(GRAD_TILE, width // 2)] * (2 * n_sets)
+    else:
+        shapes = [(count, width) for count in parts]
     return pl.pallas_call(
         functools.partial(weights_kernel, n_sets, split),
         grid=(n_tiles,),
         in_specs=[pl.BlockSpec(memory_space=pltpu.SMEM)]
-        + [pl.BlockSpec(memory_space=pl.ANY)] * 16
+        + [pl.BlockSpec(memory_space=pl.ANY)] * 12
         + [pl.BlockSpec((rows, GRAD_TILE), lambda i: (0, i))] * (4 * n_sets),
-        out_specs=[pl.BlockSpec((GRAD_TILE, columns), lambda i: (i, 0))] * n_outs,
-        scratch_shapes=[pltpu.VMEM((4 * rows, width), BF), pltpu.SemaphoreType.DMA((16,))],
-        out_shape=[jax.ShapeDtypeStruct((units, columns), BF)] * n_outs,
+        out_specs=[whole(shape) for shape in shapes],
+        scratch_shapes=[pltpu.VMEM((4 * rows, width), BF), pltpu.SemaphoreType.DMA((12,))],
+        out_shape=[jax.ShapeDtypeStruct(shape, BF) for shape in shapes],
         compiler_params=pltpu.CompilerParams(vmem_limit_bytes=36 * 2**20),
         cost_estimate=pl.CostEstimate(
             flops=4 * 10**9 * n_sets * n_tiles, bytes_accessed=2 * 10**7, transcendentals=0),
@@ -509,142 +620,150 @@
         split = blocks.reshape(2, 2, rows, 2, 3, heads_dev // 2, HEAD)
         return split.transpose(4, 2, 1, 3, 5, 0, 6).reshape(3, rows, width)
 
-    small = jnp.concatenate([w_router.T, shared_gate[None], norm_gain1[None], norm_gain2[None], b_qkv], axis=0)
-    n_small = small.shape[0]
-    small = [small.reshape(1, n_small * rows_w)]
+    def swap_core(blocks):
+        mine, give = pick(blocks, c, 2), pick(blocks, 1 - c, 2)
+        return in_order(mine, send(give, "core"), c, 2)
+
+    def swap_z(blocks, k):
+        return send(pick(blocks, lax.rem(z + k, 4)), f"z{k}")
+
+    def swap_x(blocks):
+        mine, give = pick(blocks, x, 1), pick(blocks, 1 - x, 1)
+        return in_order(mine, send(give, "x"), x, 1)
+
+    small = jnp.concatenate(
+        [w_router.T, shared_gate[None], norm_gain1[None], norm_gain2[None], b_qkv, seg_ids.astype(BF)], axis=0)
+    n_small = experts + 6
+    small = [small.reshape(1, (n_small + micro) * rows_w)]
     for _ in range(3):
         small.append(send(small[-1], "z1"))
     small = jnp.concatenate(small)
     qkv = by_fsdp(jnp.stack([w_query, w_key, w_value], axis=1))
     arrived = [send(pick(qkv, lax.bitwise_xor(my_fsdp, k)), link) for k, link in ((1, "core"), (2, "y"), (3, "yc"))]
-    seg_near, seg_far = send(seg_ids, "core"), send(seg_ids, "y")
     grad_own = out_grad.reshape(own, width)
     names = jnp.pad(routes.reshape(own, top_count).astype(BF), ((0, 0), (0, LANES - top_count)))
     g_own = [jnp.concatenate([grad_own, names], axis=1)]
     g_pair = []
     routed_mine = jnp.concatenate([ex_gate[0].T, ex_up[0].T, ex_down[0]], axis=0)
-    small, arrived, g_own[0], seg_near, seg_far, routed_mine = sync(
-        small, arrived, g_own[0], seg_near, seg_far, routed_mine)
+    small, arrived, g_own[0], routed_mine = sync(small, arrived, g_own[0], routed_mine)
     for k in range(3):
         qkv = put(qkv, arrived[k], lax.bitwise_xor(my_fsdp, k + 1))
-    block = jnp.concatenate(
-        [qkv.reshape(n_fsdp * rows_w, 3 * wide), w_out.reshape(rows_w, n_fsdp, wide).reshape(-1, wide)], axis=1)
-
+    block = jnp.concatenate([w_out[:, k * wide : (k + 1) * wide] for k in range(n_fsdp)], axis=0)
+    block = jnp.concatenate([qkv.reshape(n_fsdp * rows_w, 3 * wide), block], axis=1)
     following = send(block, "z1")
     small = jnp.concatenate([small, send(small, "x")])
     at_pair = send(sync(block, small)[0], "x")
     small = jnp.concatenate([small, send(small, "y")])
+    got = send(sync(routed_mine[:264], small)[0], "y")
     small = jnp.concatenate([small, send(small, "core")])
+    block, following, at_pair, small, got, routed_mine, sh_gate, sh_up, sh_down, hidden_in = sync(
+        block, following, at_pair, small, got, routed_mine, sh_gate, sh_up, sh_down, hidden_in)
+    a_blocks = [routed_mine[k * 264 : (k + 1) * 264] for k in range(4)]
+    got_blocks = [got]
+    weights = jnp.zeros((n_exp,) + block.shape, BF)
+
+    def ring_put(weights, step, mine, other):
+        return put(put(weights, mine, slot(step, 0)), other, slot(step, 1))
+
+    first_pair, mine = at_pair, following
+    at_pair, following = send(mine, "x"), send(mine, "z1")
     places = jnp.stack(
         [slot(step, other) * 4 + lax.bitwise_xor(my_fsdp, k) for k in (0, 2, 1, 3) for other in range(2) for step in range(4)])
     choice = (jnp.arange(n_all)[:, None] == places[None]).astype(BF)
-    small = dot_nn(choice, small).astype(BF).reshape(n_all, n_small, rows_w).transpose(1, 0, 2).reshape(n_small, width)
+    small = dot_nn(choice, small).astype(BF).reshape(n_all, n_small + micro, rows_w)
+    small = small.transpose(1, 0, 2).reshape(n_small + micro, width)
     router_rows = small[: experts + 1]
     gain_one = small[experts + 1].astype(F32)
     gain_two = small[experts + 2].astype(F32)
-    bias = pick(by_fsdp(small[experts + 3 :].astype(F32)[None]), my_fsdp)
+    bias = pick(by_fsdp(small[experts + 3 : n_small].astype(F32)[None]), my_fsdp)
+    seg_seq = lax.dynamic_slice_in_dim(small[n_small:], my_exp * seq, seq, 1).reshape(micro, n_fsdp, tok)
     hidden = hidden_in.reshape(own, width).astype(F32)
     scaled_one, inverse_one = normalize(hidden)
     normed_one = (scaled_one * gain_one).astype(BF).reshape(micro, tok, width)
     seq_far, seq_near = send(normed_one, "y"), send(normed_one, "core")
-    seg_last = send(seg_far, "core")
-    weights = jnp.zeros((n_exp,) + block.shape, BF)
-    weights = put(weights, block, slot(0, 0))
-
-    def ring_put(weights, step, mine, other):
-        return put(put(weights, mine, slot(step, 0)), other, slot(step, 1))
-
-    a_blocks = [routed_mine[k * 264 : (k + 1) * 264] for k in range(4)]
-    got_blocks = []
-    current = following
-    (current, at_pair, seq_far, seq_near, seg_last, normed_one, a_blocks, bias, router_rows) = sync(
-        current, at_pair, seq_far, seq_near, seg_last, normed_one, a_blocks, bias, router_rows)
-    weights = put(weights, at_pair, slot(0, 1))
+
+    (block, mine, following, at_pair, seq_far, seq_near, normed_one, a_blocks, bias, router_rows, seg_seq,
+     sh_gate, sh_up, sh_down) = sync(
+        block, mine, following, at_pair, seq_far, seq_near, normed_one, a_blocks, bias, router_rows, seg_seq,
+        sh_gate, sh_up, sh_down)
+
+    previous, previous_pair, mine = mine, at_pair, following
+    at_pair, following = send(mine, "x"), send(mine, "z1")
+    shared_w = pack_shared(sh_gate, sh_up, sh_down, 16, full_cols, rest_cols)
+    shared_w = swap_core(shared_w.reshape(4, 2, 2, rows_w, unit_cols))
+    weights = ring_put(ring_put(weights, 0, block, first_pair), 1, previous, previous_pair)
     seq_last = send(seq_far, "core")
-
-    def by_owner(weight):
-        full = weight[:, : 16 * full_cols].reshape(rows_w, 16, full_cols).transpose(1, 0, 2)
-        rest = weight[:, 16 * full_cols :].reshape(rows_w, 16, rest_cols).transpose(1, 0, 2)
-        return full, rest
-
-    pieces = [by_owner(weight) for weight in (sh_gate, sh_up, sh_down)]
-    shared_w = jnp.concatenate([piece[0] for piece in pieces] + [piece[1] for piece in pieces], axis=2)
-    shared_w = shared_w.reshape(4, 2, 2, rows_w, unit_cols)
-
-    def swap_core(blocks):
-        mine, give = pick(blocks, c, 2), pick(blocks, 1 - c, 2)
-        return in_order(mine, send(give, "core"), c, 2)
-
-    def swap_z(blocks, k):
-        return send(pick(blocks, lax.rem(z + k, 4)), f"z{k}")
-
-    def swap_x(blocks):
-        mine, give = pick(blocks, x, 1), pick(blocks, 1 - x, 1)
-        return in_order(mine, send(give, "x"), x, 1)
-
-    for step in (1, 2):
-        at_pair = send(current, "x")
-        following = send(current, "z1")
-        got = send(a_blocks[step - 1], "y")
-        if step == 2:
-            shared_w = swap_core(shared_w)
-        mine = current
-        current, at_pair, got, mine, a_blocks, shared_w, seq_last = sync(
-            following, at_pair, got, mine, a_blocks, shared_w, seq_last)
-        got_blocks.append(got)
-        weights = ring_put(weights, step, mine, at_pair)
-
-    at_pair = send(current, "x")
+    got = send(a_blocks[1], "y")
+    mine, following, at_pair, got, a_blocks, shared_w, seq_last, weights = sync(
+        mine, following, at_pair, got, a_blocks, shared_w, seq_last, weights)
+    got_blocks.append(got)
+
+    weights = ring_put(weights, 2, mine, at_pair)
+    at_pair = send(following, "x")
     got = send(a_blocks[2], "y")
     shared_z = {1: swap_z(shared_w, 1), 3: swap_z(shared_w, 3)}
-    current, at_pair, got, shared_z, shared_w, a_blocks, weights = sync(
-        current, at_pair, got, shared_z, shared_w, a_blocks, weights)
-    got_blocks.append(got)
-    weights = ring_put(weights, 3, current, at_pair)
-
-    got = send(a_blocks[3], "y")
-    shared_z[2] = swap_z(shared_w, 2)
-    wo_rows = weights[:, :, 3 * wide :].reshape(n_exp, rows_w, width)
-    keep = lax.dynamic_slice_in_dim(wo_rows, 4 * c, 4, 0)
-    arrived = send(lax.dynamic_slice_in_dim(wo_rows, 4 * (1 - c), 4, 0), "core")
-    wo = in_order(keep, arrived, c, 1).reshape(wide, width)
-    weights = weights.reshape(width, 4 * wide)
     order = lax.bitwise_xor(my_fsdp, jnp.arange(n_fsdp))
     places = (order[:, None] * tok + jnp.arange(tok)[None]).reshape(seq)
-    seg_seq = jnp.concatenate([seg_ids, seg_near, seg_far, seg_last], axis=1)
+    seg_seq = jnp.take(seg_seq, order, axis=1).reshape(micro, seq).astype(jnp.int32)
     normed_seq = jnp.concatenate([normed_one, seq_near, seq_far, seq_last], axis=1).reshape(micro * seq, width)
     cosine, sine = angle_tables(places)
     tables = (cosine, sine, places[:, None], seg_seq.reshape(micro * seq, 1), places[None], seg_seq)
-    weights, wo, tables, normed_seq, got, shared_z, shared_w, g_own[0] = sync(
-        weights, wo, tables, normed_seq, got, shared_z, shared_w, g_own[0])
+    following, at_pair, got, shared_z, shared_w, a_blocks, weights, tables, normed_seq, g_own[0] = sync(
+        following, at_pair, got, shared_z, shared_w, a_blocks, weights, tables, normed_seq, g_own[0])
     got_blocks.append(got)
+    weights = ring_put(weights, 3, following, at_pair)
+    wqkv = weights.reshape(width, 4 * wide)
+
+    def turned(value):
+        value = value.reshape(micro, 2, 2, tok, -1)
+        return jnp.concatenate([value[:, :, 1:], value[:, :, :1]], axis=2).reshape(micro * seq, -1)
+
+    core_place = c.reshape(1)
+    got = [send(a_blocks[3][:132], "y")]
+    far_w = pick(shared_w, lax.rem(z + 2, 4))
+    shared_z[2] = [send(far_w[0], "z2")]
+    g_pair.append(send(g_own[0], "x"))
+    qkv_seq, keep, give = attend(normed_seq, wqkv, bias, tables, seq, core=core_place)
+    wo = sync(weights, give)[0]
+    wo = [wo[:, k * rows_w : (k + 1) * rows_w, 3 * wide :].reshape(n_exp * rows_w, wide) for k in range(n_fsdp)]
+    wo = jnp.concatenate(wo, axis=1)
+    got, shared_z, qkv_seq, keep, give, wqkv, wo, far_w, g_pair, a_blocks = sync(
+        got, shared_z, qkv_seq, keep, give, wqkv, wo, far_w, g_pair, a_blocks)
+    got.append(send(a_blocks[3][132:], "y"))
+    shared_z[2].append(send(far_w[1], "z2"))
+    arrived = turned(send(give, "core"))
+    attended = jnp.where(c == 0, jnp.concatenate([keep, arrived], axis=1), jnp.concatenate([arrived, keep], axis=1))
+    attn_part = contract("tc,cd->td", attended, wo).reshape(micro, 2, 2, tok, width)
+    attn_part = attn_part[:, :, 0] + send(attn_part[:, :, 1].astype(BF), "core").astype(F32)
+    near, last = attn_part[:, 0], attn_part[:, 1].astype(BF)
+    last, near, got, shared_z, shared_w, g_own, g_pair = sync(last, near, got, shared_z, shared_w, g_own, g_pair)
+    got_blocks += got
     for k in (1, 2, 3):
-        shared_w = put(shared_w, shared_z[k], lax.rem(z + 4 - k, 4))
+        arrived = jnp.stack(shared_z[2]) if k == 2 else shared_z[k]
+        shared_w = put(shared_w, arrived, lax.rem(z + 4 - k, 4))
+
+    last = send(last, "y")
     shared_w = swap_x(shared_w)
     g_own.append(send(g_own[0], "z1"))
-    qkv_seq, attended = attend(normed_seq, weights, bias, tables, seq)
-    attn_part = contract("tc,cd->td", attended, wo).reshape(micro, n_fsdp, tok, width)
-    last = (attn_part[:, 2] + send(attn_part[:, 3].astype(BF), "core").astype(F32)).astype(BF)
-    near = attn_part[:, 0] + send(attn_part[:, 1].astype(BF), "core").astype(F32)
-    last, near, shared_w, g_own, got_blocks = sync(last, near, shared_w, g_own, got_blocks)
-
-    last = send(last, "y")
-    g_pair.append(send(g_own[0], "x"))
-    g_own.append(send(g_own[1], "z1"))
-    shared_w = shared_w.reshape(16 * rows_w, unit_cols).T
+
+    def blocks_of(mine, other):
+        return [mine, other, send(jnp.concatenate([mine, other]), "core")]
+
+    g_four = [blocks_of(g_own[0], g_pair[0])]
     after_attn = hidden + near.reshape(own, width) + last.astype(F32).reshape(own, width)
     scaled_two, inverse_two = normalize(after_attn)
     normed_two = (scaled_two * gain_two).astype(BF)
     x_own, x_pair = [normed_two], []
-    shared_w, x_own, after_attn, scaled_two, g_own, g_pair, got_blocks = sync(
-        shared_w, x_own, after_attn, scaled_two, g_own, g_pair, got_blocks)
+    shared_w, x_own, after_attn, scaled_two, g_own, g_pair, got_blocks, g_four = sync(
+        shared_w, x_own, after_attn, scaled_two, g_own, g_pair, got_blocks, g_four)
 
     half = unit_cols // 2
+    shared_w = shared_w.reshape(16 * rows_w, unit_cols).T
     arrived = [send(shared_w[:half], "y")]
     x_pair.append(send(x_own[0], "x"))
     g_pair.append(send(g_own[1], "x"))
     x_own.append(send(x_own[0], "z1"))
-    g_own.append(send(g_own[2], "z1"))
+    g_own.append(send(g_own[1], "z1"))
     routed_other = jnp.concatenate(got_blocks, axis=0)
     pad = jnp.zeros((2 * GRAD_TILE - 2 * ex_cols, width), BF)
     routed_w = [
@@ -653,16 +772,13 @@
         for k in range(3)
     ]
 
-    def four(mine, other):
-        return [mine, other, send(mine, "core"), send(other, "core")]
-
     arrived, shared_w, x_own, g_own, x_pair, g_pair, routed_w = sync(
         arrived, shared_w, x_own, g_own, x_pair, g_pair, routed_w)
     arrived.append(send(shared_w[half:], "y"))
     x_pair.append(send(x_own[1], "x"))
     g_pair.append(send(g_own[2], "x"))
     x_own.append(send(x_own[1], "z1"))
-    x_four, g_four = [four(x_own[0], x_pair[0])], [four(g_own[k], g_pair[k]) for k in range(2)]
+    x_four = [blocks_of(x_own[0], x_pair[0])]
     behind = jnp.pad(router_rows, ((0, GRAD_TILE - sh_cols - experts - 1), (0, 0)))
     arrived, shared_w, x_four, g_four, x_own, g_own, x_pair, g_pair, routed_w, behind = sync(
         arrived, shared_w, x_four, g_four, x_own, g_own, x_pair, g_pair, routed_w, behind)
@@ -672,37 +788,44 @@
     ]
     y_place = y.reshape(1)
     shared_w = join_shared(y_place, shared_w, arrived[0], arrived[1], behind, cuts)
-    g_pair.append(send(g_own[3], "x"))
-    x_four.append(four(x_own[1], x_pair[1]))
-    g_four.append(four(g_own[2], g_pair[2]))
 
     expert = my_exp.reshape(1)
-    fed, near_sums, sums = [], [], []
+    fed, near_sums, sums, out_near, out_sums = [], [], [], [], []
 
     def core_sums(found):
-        return [found[k].astype(F32) + send(found[2 + k], "core").astype(F32) for k in range(2)]
+        arrived = send(found[2], "core").astype(F32)
+        return [found[0].astype(F32) + arrived[:own], found[1].astype(F32) + arrived[own:]]
 
     def pair_sums(parts):
         return parts[0] + send(parts[1].astype(BF), "x").astype(F32)
 
     for step in range(4):
-        shared_w, routed_w, x_four, g_four, x_own, x_pair, g_pair, near_sums, sums, fed = sync(
-            shared_w, routed_w, x_four, g_four, x_own, x_pair, g_pair, near_sums, sums, fed)
+        shared_w, routed_w, x_four, g_four, x_own, g_own, x_pair, g_pair, near_sums, sums, fed, out_near, out_sums = sync(
+            shared_w, routed_w, x_four, g_four, x_own, g_own, x_pair, g_pair, near_sums, sums, fed, out_near, out_sums)
         if step == 0:
             x_pair.append(send(x_own[2], "x"))
             x_own.append(send(x_own[2], "z1"))
-            g_four.append(four(g_own[3], g_pair[3]))
+            g_own.append(send(g_own[2], "z1"))
+            x_four.append(blocks_of(x_own[1], x_pair[1]))
+            g_four.append(blocks_of(g_own[1], g_pair[1]))
         if step == 1:
             x_pair.append(send(x_own[3], "x"))
-            x_four.append(four(x_own[2], x_pair[2]))
+            g_pair.append(send(g_own[3], "x"))
+            x_four.append(blocks_of(x_own[2], x_pair[2]))
+            g_four.append(blocks_of(g_own[2], g_pair[2]))
         if step == 2:
-            x_four.append(four(x_own[3], x_pair[3]))
+            x_four.append(blocks_of(x_own[3], x_pair[3]))
+            g_four.append(blocks_of(g_own[3], g_pair[3]))
         if step >= 1:
             near_sums.append(core_sums(fed[step - 1][2]))
         if step >= 2:
             sums.append(pair_sums(near_sums[step - 2]))
+            out_near.append(core_sums(fed[step - 2][3]))
+        if step == 3:
+            out_sums.append(pair_sums(out_near[0]))
         fed.append(feed(expert, x_four[step], g_four[step], shared_w, routed_w, experts, sh_cols))
-    near_sums, sums, fed, x_four, g_four = sync(near_sums, sums, fed, x_four, g_four)
+    near_sums, sums, fed, x_four, g_four, out_near, out_sums, normed_two = sync(
+        near_sums, sums, fed, x_four, g_four, out_near, out_sums, normed_two)
 
     x_blocks = [item for four_of in x_four for item in four_of]
     g_blocks = [item for four_of in g_four for item in four_of]
@@ -711,21 +834,25 @@
     flying = send(sums[1].astype(BF), "z1")
     sums.append(pair_sums(near_sums[2]))
     near_sums.append(core_sums(fed[3][2]))
-    sg_mine, sg_give, su_mine, su_give = weight_grads(y_place, x_blocks, [shared_sets[1], shared_sets[2]], width, True)
-    sums, near_sums, flying, sg_mine, sg_give, su_mine, su_give, x_blocks, g_blocks, shared_sets, routed_sets = sync(
-        sums, near_sums, flying, sg_mine, sg_give, su_mine, su_give, x_blocks, g_blocks, shared_sets, routed_sets)
+    out_near.append(core_sums(fed[2][3]))
+    sg_mine, sg_give, su_mine, su_give = weight_grads(y_place, x_blocks, [shared_sets[1], shared_sets[2]], width)
+    (sums, near_sums, flying, sg_mine, sg_give, su_mine, su_give, x_blocks, g_blocks, shared_sets, routed_sets,
+     out_near, fed) = sync(sums, near_sums, flying, sg_mine, sg_give, su_mine, su_give, x_blocks, g_blocks,
+                           shared_sets, routed_sets, out_near, fed)
     sums.append(pair_sums(near_sums[3]))
     flying = send((sums[2] + flying.astype(F32)).astype(BF), "z1")
     sg_got = send(sg_give, "y")
-    sd_mine, sd_give = weight_grads(y_place, g_blocks, [shared_sets[0]], width, True)
-    (ed_grad,) = weight_grads(y_place, g_blocks, [routed_sets[0]], width)
-    sums, flying, sg_got, su_give, sd_mine, sd_give, ed_grad, x_blocks, routed_sets, fed = sync(
-        sums, flying, sg_got, su_give, sd_mine, sd_give, ed_grad, x_blocks, routed_sets, fed)
+    out_near.append(core_sums(fed[3][3]))
+    sd_mine, sd_give = weight_grads(y_place, g_blocks, [shared_sets[0]], width)
+    sums, flying, sg_got, su_give, sd_mine, sd_give, x_blocks, g_blocks, routed_sets, out_near, out_sums = sync(
+        sums, flying, sg_got, su_give, sd_mine, sd_give, x_blocks, g_blocks, routed_sets, out_near, out_sums)
     flying = send((sums[3] + flying.astype(F32)).astype(BF), "z1")
     su_got = send(su_give, "y")
-    out_near = [core_sums(fed[step][3]) for step in range(4)]
-    grad_sum, out_near, su_got, sd_give, x_blocks, routed_sets, ed_grad = sync(
-        sums[0] + flying.astype(F32), out_near, su_got, sd_give, x_blocks, routed_sets, ed_grad)
+    out_sums.append(pair_sums(out_near[1]))
+    e_parts = (ex_cols, ex_cols // 2, ex_cols // 2)
+    ed_grad = weight_grads(y_place, g_blocks, [routed_sets[0]], width, e_parts)
+    grad_sum, out_near, out_sums, su_got, sd_give, ed_grad, x_blocks, routed_sets = sync(
+        sums[0] + flying.astype(F32), out_near, out_sums, su_got, sd_give, ed_grad, x_blocks, routed_sets)
 
     own_logits = contract("td,cd->tc", normed_two, router_rows)
     own_probs = jax.nn.softmax(own_logits[:, :experts], axis=-1)
@@ -740,99 +867,108 @@
     gain_two_part = jnp.sum(grad_normed_two * scaled_two, axis=0)
     low = grad_after.astype(BF).reshape(micro, tok, width)
     sd_got = send(sd_give, "y")
-    out_sums = [pair_sums(out_near[0])]
-    low, grad_after, out_sums, out_near, sd_got, x_blocks, routed_sets, ed_grad = sync(
-        low, grad_after, out_sums, out_near, sd_got, x_blocks, routed_sets, ed_grad)
+    out_sums.append(pair_sums(out_near[2]))
+    flying_out = send(out_sums[1].astype(BF), "z1")
+    low, grad_after, out_sums, out_near, sd_got, flying_out, gain_two_part, router_part, x_blocks, routed_sets = sync(
+        low, grad_after, out_sums, out_near, sd_got, flying_out, gain_two_part, router_part, x_blocks, routed_sets)
     far, near = send(low, "y"), send(low, "core")
-    out_sums.append(pair_sums(out_near[1]))
-    eg_grad, eu_grad = weight_grads(y_place, x_blocks, [routed_sets[1], routed_sets[2]], width)
-    shared_grads = [
-        (mine.astype(F32) + got.astype(F32)).astype(BF)
-        for mine, got in ((sg_mine, sg_got), (su_mine, su_got), (sd_mine, sd_got))
-    ]
-    shared_grads = jnp.concatenate(
-        [grad[:full_cols] for grad in shared_grads] + [grad[full_cols:sh_cols] for grad in shared_grads], axis=0)
-    shared_grads = shared_grads.T.reshape(4, 2, 2, rows_w, unit_cols)
-    far, near, low, grad_after, out_sums, out_near, eg_grad, eu_grad, ed_grad, shared_grads = sync(
-        far, near, low, grad_after, out_sums, out_near, eg_grad, eu_grad, ed_grad, shared_grads)
-
-    e_grads = (eg_grad, eu_grad, ed_grad)
-    e_give = jnp.concatenate([grad[ex_cols : 2 * ex_cols] for grad in e_grads], axis=0)
-    e_got = []
+    out_sums.append(pair_sums(out_near[3]))
+    flying_out = send((out_sums[2] + flying_out.astype(F32)).astype(BF), "z1")
+    shared_grads = fold_shared([(sg_mine, sg_got), (su_mine, su_got), (sd_mine, sd_got)], full_cols, rest_cols)
+    shared_grads = shared_grads.reshape(4, 2, 2, rows_w, unit_cols)
+    far, near, low, out_sums, flying_out, shared_grads, ed_grad, x_blocks, routed_sets = sync(
+        far, near, low, out_sums, flying_out, shared_grads, ed_grad, x_blocks, routed_sets)
+
+    def panel_sum(panel, gives, step):
+        return pick(panel, slot(step, 0)).astype(F32) + send(gives[step], "x").astype(F32)
+
     shared_grads = swap_core(shared_grads)
+    flying_out = send((out_sums[3] + flying_out.astype(F32)).astype(BF), "z1")
     grad_attn = jnp.concatenate([low, near, far, send(far, "core")], axis=1).reshape(micro * seq, width)
-    grad_lin, grad_normed_one = attend(normed_seq, weights, bias, tables, seq, (grad_attn, wo, qkv_seq))
+    grad_attended = contract("td,cd->tc", grad_attn, wo).astype(BF)
+    half = wide // 2
+    keep = lax.dynamic_slice_in_dim(grad_attended, c * half, half, 1)
+    give = lax.dynamic_slice_in_dim(grad_attended, (1 - c) * half, half, 1)
+    arrived = turned(send(give, "core"))
+    wo_part = contract("tc,td->cd", attended, grad_attn).astype(BF).reshape(n_exp, rows_w, width)
+    wo_gives = [pick(wo_part, slot(step, 1)) for step in range(4)]
+    shared_far = pick(shared_grads, lax.rem(z + 2, 4))
+    shared_grads, shared_far, keep, arrived, flying_out, wo_part, wo_gives, ed_grad, x_blocks, routed_sets = sync(
+        shared_grads, shared_far, keep, arrived, flying_out, wo_part, wo_gives, ed_grad, x_blocks, routed_sets)
+    hidden_out = (after_attn + out_sums[0] + flying_out.astype(F32)).astype(BF)
+    e_got = [send(ed_grad[1], "y")]
+    shared_z = {2: send(shared_far, "z2")}
+    wo_sums = {step: panel_sum(wo_part, wo_gives, step) for step in (1, 2)}
+    behind_rows = 8
+    panel_shape = (n_exp, n_fsdp * rows_w + behind_rows, 3 * wide)
+    grad_lin, grad_normed_one, panel = attend(
+        normed_seq, wqkv, bias, tables, seq, (keep, arrived, qkv_seq), core_place, panel_shape)
+    shared_far = {k: pick(shared_grads, lax.rem(z + k, 4)) for k in (1, 3)}
+    (grad_lin, grad_normed_one, panel, hidden_out, e_got, shared_z, shared_far, shared_grads, wo_part, wo_gives,
+     wo_sums, ed_grad, x_blocks, routed_sets) = sync(
+        grad_lin, grad_normed_one, panel, hidden_out, e_got, shared_z, shared_far, shared_grads, wo_part, wo_gives,
+        wo_sums, ed_grad, x_blocks, routed_sets)
+    parts = grad_normed_one.reshape(micro, 2, 2, tok, width)
+    parts = parts[:, :, 0] + send(parts[:, :, 1].astype(BF), "core").astype(F32)
+    near, last = parts[:, 0], parts[:, 1].astype(BF)
+    e_got.append(send(ed_grad[2], "y"))
+    eg_grad = weight_grads(y_place, x_blocks, [routed_sets[1]], width, e_parts)
+    for k in (1, 3):
+        shared_z[k] = send(shared_far[k], f"z{k}")
+    for step in (3, 0):
+        wo_sums[step] = panel_sum(wo_part, wo_gives, step)
     gain_one_part = jnp.sum(grad_normed_one * normed_seq.astype(F32), axis=0) / gain_one
-    parts = grad_normed_one.reshape(micro, n_fsdp, tok, width)
-    last = (parts[:, 2] + send(parts[:, 3].astype(BF), "core").astype(F32)).astype(BF)
-    near = parts[:, 0] + send(parts[:, 1].astype(BF), "core").astype(F32)
-    out_sums.append(pair_sums(out_near[2]))
-    flying = send(out_sums[1].astype(BF), "z1")
-    out_grad_part = contract("tc,td->cd", attended, grad_attn).astype(BF)
-    split = out_grad_part.reshape(heads_dev, 2, HEAD // 2, width)
-    keep = pick(split, c, 1)
-    arrived = send(pick(split, 1 - c, 1), "core")
-    wo_part = jnp.where(c == 0, jnp.concatenate([keep, arrived]), jnp.concatenate([arrived, keep]))
-    grad_lin, gain_one_part, last, near, out_sums, out_near, flying, shared_grads, e_give, wo_part = sync(
-        grad_lin, gain_one_part, last, near, out_sums, out_near, flying, shared_grads, e_give, wo_part)
-
-    def panel_sum(panel, step):
-        return pick(panel, slot(step, 0)).astype(F32) + send(pick(panel, slot(step, 1)), "x").astype(F32)
-
-    far = send(last, "y")
-    shared_z = {1: swap_z(shared_grads, 1), 3: swap_z(shared_grads, 3)}
-    out_sums.append(pair_sums(out_near[3]))
-    wo_sums = {step: panel_sum(wo_part, step) for step in (1, 2)}
-    qkv_part = contract("td,tc->dc", normed_seq, grad_lin).astype(BF)
     bias_place = put(jnp.zeros((n_fsdp, 1, 3 * wide), F32), jnp.sum(grad_lin.astype(F32), axis=0)[None], my_fsdp)
     bias_place = from_fsdp(bias_place)[:, 0]
     small_part = jnp.concatenate([router_part, gain_one_part[None], gain_two_part[None], bias_place], axis=0)
     small_part = small_part.astype(BF).reshape(n_small, n_exp, n_fsdp, rows_w).transpose(1, 2, 0, 3)
     small_part = small_part.reshape(n_exp, n_fsdp * n_small * rows_w)
-    behind_rows = 8
     small_part = jnp.pad(small_part, ((0, 0), (0, behind_rows * 3 * wide - small_part.shape[1])))
-    panel = qkv_part.reshape(n_exp, n_fsdp * rows_w, 3 * wide)
-    panel = jnp.concatenate([panel, small_part.reshape(n_exp, behind_rows, 3 * wide)], axis=1)
-    far, out_sums, flying, panel, near, shared_z, shared_grads, wo_sums, wo_part, e_give = sync(
-        far, out_sums, flying, panel, near, shared_z, shared_grads, wo_sums, wo_part, e_give)
-    grad_normed_one = (near + far.astype(F32)).reshape(own, width)
-    in_grad = grad_after + norm_back(grad_normed_one, scaled_one, inverse_one, gain_one)
-
-    sums = {}
+    panel = lax.dynamic_update_slice_in_dim(
+        panel, small_part.reshape(n_exp, behind_rows, 3 * wide), n_fsdp * rows_w, 1)
+    gives = [pick(panel, slot(step, 1)) for step in range(4)]
+    gives, panel, last, near, e_got, shared_z, shared_grads, wo_sums, eg_grad, x_blocks, routed_sets = sync(
+        gives, panel, last, near, e_got, shared_z, shared_grads, wo_sums, eg_grad, x_blocks, routed_sets)
+
+    far = send(last, "y")
+    eu_grad = weight_grads(y_place, x_blocks, [routed_sets[2]], width, e_parts)
+    e_grads = (eg_grad, eu_grad, ed_grad)
+    for k in (1, 2, 3):
+        shared_grads = put(shared_grads, shared_z[k], lax.rem(z + 4 - k, 4))
+    shared_mine, shared_give = pick(shared_grads, x, 1), pick(shared_grads, 1 - x, 1)
+    shared_x, sums = [], {}
+
     for turn, step in enumerate((1, 2, 3, 0)):
-        sums[step] = panel_sum(panel, step)
-        e_got.append(send(e_give[turn * 264 : (turn + 1) * 264], "y"))
+        sums[step] = panel_sum(panel, gives, step)
+        shared_x.append(send(shared_give[turn], "x"))
+        e_got.append(send(e_grads[turn // 2][1 + turn % 2], "y"))
         if turn == 0:
-            shared_z[2] = swap_z(shared_grads, 2)
-            flying_out = send((out_sums[2] + flying.astype(F32)).astype(BF), "z1")
-        elif turn == 1:
-            for k in (1, 2, 3):
-                shared_grads = put(shared_grads, shared_z[k], lax.rem(z + 4 - k, 4))
+            flying_wo = send(wo_sums[1].astype(BF), "z1")
+            (far, near, sums, e_got, shared_x, shared_give, shared_mine, e_grads, panel, gives, flying_wo,
+             wo_sums) = sync(far, near, sums, e_got, shared_x, shared_give, shared_mine, e_grads, panel, gives,
+                             flying_wo, wo_sums)
+            continue
+        if turn == 1:
+            routed_grads = {2: ed_grad[0].astype(F32) + jnp.concatenate(e_got[:2]).astype(F32)}
             flying = send(sums[1].astype(BF), "z1")
-            flying_out = send((out_sums[3] + flying_out.astype(F32)).astype(BF), "z1")
-            flying_wo = send(wo_sums[1].astype(BF), "z1")
-            wo_sums[3] = panel_sum(wo_part, 3)
-            shared_x = [send(pick(shared_grads, 1 - x, 1)[:2], "x")]
-        elif turn == 2:
-            flying = send((sums[2] + flying.astype(F32)).astype(BF), "z1")
-            flying_wo = send((wo_sums[2] + flying_wo.astype(F32)).astype(BF), "z1")
-            wo_sums[0] = panel_sum(wo_part, 0)
-            shared_x.append(send(pick(shared_grads, 1 - x, 1)[2:], "x"))
+            grad_normed_one = (near + far.astype(F32)).reshape(own, width)
+            in_grad = grad_after + norm_back(grad_normed_one, scaled_one, inverse_one, gain_one)
         else:
-            flying = send((sums[3] + flying.astype(F32)).astype(BF), "z1")
-            flying_wo = send((wo_sums[3] + flying_wo.astype(F32)).astype(BF), "z1")
-            shared_grads = in_order(pick(shared_grads, x, 1), jnp.concatenate(shared_x), x, 1)
-        if turn == 0:
-            sums, e_got, shared_z, shared_grads, e_give, panel, flying_out, wo_part = sync(
-                sums, e_got, shared_z, shared_grads, e_give, panel, flying_out, wo_part)
-        elif turn < 3:
-            sums, e_got, shared_x, shared_grads, flying, e_give, panel, flying_out, flying_wo, wo_sums, wo_part = sync(
-                sums, e_got, shared_x, shared_grads, flying, e_give, panel, flying_out, flying_wo, wo_sums, wo_part)
-    hidden_out = (after_attn + out_sums[0] + flying_out.astype(F32)).astype(BF)
-    out_own = wo_sums[0] + flying_wo.astype(F32)
+            flying = send((sums[turn] + flying.astype(F32)).astype(BF), "z1")
+        if turn == 2:
+            routed_grads[0] = (eg_grad[0].astype(F32) + jnp.concatenate(e_got[2:4]).astype(F32)).T
+        if turn < 3:
+            flying_wo = send((wo_sums[turn + 1] + flying_wo.astype(F32)).astype(BF), "z1")
+            sums, e_got, shared_x, shared_give, flying, e_grads, panel, gives, flying_wo, in_grad, routed_grads = sync(
+                sums, e_got, shared_x, shared_give, flying, e_grads, panel, gives, flying_wo, in_grad, routed_grads)
+        else:
+            out_own = wo_sums[0] + flying_wo.astype(F32)
+            flying, sums, out_own, e_got, shared_x = sync(flying, sums, out_own, e_got, shared_x)
+    shared_grads = in_order(shared_mine, jnp.stack(shared_x), x, 1).reshape(16, rows_w, unit_cols)
+    shared_own = unpack_shared(shared_grads, full_cols, rest_cols)
+    routed_grads[1] = (eu_grad[0].astype(F32) + jnp.concatenate(e_got[4:6]).astype(F32)).T
     total = (sums[0] + flying.astype(F32)).astype(BF)
 
-    total, shared_grads, e_got = sync(total, shared_grads, e_got)
     count = n_fsdp * rows_w
     small_sum = total[count:].reshape(-1)[: n_fsdp * n_small * rows_w].reshape(n_fsdp, n_small * rows_w)
     small_sum = jnp.pad(small_sum, ((0, 0), (0, 3 * wide - n_small * rows_w)))
@@ -843,20 +979,6 @@
         qkv_own = put(qkv_own, send(pick(blocks, place), link), place)
     small_own = jnp.sum(qkv_own[:, rows_w, : n_small * rows_w].astype(F32), axis=0).reshape(n_small, rows_w)
     qkv_own = from_fsdp(qkv_own[:, :rows_w]).astype(F32)
-    shared_grads = shared_grads.reshape(16, rows_w, unit_cols)
-
-    def from_owner(k):
-        full = shared_grads[:, :, k * full_cols : (k + 1) * full_cols]
-        rest = shared_grads[:, :, rest_at + k * rest_cols : rest_at + (k + 1) * rest_cols]
-        return jnp.concatenate(
-            [full.transpose(1, 0, 2).reshape(rows_w, -1), rest.transpose(1, 0, 2).reshape(rows_w, -1)], axis=1
-        ).astype(F32)
-
-    e_got = jnp.concatenate(e_got, axis=0)
-    routed_grads = [
-        grad[:ex_cols].astype(F32) + e_got[k * ex_cols : (k + 1) * ex_cols].astype(F32)
-        for k, grad in enumerate(e_grads)
-    ]
     return (
         hidden_out.reshape(micro, tok, width),
         in_grad.reshape(micro, tok, width),
@@ -869,11 +991,11 @@
         small_own[experts + 2],
         small_own[:experts].T,
         small_own[experts],
-        from_owner(0),
-        from_owner(1),
-        from_owner(2),
-        routed_grads[0].T[None],
-        routed_grads[1].T[None],
+        shared_own[0],
+        shared_own[1],
+        shared_own[2],
+        routed_grads[0][None],
+        routed_grads[1][None],
         routed_grads[2][None],
     )
 

time: 861 us -> 769 us (0.89)
  waiting for transfers between devices: 340 us -> 261 us
  local copies, waits for them, and re-layouts: 140 us -> 115 us
  Pallas kernels: 154 us -> 166 us
    ppermute x134 -> x119, waiting for transfers between devices: 340 us -> 261 us  [send(): return lax.ppermute(value, ALL, ring_perm(MOVES[link]))]
    reshape x14 -> x4, local copies, waits for them, and re-layouts: 11.2 us -> 0.35 us  [the longest x2 0.18 us: on_device_ring(): dot_nn(choice, small).astype(BF).reshape(n_all, n_small + micro, rows_w)]
    pallas_call x2 -> x5, Pallas kernels: 21.1 us -> 31.9 us  [the longest x1 18.7 us: attend(): pl.pallas_call(functools.partial(attend_back_kernel, heads, seq, scale, s...]
    slice x22 -> x9, local copies, waits for them, and re-layouts: 14.8 us -> 4.02 us  [the longest x1 1.74 us: on_device_ring(): wo[:, k * rows_w:(k + 1) * rows_w, 3 * wide:].reshape(n_exp * rows_w, wide)]
    unnamed x454 -> x425, local copies, waits for them, and re-layouts: 50.4 us -> 40.9 us
    dynamic_update_slice x20, local copies, waits for them, and re-layouts: 9.08 us -> 17.8 us  [put(): return lax.dynamic_update_index_in_dim(value, block, place, axis)]
    ppermute x134 -> x119, starting transfers between devices: 93.2 us -> 101 us  [send(): return lax.ppermute(value, ALL, ring_perm(MOVES[link]))]
    pallas_call x4 -> x5, Pallas kernels: 42.6 us -> 43.6 us  [weight_grads(): pl.pallas_call(functools.partial(weights_kernel, n_sets, split), grid=(n_...]
  transfers between devices with their start and end apart: 134 -> 119, of which waited for: 44 -> 44; matrix products, arithmetic and copies ran while one was open for 20% -> 20% of each run, Pallas kernels for 17% -> 22%
where the time goes in v3:
time: 769 us; the launch traced here: 759 us
  waiting for transfers between devices  261 us (34%)
  Pallas kernels  166 us (22%)
  local copies, waits for them, and re-layouts  115 us (15%)
  other arithmetic  103 us (13%)
  starting transfers between devices  101 us (13%)
  matrix products  8.36 us (1%)
    ppermute x119, waiting for transfers between devices, send(): return lax.ppermute(value, ALL, ring_perm(MOVES[link]))  261 us
    ppermute x119, starting transfers between devices, send(): return lax.ppermute(value, ALL, ring_perm(MOVES[link]))  101 us
    pallas_call x4, Pallas kernels, feed(): pl.pallas_call(functools.partial(feed_kernel, experts, shared), in_specs=...  88.4 us
    pallas_call x5, Pallas kernels, weight_grads(): pl.pallas_call(functools.partial(weights_kernel, n_sets, split), grid=(n_...  43.6 us
    unnamed x425, local copies, waits for them, and re-layouts  40.9 us
    pallas_call x1, Pallas kernels, attend(): pl.pallas_call(functools.partial(attend_back_kernel, heads, seq, scale, s...  18.7 us
    dynamic_update_slice x20, local copies, waits for them, and re-layouts, put(): return lax.dynamic_update_index_in_dim(value, block, place, axis)  17.8 us
  transfers between devices with their start and end apart: 119, of which 44 were waited for; matrix products, arithmetic and copies ran while one was open for 20% of the time, Pallas kernels for 22%

profile of v3, /device:TPU:0, one launch (start us, length us, event | category | flops | bytes accessed | tf_op | source)
XLA Modules:
  0.0 758.6 jit_solution(16598046596218880540)
XLA Ops:
  38.0 17.4 %collective-permute-done.6 = bf16[256,2048]{1,0:T(8,128)(2,1)} collective-permute-done((bf16[256,2048]{1,0:T(8,128)(2,1)S(1)}, bf16[256,2048]{1,0:T(8,128)(2,1)}, u32[]{:S(2)}, u32[]{:S(2)}) %collective-permute-start.6) | collective-permute-done | bytes 1048608 | tf_op jit(solution)/shard_map/ppermute | solution.py:571
  68.7 11.7 %collective-permute-done.12 = bf16[256,2048]{1,0:T(8,128)(2,1)} collective-permute-done((bf16[256,2048]{1,0:T(8,128)(2,1)}, bf16[256,2048]{1,0:T(8,128)(2,1)}, u32[]{:S(2)}, u32[]{:S(2)}) %collective-permute-start.12) | collective-permute-done | bytes 1048608 | tf_op jit(solution)/shard_map/ppermute | solution.py:571
  121.7 10.4 %collective-permute-done.24 = bf16[2,2,64,1056]{3,2,1,0:T(8,128)(2,1)S(1)} collective-permute-done((bf16[2,2,64,1056]{3,2,1,0:T(8,128)(2,1)S(1)}, bf16[2,2,64,1056]{3,2,1,0:T(8,128)(2,1)S(1)}, u32[]{:S(2)}, u32[]{:S(2)}) %collective-permute-start.24) | collective-permute-done | bytes 540704 | tf_op jit(solution)/shard_map/ppermute | solution.py:571
  138.7 9.6 %attend.1 = (bf16[512,1536]{1,0:T(8,128)(2,1)S(1)}, bf16[512,256]{1,0:T(8,128)(2,1)S(1)}, bf16[512,256]{1,0:T(8,128)(2,1)}) custom-call(bf16[512,2048]{1,0:T(8,128)(2,1)S(1)} %bitcast.312, bf16[2048,2048]{1,0:T(8,128)(2,1)} %bitcast.72.w_ref, f32[1,1536]{1,0:T(1,128)S(1)} %fusion.44.bias_ref, f32[256,128]{1,0:T(8,128)S(1)} %get-tuple-element.861.cos_ref, ...), custom_call_target="tpu_custom_call" | custom-call | flops 100000000 | bytes 1000000 | tf_op jit(solution)/shard_map/attend/pallas_call | solution.py:213
  154.1 7.7 %collective-permute-done.27.refs_4_.refs_1_ = bf16[128,2176]{1,0:T(8,128)(2,1)S(1)} collective-permute-done((bf16[128,2176]{1,0:T(8,128)(2,1)S(1)}, bf16[128,2176]{1,0:T(8,128)(2,1)S(1)}, u32[]{:S(2)}, u32[]{:S(2)}) %collective-permute-start.27) | collective-permute-done | bytes 557088 | tf_op jit(solution)/shard_map/ppermute | solution.py:571
  174.2 13.1 %collective-permute-done.31 = bf16[2,64,1056]{2,1,0:T(8,128)(2,1)S(1)} collective-permute-done((bf16[2,64,1056]{2,1,0:T(8,128)(2,1)S(1)}, bf16[2,64,1056]{2,1,0:T(8,128)(2,1)S(1)}, u32[]{:S(2)}, u32[]{:S(2)}) %collective-permute-start.31) | collective-permute-done | bytes 270368 | tf_op jit(solution)/shard_map/ppermute | solution.py:571
  203.9 13.9 %collective-permute-done.33 = bf16[4,2,64,1056]{3,2,1,0:T(8,128)(2,1)} collective-permute-done((bf16[4,2,64,1056]{3,2,1,0:T(8,128)(2,1)}, bf16[4,2,64,1056]{3,2,1,0:T(8,128)(2,1)}, u32[]{:S(2)}, u32[]{:S(2)}) %collective-permute-start.33) | collective-permute-done | bytes 1081376 | tf_op jit(solution)/shard_map/ppermute | solution.py:571
  229.5 8.1 %fusion.2 = (bf16[768,2048]{1,0:T(8,128)(2,1)}, bf16[768,2048]{1,0:T(8,128)(2,1)}, bf16[768,2048]{1,0:T(8,128)(2,1)}) fusion(bf16[132,2048]{1,0:T(8,128)(2,1)} %collective-permute-done.30, bf16[132,2048]{1,0:T(8,128)(2,1)} %collective-permute-done.25, bf16[264,2048]{1,0:T(8,128)(2,1)} %copy-done.147, bf16[352,2048]{1,0:T(8,128)(2,1)S(1)} %copy-done.127, ...), kind=kLoop, calls=%fused_computation.8 | loop fusion | flops 48758784 | bytes 18089472 | tf_op jit(solution)/shard_map/concatenate | solution.py:770
  238.2 8.8 %collective-permute-done.38.refs_3_.refs_6_ = bf16[128,2176]{1,0:T(8,128)(2,1)S(1)} collective-permute-done((bf16[128,2176]{1,0:T(8,128)(2,1)}, bf16[128,2176]{1,0:T(8,128)(2,1)S(1)}, u32[]{:S(2)}, u32[]{:S(2)}) %collective-permute-start.38) | collective-permute-done | bytes 557088 | tf_op jit(solution)/shard_map/ppermute | solution.py:571
  260.0 12.5 %collective-permute-done.43.refs_0_.refs_6_ = bf16[128,2048]{1,0:T(8,128)(2,1)S(1)} collective-permute-done((bf16[128,2048]{1,0:T(8,128)(2,1)}, bf16[128,2048]{1,0:T(8,128)(2,1)S(1)}, u32[]{:S(2)}, u32[]{:S(2)}) %collective-permute-start.43) | collective-permute-done | bytes 524320 | tf_op jit(solution)/shard_map/ppermute | solution.py:571
  272.5 8.9 %collective-permute-done.44.refs_1_.refs_4_ = bf16[128,2048]{1,0:T(8,128)(2,1)} collective-permute-done((bf16[128,2048]{1,0:T(8,128)(2,1)}, bf16[128,2048]{1,0:T(8,128)(2,1)}, u32[]{:S(2)}, u32[]{:S(2)}) %collective-permute-start.44) | collective-permute-done | bytes 524320 | tf_op jit(solution)/shard_map/ppermute | solution.py:571
  295.3 22.0 %feed.4 = (bf16[512,384]{1,0:T(8,128)(2,1)}, bf16[512,384]{1,0:T(8,128)(2,1)}, bf16[512,384]{1,0:T(8,128)(2,1)}, bf16[512,768]{1,0:T(8,128)(2,1)}, bf16[512,768]...) custom-call(s32[1]{0:T(128)} %bitcast.100.expert_ref, ...), custom_call_target="tpu_custom_call" | custom-call | flops 16000000000 | bytes 30000000 | tf_op jit(solution)/shard_map/feed/pallas_call | solution.py:322
  322.4 22.1 %feed.5 = (bf16[512,384]{1,0:T(8,128)(2,1)}, bf16[512,384]{1,0:T(8,128)(2,1)}, bf16[512,384]{1,0:T(8,128)(2,1)}, bf16[512,768]{1,0:T(8,128)(2,1)}, bf16[512,768]...) custom-call(s32[1]{0:T(128)} %bitcast.100.expert_ref, ...), custom_call_target="tpu_custom_call" | custom-call | flops 16000000000 | bytes 30000000 | tf_op jit(solution)/shard_map/feed/pallas_call | solution.py:322
  351.5 22.3 %feed.6 = (bf16[512,384]{1,0:T(8,128)(2,1)}, bf16[512,384]{1,0:T(8,128)(2,1)}, bf16[512,384]{1,0:T(8,128)(2,1)}, bf16[512,768]{1,0:T(8,128)(2,1)}, bf16[512,768]...) custom-call(s32[1]{0:T(128)} %bitcast.100.expert_ref, ...), custom_call_target="tpu_custom_call" | custom-call | flops 16000000000 | bytes 30000000 | tf_op jit(solution)/shard_map/feed/pallas_call | solution.py:322
  382.2 22.0 %feed.7 = (bf16[512,384]{1,0:T(8,128)(2,1)}, bf16[512,384]{1,0:T(8,128)(2,1)}, bf16[512,384]{1,0:T(8,128)(2,1)}, bf16[512,768]{1,0:T(8,128)(2,1)}, bf16[512,768]...) custom-call(s32[1]{0:T(128)} %bitcast.100.expert_ref, ...), custom_call_target="tpu_custom_call" | custom-call | flops 16000000000 | bytes 30000000 | tf_op jit(solution)/shard_map/feed/pallas_call | solution.py:322
  429.4 8.9 %weight_grads.5 = (bf16[384,1024]{1,0:T(8,128)(2,1)S(1)}, bf16[384,1024]{1,0:T(8,128)(2,1)S(1)}, bf16[384,1024]{1,0:T(8,128)(2,1)S(1)}, bf16[384,1024]{1,0:T(8,128)(2,1)S(1)}) custom-call(s32[1]{0:T(128)} %bitcast.87.y_ref, bf16[128,2048]{1,0:T(8,128)(2,1)S(1)} %copy-done.3, bf16[128,2048]{1,0:T(8,128)(2,1)} %collective-permute-done.39.refs_1_, ...), custom_call_target="tpu_custom_call" | custom-call | flops 8000000000 | bytes 20000000 | tf_op jit(solution)/shard_map/weight_grads/pallas_call | solution.py:502
  475.2 9.2 %weight_grads.7 = (bf16[352,2048]{1,0:T(8,128)(2,1)S(1)}, bf16[176,2048]{1,0:T(8,128)(2,1)S(1)}, bf16[176,2048]{1,0:T(8,128)(2,1)S(1)}) custom-call(s32[1]{0:T(128)} %bitcast.87.y_ref, bf16[128,2176]{1,0:T(8,128)(2,1)S(1)} %copy-done.10, bf16[128,2176]{1,0:T(8,128)(2,1)S(1)} %copy-done.35, bf16[256,2176]{1,0:T(8,128)(2,1)S(1)} %copy-done.66, ...), custom_call_target="tpu_custom_call" | custom-call | flops 8000000000 | bytes 20000000 | tf_op jit(solution)/shard_map/weight_grads/pallas_call | solution.py:502
  543.7 7.7 %collective-permute-done.86 = bf16[128,2048]{1,0:T(8,128)(2,1)S(1)} collective-permute-done((bf16[128,2048]{1,0:T(8,128)(2,1)S(1)}, bf16[128,2048]{1,0:T(8,128)(2,1)S(1)}, u32[]{:S(2)}, u32[]{:S(2)}) %collective-permute-start.86) | collective-permute-done | bytes 524320 | tf_op jit(solution)/shard_map/ppermute | solution.py:571
  554.9 18.7 %attend_back.1 = (bf16[512,1536]{1,0:T(8,128)(2,1)S(1)}, f32[512,2048]{1,0:T(8,128)}, bf16[8,264,1536]{2,1,0:T(8,128)(2,1)}) custom-call(bf16[512,256]{1,0:T(8,128)(2,1)S(1)} %get-tuple-element.1427.grad_ref, bf16[512,256]{1,0:T(8,128)(2,1)S(1)} %bitcast.321, bf16[512,1536]{1,0:T(8,128)(2,1)S(1)} %copy-done.12, f32[256,128]{1,0:T(8,128)S(1)} %copy-done.18, ...), custom_call_target="tpu_custom_call" | custom-call | flops 100000000 | bytes 1000000 | tf_op jit(solution)/shard_map/attend_back/pallas_call | solution.py:229
  598.3 10.6 %weight_grads.8 = (bf16[352,2048]{1,0:T(8,128)(2,1)S(1)}, bf16[176,2048]{1,0:T(8,128)(2,1)S(1)}, bf16[176,2048]{1,0:T(8,128)(2,1)}) custom-call(s32[1]{0:T(128)} %bitcast.87.y_ref, bf16[128,2048]{1,0:T(8,128)(2,1)S(1)} %copy-done.3, bf16[128,2048]{1,0:T(8,128)(2,1)} %collective-permute-done.39.refs_1_, bf16[256,2048]{1,0:T(8,128)(2,1)} %collective-permute-done.42.refs_2_, ...), custom_call_target="tpu_custom_call" | custom-call | flops 8000000000 | bytes 20000000 | tf_op jit(solution)/shard_map/weight_grads/pallas_call | solution.py:502
  619.9 9.4 %collective-permute-done.94 = bf16[2,2,64,1056]{3,2,1,0:T(8,128)(2,1)S(1)} collective-permute-done((bf16[2,2,64,1056]{3,2,1,0:T(8,128)(2,1)S(1)}, bf16[2,2,64,1056]{3,2,1,0:T(8,128)(2,1)S(1)}, u32[]{:S(2)}, u32[]{:S(2)}) %collective-permute-start.94) | collective-permute-done | bytes 540704 | tf_op jit(solution)/shard_map/ppermute | solution.py:571
  635.0 9.8 %weight_grads.9 = (bf16[352,2048]{1,0:T(8,128)(2,1)S(1)}, bf16[176,2048]{1,0:T(8,128)(2,1)S(1)}, bf16[176,2048]{1,0:T(8,128)(2,1)S(1)}) custom-call(s32[1]{0:T(128)} %bitcast.87.y_ref, bf16[128,2048]{1,0:T(8,128)(2,1)S(1)} %copy-done.3, bf16[128,2048]{1,0:T(8,128)(2,1)} %collective-permute-done.39.refs_1_, ...), custom_call_target="tpu_custom_call" | custom-call | flops 8000000000 | bytes 20000000 | tf_op jit(solution)/shard_map/weight_grads/pallas_call | solution.py:502
  696.5 11.0 %collective-permute-done.107 = bf16[264,1536]{1,0:T(8,128)(2,1)S(1)} collective-permute-done((bf16[264,1536]{1,0:T(8,128)(2,1)S(1)}, bf16[264,1536]{1,0:T(8,128)(2,1)S(1)}, u32[]{:S(2)}, u32[]{:S(2)}) %collective-permute-start.107) | collective-permute-done | bytes 811040 | tf_op jit(solution)/shard_map/ppermute | solution.py:571
  721.1 11.6 %collective-permute-done.113 = bf16[264,1536]{1,0:T(8,128)(2,1)S(1)} collective-permute-done((bf16[264,1536]{1,0:T(8,128)(2,1)S(1)}, bf16[264,1536]{1,0:T(8,128)(2,1)S(1)}, u32[]{:S(2)}, u32[]{:S(2)}) %collective-permute-start.113) | collective-permute-done | bytes 811040 | tf_op jit(solution)/shard_map/ppermute | solution.py:571
  (924 shorter events, 446.8 us)
Async XLA Ops:
  102.3 29.8 %collective-permute-start.21 = (bf16[256,2048]{1,0:T(8,128)(2,1)}, bf16[256,2048]{1,0:T(8,128)(2,1)S(1)}, u32[]{:S(2)}, u32[]{:S(2)}) collective-permute-start(bf16[256,2048]{1,0:T(8,128)(2,1)} %collective-permute-done.16), channel_id=1, source_target_pairs={{0,4},{1,5},{2,6},{3,7},{4,0},{5,1},{6,2},{7,3},{8,12},{9,13},{10,... | collective-permute-start | bytes 3145736 | tf_op jit(solution)/shard_map/ppermute | solution.py:571
  102.3 29.7 %collective-permute-start.22 = (bf16[264,2048]{1,0:T(8,128)(2,1)S(1)}, bf16[264,2048]{1,0:T(8,128)(2,1)S(1)}, u32[]{:S(2)}, u32[]{:S(2)}) collective-permute-start(bf16[264,2048]{1,0:T(8,128)(2,1)S(1)} %copy-done.148), channel_id=1, source_target_pairs={{0,2},{1,3},{2,0},{3,1},{4,6},{5,7},{6,4},{7,5},{8,10},{9,11},{10,... | collective-permute-start | bytes 3244040 | tf_op jit(solution)/shard_map/ppermute | solution.py:571
  190.7 27.1 %collective-permute-start.33 = (bf16[4,2,64,1056]{3,2,1,0:T(8,128)(2,1)}, bf16[4,2,64,1056]{3,2,1,0:T(8,128)(2,1)}, u32[]{:S(2)}, u32[]{:S(2)}) collective-permute-start(bf16[4,2,64,1056]{3,2,1,0:T(8,128)(2,1)} %get-tuple-element.1641), channel_id=1, source_target_pairs={{0,4},{1,5},{2,6},{3,7},{4,0},{5,1},{6,2},{7,3},{8,12},{9,13},{10,... | collective-permute-start | bytes 3244040 | tf_op jit(solution)/shard_map/ppermute | solution.py:571
  192.1 29.4 %collective-permute-start.34 = (bf16[128,2176]{1,0:T(8,128)(2,1)S(1)}, bf16[128,2176]{1,0:T(8,128)(2,1)}, u32[]{:S(2)}, u32[]{:S(2)}) collective-permute-start(bf16[128,2176]{1,0:T(8,128)(2,1)S(1)} %fusion.27.refs_3_.refs_0_), channel_id=1, source_target_pairs={{0,8},{1,9},{2,10},{3,11},{4,12},{5,13},{6,14},{7,15},{8,16},{9,17... | collective-permute-start | bytes 1671176 | tf_op jit(solution)/shard_map/ppermute | solution.py:571
  193.1 28.3 %collective-permute-start.35 = (bf16[256,2176]{1,0:T(8,128)(2,1)}, bf16[256,2176]{1,0:T(8,128)(2,1)S(1)}, u32[]{:S(2)}, u32[]{:S(2)}) collective-permute-start(bf16[256,2176]{1,0:T(8,128)(2,1)} %pad_maximum_fusion.7), channel_id=1, source_target_pairs={{0,1},{1,0},{2,3},{3,2},{4,5},{5,4},{6,7},{7,6},{8,9},{9,8},{10,11... | collective-permute-start | bytes 3342344 | tf_op jit(solution)/shard_map/ppermute | solution.py:571
  252.4 29.0 %collective-permute-start.41 = (bf16[528,1024]{1,0:T(8,128)(2,1)}, bf16[528,1024]{1,0:T(8,128)(2,1)}, u32[]{:S(2)}, u32[]{:S(2)}) collective-permute-start(bf16[528,1024]{1,0:T(8,128)(2,1)} %slice.320), channel_id=1, source_target_pairs={{0,2},{1,3},{2,0},{3,1},{4,6},{5,7},{6,4},{7,5},{8,10},{9,11},{10,... | collective-permute-start | bytes 3244040 | tf_op jit(solution)/shard_map/ppermute | solution.py:571
  285.1 32.2 %collective-permute-start.48 = (bf16[128,2048]{1,0:T(8,128)(2,1)S(1)}, bf16[128,2048]{1,0:T(8,128)(2,1)S(1)}, u32[]{:S(2)}, u32[]{:S(2)}) collective-permute-start(bf16[128,2048]{1,0:T(8,128)(2,1)S(1)} %copy-done.44), channel_id=1, source_target_pairs={{0,8},{1,9},{2,10},{3,11},{4,12},{5,13},{6,14},{7,15},{8,16},{9,17... | collective-permute-start | bytes 1572872 | tf_op jit(solution)/shard_map/ppermute | solution.py:571
  288.0 29.3 %collective-permute-start.50 = (bf16[128,2048]{1,0:T(8,128)(2,1)S(1)}, bf16[128,2048]{1,0:T(8,128)(2,1)S(1)}, u32[]{:S(2)}, u32[]{:S(2)}) collective-permute-start(bf16[128,2048]{1,0:T(8,128)(2,1)S(1)} %copy-done.44), channel_id=1, source_target_pairs={{0,4},{1,5},{2,6},{3,7},{4,0},{5,1},{6,2},{7,3},{8,12},{9,13},{10,... | collective-permute-start | bytes 1572872 | tf_op jit(solution)/shard_map/ppermute | solution.py:571
  289.8 27.5 %collective-permute-start.46 = (bf16[256,2048]{1,0:T(8,128)(2,1)S(1)}, bf16[256,2048]{1,0:T(8,128)(2,1)S(1)}, u32[]{:S(2)}, u32[]{:S(2)}) collective-permute-start(bf16[256,2048]{1,0:T(8,128)(2,1)S(1)} %pad_maximum_fusion.12), channel_id=1, source_target_pairs={{0,1},{1,0},{2,3},{3,2},{4,5},{5,4},{6,7},{7,6},{8,9},{9,8},{10,11... | collective-permute-start | bytes 3145736 | tf_op jit(solution)/shard_map/ppermute | solution.py:571
  318.6 28.9 %collective-permute-start.51 = (bf16[256,2048]{1,0:T(8,128)(2,1)}, bf16[256,2048]{1,0:T(8,128)(2,1)}, u32[]{:S(2)}, u32[]{:S(2)}) collective-permute-start(bf16[256,2048]{1,0:T(8,128)(2,1)} %pad_maximum_fusion.13), channel_id=1, source_target_pairs={{0,1},{1,0},{2,3},{3,2},{4,5},{5,4},{6,7},{7,6},{8,9},{9,8},{10,11... | collective-permute-start | bytes 3145736 | tf_op jit(solution)/shard_map/ppermute | solution.py:571
  320.1 27.5 %collective-permute-start.52 = (bf16[256,2176]{1,0:T(8,128)(2,1)S(1)}, bf16[256,2176]{1,0:T(8,128)(2,1)S(1)}, u32[]{:S(2)}, u32[]{:S(2)}) collective-permute-start(bf16[256,2176]{1,0:T(8,128)(2,1)S(1)} %pad_maximum_fusion.9), channel_id=1, source_target_pairs={{0,1},{1,0},{2,3},{3,2},{4,5},{5,4},{6,7},{7,6},{8,9},{9,8},{10,11... | collective-permute-start | bytes 3342344 | tf_op jit(solution)/shard_map/ppermute | solution.py:571
  320.4 27.2 %collective-permute-start.53 = (bf16[128,2048]{1,0:T(8,128)(2,1)S(1)}, bf16[128,2048]{1,0:T(8,128)(2,1)S(1)}, u32[]{:S(2)}, u32[]{:S(2)}) collective-permute-start(bf16[128,2048]{1,0:T(8,128)(2,1)S(1)} %collective-permute-done.48.refs_0_.refs_9_), channel_id=1, source_target_pairs={{0,4},{1,5},{2,6},{3,7},{4,0},{5,1},{6,2},{7,3},{8,12},{9,13},{10,... | collective-permute-start | bytes 1572872 | tf_op jit(solution)/shard_map/ppermute | solution.py:571
  348.8 30.7 %collective-permute-start.56 = (bf16[256,2048]{1,0:T(8,128)(2,1)}, bf16[256,2048]{1,0:T(8,128)(2,1)S(1)}, u32[]{:S(2)}, u32[]{:S(2)}) collective-permute-start(bf16[256,2048]{1,0:T(8,128)(2,1)} %pad_maximum_fusion.14), channel_id=1, source_target_pairs={{0,1},{1,0},{2,3},{3,2},{4,5},{5,4},{6,7},{7,6},{8,9},{9,8},{10,11... | collective-permute-start | bytes 3145736 | tf_op jit(solution)/shard_map/ppermute | solution.py:571
  349.5 30.1 %collective-permute-start.57 = (bf16[256,2176]{1,0:T(8,128)(2,1)S(1)}, bf16[256,2176]{1,0:T(8,128)(2,1)S(1)}, u32[]{:S(2)}, u32[]{:S(2)}) collective-permute-start(bf16[256,2176]{1,0:T(8,128)(2,1)S(1)} %pad_maximum_fusion.10), channel_id=1, source_target_pairs={{0,1},{1,0},{2,3},{3,2},{4,5},{5,4},{6,7},{7,6},{8,9},{9,8},{10,11... | collective-permute-start | bytes 3342344 | tf_op jit(solution)/shard_map/ppermute | solution.py:571
  349.8 27.3 %collective-permute-start.58 = (bf16[256,2176]{1,0:T(8,128)(2,1)}, bf16[256,2176]{1,0:T(8,128)(2,1)}, u32[]{:S(2)}, u32[]{:S(2)}) collective-permute-start(bf16[256,2176]{1,0:T(8,128)(2,1)} %get-tuple-element.1052), channel_id=1, source_target_pairs={{0,1},{1,0},{2,3},{3,2},{4,5},{5,4},{6,7},{7,6},{8,9},{9,8},{10,11... | collective-permute-start | bytes 3342344 | tf_op jit(solution)/shard_map/ppermute | solution.py:571
  379.6 31.7 %collective-permute-start.61 = (bf16[256,2176]{1,0:T(8,128)(2,1)}, bf16[256,2176]{1,0:T(8,128)(2,1)S(1)}, u32[]{:S(2)}, u32[]{:S(2)}) collective-permute-start(bf16[256,2176]{1,0:T(8,128)(2,1)} %get-tuple-element.1087), channel_id=1, source_target_pairs={{0,1},{1,0},{2,3},{3,2},{4,5},{5,4},{6,7},{7,6},{8,9},{9,8},{10,11... | collective-permute-start | bytes 3342344 | tf_op jit(solution)/shard_map/ppermute | solution.py:571
  380.7 27.5 %collective-permute-start.63 = (bf16[256,2048]{1,0:T(8,128)(2,1)}, bf16[256,2048]{1,0:T(8,128)(2,1)S(1)}, u32[]{:S(2)}, u32[]{:S(2)}) collective-permute-start(bf16[256,2048]{1,0:T(8,128)(2,1)} %get-tuple-element.1104), channel_id=1, source_target_pairs={{0,1},{1,0},{2,3},{3,2},{4,5},{5,4},{6,7},{7,6},{8,9},{9,8},{10,11... | collective-permute-start | bytes 3145736 | tf_op jit(solution)/shard_map/ppermute | solution.py:571
  415.9 29.5 %collective-permute-start.66 = (bf16[256,2176]{1,0:T(8,128)(2,1)}, bf16[256,2176]{1,0:T(8,128)(2,1)}, u32[]{:S(2)}, u32[]{:S(2)}) collective-permute-start(bf16[256,2176]{1,0:T(8,128)(2,1)} %get-tuple-element.1163), channel_id=1, source_target_pairs={{0,1},{1,0},{2,3},{3,2},{4,5},{5,4},{6,7},{7,6},{8,9},{9,8},{10,11... | collective-permute-start | bytes 3342344 | tf_op jit(solution)/shard_map/ppermute | solution.py:571
  415.9 31.4 %collective-permute-start.67 = (bf16[128,2176]{1,0:T(8,128)(2,1)}, bf16[128,2176]{1,0:T(8,128)(2,1)}, u32[]{:S(2)}, u32[]{:S(2)}) collective-permute-start(bf16[128,2176]{1,0:T(8,128)(2,1)} %convert_add_fusion.8), channel_id=1, source_target_pairs={{0,8},{1,9},{2,10},{3,11},{4,12},{5,13},{6,14},{7,15},{8,16},{9,17... | collective-permute-start | bytes 1671176 | tf_op jit(solution)/shard_map/ppermute | solution.py:571
  587.3 32.0 %collective-permute-start.91 = (bf16[2,2,64,2048]{3,2,0,1:T(8,128)(2,1)S(1)}, bf16[2,2,64,2048]{3,2,0,1:T(8,128)(2,1)S(1)}, u32[]{:S(2)}, u32[]{:S(2)}) collective-permute-start(bf16[2,2,64,2048]{3,2,0,1:T(8,128)(2,1)S(1)} %fusion.13), channel_id=1, source_target_pairs={{0,1},{1,0},{2,3},{3,2},{4,5},{5,4},{6,7},{7,6},{8,9},{9,8},{10,11... | collective-permute-start | bytes 3145736 | tf_op jit(solution)/shard_map/ppermute | solution.py:571
  587.4 41.9 %collective-permute-start.92 = (bf16[176,2048]{1,0:T(8,128)(2,1)}, bf16[176,2048]{1,0:T(8,128)(2,1)S(1)}, u32[]{:S(2)}, u32[]{:S(2)}) collective-permute-start(bf16[176,2048]{1,0:T(8,128)(2,1)} %copy-done.84), channel_id=1, source_target_pairs={{0,2},{1,3},{2,0},{3,1},{4,6},{5,7},{6,4},{7,5},{8,10},{9,11},{10,... | collective-permute-start | bytes 2162696 | tf_op jit(solution)/shard_map/ppermute | solution.py:571
  589.0 30.8 %collective-permute-start.93 = (bf16[2,2,64,1056]{3,2,1,0:T(8,128)(2,1)S(1)}, bf16[2,2,64,1056]{3,2,1,0:T(8,128)(2,1)S(1)}, u32[]{:S(2)}, u32[]{:S(2)}) collective-permute-start(bf16[2,2,64,1056]{3,2,1,0:T(8,128)(2,1)S(1)} %copy-done.168), channel_id=1, source_target_pairs={{0,8},{1,9},{2,10},{3,11},{4,12},{5,13},{6,14},{7,15},{8,16},{9,17... | collective-permute-start | bytes 1622024 | tf_op jit(solution)/shard_map/ppermute | solution.py:571
  589.7 27.5 %collective-permute-start.95 = (bf16[64,2048]{1,0:T(8,128)(2,1)}, bf16[64,2048]{1,0:T(8,128)(2,1)S(1)}, u32[]{:S(2)}, u32[]{:S(2)}) collective-permute-start(bf16[64,2048]{1,0:T(8,128)(2,1)} %get-tuple-element.1480), channel_id=1, source_target_pairs={{0,4},{1,5},{2,6},{3,7},{4,0},{5,1},{6,2},{7,3},{8,12},{9,13},{10,... | collective-permute-start | bytes 786440 | tf_op jit(solution)/shard_map/ppermute | solution.py:571
  660.3 27.5 %collective-permute-start.103 = (bf16[176,2048]{1,0:T(8,128)(2,1)}, bf16[176,2048]{1,0:T(8,128)(2,1)}, u32[]{:S(2)}, u32[]{:S(2)}) collective-permute-start(bf16[176,2048]{1,0:T(8,128)(2,1)} %get-tuple-element.1553), channel_id=1, source_target_pairs={{0,2},{1,3},{2,0},{3,1},{4,6},{5,7},{6,4},{7,5},{8,10},{9,11},{10,... | collective-permute-start | bytes 2162696 | tf_op jit(solution)/shard_map/ppermute | solution.py:571
  (307 other events, 3731.5 us)

commit v4 on v3

--- a/solution.py
+++ b/solution.py
@@ -137,7 +137,7 @@
 
 
 def attend_back_kernel(heads, seq, scale, split, grad_ref, other_ref, qkv_ref, cos_ref, sin_ref, place_ref, seg_ref,
-                       place_row_ref, seg_row_ref, core_ref, w_ref, x_ref, lin_ref, normed_ref, *panel_refs):
+                       place_row_ref, seg_row_ref, core_ref, w_ref, x_ref, lin_ref, normed_ref, gain_ref, *panel_refs):
     cosine, sine = cos_ref[...], sin_ref[...]
     span = heads * HEAD
     if split:
@@ -187,7 +187,9 @@
 
     @pl.when(pl.program_id(0) > 0)
     def _():
-        normed_ref[...] += part
+        total = normed_ref[...] + part
+        normed_ref[...] = total
+        gain_ref[...] = jnp.sum(total * x_ref[...].astype(F32), axis=0, keepdims=True)
 
 
 def whole(shape):
@@ -233,9 +235,11 @@
         + [pl.BlockSpec((rows, 3 * span), lambda p: (0, p))]
         + common_specs
         + [pl.BlockSpec((wqkv.shape[0], 3 * span), lambda p: (0, p)), whole(normed.shape)],
-        out_specs=[pl.BlockSpec((rows, 3 * span), lambda p: (0, p)), whole((rows, wqkv.shape[0]))]
+        out_specs=[
+            pl.BlockSpec((rows, 3 * span), lambda p: (0, p)), whole((rows, wqkv.shape[0])), whole((1, wqkv.shape[0]))]
         + ([pl.BlockSpec(panel[:2] + (3 * span,), lambda p: (0, 0, p))] if split else []),
-        out_shape=[jax.ShapeDtypeStruct((rows, wide3), BF), jax.ShapeDtypeStruct((rows, wqkv.shape[0]), F32)]
+        out_shape=[jax.ShapeDtypeStruct((rows, wide3), BF)]
+        + [jax.ShapeDtypeStruct((count, wqkv.shape[0]), F32) for count in (rows, 1)]
         + ([jax.ShapeDtypeStruct(panel, BF)] if split else []),
         compiler_params=params,
         cost_estimate=cost,
@@ -363,30 +367,30 @@
     )(gate, up, down)
 
 
-def unpack_kernel(full, rest, in_ref, *out_refs):
+def unpack_kernel(full, rest, order_ref, in_ref, *out_refs):
     count = in_ref.shape[0]
     for k in range(3):
         for j in range(count):
-            out_refs[k][:, j * full : (j + 1) * full] = in_ref[j, :, k * full : (k + 1) * full].astype(F32)
+            out_refs[k][:, j * full : (j + 1) * full] = in_ref[order_ref[j], :, k * full : (k + 1) * full].astype(F32)
         low = 3 * full + k * rest
         for j in range(0, count, 4):
             at = count * full + j * rest
-            piece = jnp.concatenate([in_ref[j + i, :, low : low + rest] for i in range(4)], axis=1)
+            piece = jnp.concatenate([in_ref[order_ref[j + i], :, low : low + rest] for i in range(4)], axis=1)
             out_refs[k][:, at : at + 4 * rest] = piece.astype(F32)
 
 
-def unpack_shared(blocks, full, rest):
+def unpack_shared(blocks, order, full, rest):
     count, rows, _ = blocks.shape
     vmem = pl.BlockSpec(memory_space=pltpu.VMEM)
     return pl.pallas_call(
         functools.partial(unpack_kernel, full, rest),
-        in_specs=[vmem],
+        in_specs=[pl.BlockSpec(memory_space=pltpu.SMEM), vmem],
         out_specs=[vmem] * 3,
         out_shape=[jax.ShapeDtypeStruct((rows, count * (full + rest)), F32)] * 3,
         compiler_params=pltpu.CompilerParams(vmem_limit_bytes=16 * 2**20),
         cost_estimate=SMALL_COST,
         name="unpack_shared",
-    )(blocks)
+    )(order, blocks)
 
 
 def fold_kernel(full, rest, *refs):
@@ -412,39 +416,35 @@
     )(*[item for pair in pairs for item in pair])
 
 
-def join_kernel(cuts, y_ref, mine_ref, low_ref, high_ref, behind_ref, *out_refs):
-    half = low_ref.shape[0]
+def join_kernel(cuts, places_ref, *refs):
+    mine_refs, far_refs, behind_ref, out_refs = refs[:2], refs[2:4], refs[4], refs[5:]
+    n_blocks = mine_refs[0].shape[1] // LANES
+    y = places_ref[2 * n_blocks]
     for k, pieces in enumerate(cuts):
         at = 0
         for low, count in pieces:
-            for block in range(mine_ref.shape[1] // LANES):
-                columns = slice(block * LANES, (block + 1) * LANES)
-                target = pl.ds(pl.multiple_of((2 * block + y_ref[0]) * LANES, LANES), LANES)
-                out_refs[k][at : at + count, target] = mine_ref[low : low + count, columns]
-                target = pl.ds(pl.multiple_of((2 * block + 1 - y_ref[0]) * LANES, LANES), LANES)
-                middle = min(max(half - low, 0), count)
-                if middle:
-                    out_refs[k][at : at + middle, target] = low_ref[low : low + middle, columns]
-                if middle < count:
-                    begin = low + middle - half
-                    out_refs[k][at + middle : at + count, target] = high_ref[begin : begin + count - middle, columns]
+            for block in range(2 * n_blocks):
+                half, column = block // n_blocks, block % n_blocks * LANES
+                for source, side in ((mine_refs[half], y), (far_refs[half], 1 - y)):
+                    target = pl.ds(pl.multiple_of((2 * places_ref[block] + side) * LANES, LANES), LANES)
+                    out_refs[k][at : at + count, target] = source[low : low + count, column : column + LANES]
             at += count
         rest = out_refs[k].shape[0] - at
         out_refs[k][at:, :] = behind_ref[...] if k == 0 else jnp.zeros((rest, out_refs[k].shape[1]), BF)
 
 
-def join_shared(y, mine, low, high, behind, cuts):
+def join_shared(places, mine, far, behind, cuts):
     rows = sum(count for _, count in cuts[0]) + behind.shape[0]
     vmem = pl.BlockSpec(memory_space=pltpu.VMEM)
     return pl.pallas_call(
         functools.partial(join_kernel, cuts),
-        in_specs=[pl.BlockSpec(memory_space=pltpu.SMEM)] + [vmem] * 4,
+        in_specs=[pl.BlockSpec(memory_space=pltpu.SMEM)] + [vmem] * 5,
         out_specs=[vmem] * 3,
-        out_shape=[jax.ShapeDtypeStruct((rows, 2 * mine.shape[1]), BF)] * 3,
+        out_shape=[jax.ShapeDtypeStruct((rows, 4 * mine[0].shape[1]), BF)] * 3,
         compiler_params=pltpu.CompilerParams(vmem_limit_bytes=24 * 2**20),
-        cost_estimate=pl.CostEstimate(flops=0, bytes_accessed=10**7, transcendentals=0),
+        cost_estimate=SMALL_COST,
         name="join_shared",
-    )(y, mine, low, high, behind)
+    )(places, *mine, *far, behind)
 
 
 def weights_kernel(n_sets, split, y_ref, *refs):
@@ -508,7 +508,7 @@
         out_specs=[whole(shape) for shape in shapes],
         scratch_shapes=[pltpu.VMEM((4 * rows, width), BF), pltpu.SemaphoreType.DMA((12,))],
         out_shape=[jax.ShapeDtypeStruct(shape, BF) for shape in shapes],
-        compiler_params=pltpu.CompilerParams(vmem_limit_bytes=36 * 2**20),
+        compiler_params=pltpu.CompilerParams(vmem_limit_bytes=56 * 2**20),
         cost_estimate=pl.CostEstimate(
             flops=4 * 10**9 * n_sets * n_tiles, bytes_accessed=2 * 10**7, transcendentals=0),
         name="weight_grads",
@@ -627,10 +627,6 @@
     def swap_z(blocks, k):
         return send(pick(blocks, lax.rem(z + k, 4)), f"z{k}")
 
-    def swap_x(blocks):
-        mine, give = pick(blocks, x, 1), pick(blocks, 1 - x, 1)
-        return in_order(mine, send(give, "x"), x, 1)
-
     small = jnp.concatenate(
         [w_router.T, shared_gate[None], norm_gain1[None], norm_gain2[None], b_qkv, seg_ids.astype(BF)], axis=0)
     n_small = experts + 6
@@ -719,31 +715,48 @@
         return jnp.concatenate([value[:, :, 1:], value[:, :, :1]], axis=2).reshape(micro * seq, -1)
 
     core_place = c.reshape(1)
-    got = [send(a_blocks[3][:132], "y")]
+    got = send(a_blocks[3], "y")
     far_w = pick(shared_w, lax.rem(z + 2, 4))
     shared_z[2] = [send(far_w[0], "z2")]
+    shared_z[0] = pick(shared_w, z)
+    shared_x = {}
+
+    def swap_x(steps):
+        arrived = send(jnp.stack([pick(shared_z[step], 1 - x) for step in steps]), "x")
+        return arrived, [pick(shared_z[step], x) for step in steps]
+
+    def as_columns(parts):
+        blocks = [
+            in_order(mine, arrived[k], x, 0) for arrived, all_mine in parts for k, mine in enumerate(all_mine)
+        ]
+        return jnp.stack(blocks).reshape(-1, unit_cols).T
+
+    shared_x = [swap_x((0, 1))]
     g_pair.append(send(g_own[0], "x"))
     qkv_seq, keep, give = attend(normed_seq, wqkv, bias, tables, seq, core=core_place)
     wo = sync(weights, give)[0]
     wo = [wo[:, k * rows_w : (k + 1) * rows_w, 3 * wide :].reshape(n_exp * rows_w, wide) for k in range(n_fsdp)]
     wo = jnp.concatenate(wo, axis=1)
-    got, shared_z, qkv_seq, keep, give, wqkv, wo, far_w, g_pair, a_blocks = sync(
-        got, shared_z, qkv_seq, keep, give, wqkv, wo, far_w, g_pair, a_blocks)
-    got.append(send(a_blocks[3][132:], "y"))
+    got, shared_z, shared_x, qkv_seq, keep, give, wqkv, wo, far_w, g_pair = sync(
+        got, shared_z, shared_x, qkv_seq, keep, give, wqkv, wo, far_w, g_pair)
+    got_blocks.append(got)
+    shared_w = [as_columns(shared_x)]
+    arrived = turned(send(give, "core"))
+    shared_z, shared_w, arrived, keep, wo, far_w, g_own, g_pair = sync(
+        shared_z, shared_w, arrived, keep, wo, far_w, g_own, g_pair)
     shared_z[2].append(send(far_w[1], "z2"))
-    arrived = turned(send(give, "core"))
+    arrived_w = [send(shared_w[0], "y")]
+    shared_x = [swap_x((3,))]
     attended = jnp.where(c == 0, jnp.concatenate([keep, arrived], axis=1), jnp.concatenate([arrived, keep], axis=1))
     attn_part = contract("tc,cd->td", attended, wo).reshape(micro, 2, 2, tok, width)
     attn_part = attn_part[:, :, 0] + send(attn_part[:, :, 1].astype(BF), "core").astype(F32)
     near, last = attn_part[:, 0], attn_part[:, 1].astype(BF)
-    last, near, got, shared_z, shared_w, g_own, g_pair = sync(last, near, got, shared_z, shared_w, g_own, g_pair)
-    got_blocks += got
-    for k in (1, 2, 3):
-        arrived = jnp.stack(shared_z[2]) if k == 2 else shared_z[k]
-        shared_w = put(shared_w, arrived, lax.rem(z + 4 - k, 4))
+    last, near, shared_z, shared_x, shared_w, arrived_w, g_own, g_pair = sync(
+        last, near, shared_z, shared_x, shared_w, arrived_w, g_own, g_pair)
+    shared_z[2] = jnp.stack(shared_z[2])
 
     last = send(last, "y")
-    shared_w = swap_x(shared_w)
+    shared_x.append(swap_x((2,)))
     g_own.append(send(g_own[0], "z1"))
 
     def blocks_of(mine, other):
@@ -754,12 +767,11 @@
     scaled_two, inverse_two = normalize(after_attn)
     normed_two = (scaled_two * gain_two).astype(BF)
     x_own, x_pair = [normed_two], []
-    shared_w, x_own, after_attn, scaled_two, g_own, g_pair, got_blocks, g_four = sync(
-        shared_w, x_own, after_attn, scaled_two, g_own, g_pair, got_blocks, g_four)
-
-    half = unit_cols // 2
-    shared_w = shared_w.reshape(16 * rows_w, unit_cols).T
-    arrived = [send(shared_w[:half], "y")]
+    shared_w.append(as_columns(shared_x))
+    shared_w, arrived_w, x_own, after_attn, scaled_two, g_own, g_pair, got_blocks, g_four = sync(
+        shared_w, arrived_w, x_own, after_attn, scaled_two, g_own, g_pair, got_blocks, g_four)
+
+    arrived_w.append(send(shared_w[1], "y"))
     x_pair.append(send(x_own[0], "x"))
     g_pair.append(send(g_own[1], "x"))
     x_own.append(send(x_own[0], "z1"))
@@ -772,29 +784,27 @@
         for k in range(3)
     ]
 
-    arrived, shared_w, x_own, g_own, x_pair, g_pair, routed_w = sync(
-        arrived, shared_w, x_own, g_own, x_pair, g_pair, routed_w)
-    arrived.append(send(shared_w[half:], "y"))
+    shared_w, arrived_w, x_own, g_own, x_pair, g_pair, routed_w = sync(
+        shared_w, arrived_w, x_own, g_own, x_pair, g_pair, routed_w)
     x_pair.append(send(x_own[1], "x"))
-    g_pair.append(send(g_own[2], "x"))
     x_own.append(send(x_own[1], "z1"))
+    g_four.append(blocks_of(g_own[1], g_pair[1]))
     x_four = [blocks_of(x_own[0], x_pair[0])]
     behind = jnp.pad(router_rows, ((0, GRAD_TILE - sh_cols - experts - 1), (0, 0)))
-    arrived, shared_w, x_four, g_four, x_own, g_own, x_pair, g_pair, routed_w, behind = sync(
-        arrived, shared_w, x_four, g_four, x_own, g_own, x_pair, g_pair, routed_w, behind)
     rest_at = 3 * full_cols
     cuts = [
         [(k * full_cols, full_cols), (rest_at + k * rest_cols, rest_cols)] for k in range(3)
     ]
     y_place = y.reshape(1)
-    shared_w = join_shared(y_place, shared_w, arrived[0], arrived[1], behind, cuts)
+    places = jnp.stack([lax.rem(z + 4 - step, 4) * 2 + side for step in (0, 1, 3, 2) for side in range(2)] + [y])
+    shared_w = join_shared(places, shared_w, arrived_w, behind, cuts)
 
     expert = my_exp.reshape(1)
     fed, near_sums, sums, out_near, out_sums = [], [], [], [], []
 
     def core_sums(found):
-        arrived = send(found[2], "core").astype(F32)
-        return [found[0].astype(F32) + arrived[:own], found[1].astype(F32) + arrived[own:]]
+        arrived = send(found[2], "core")
+        return [found[0].astype(F32) + arrived[:own].astype(F32), found[1].astype(F32) + arrived[own:].astype(F32)]
 
     def pair_sums(parts):
         return parts[0] + send(parts[1].astype(BF), "x").astype(F32)
@@ -806,8 +816,8 @@
             x_pair.append(send(x_own[2], "x"))
             x_own.append(send(x_own[2], "z1"))
             g_own.append(send(g_own[2], "z1"))
+            g_pair.append(send(g_own[2], "x"))
             x_four.append(blocks_of(x_own[1], x_pair[1]))
-            g_four.append(blocks_of(g_own[1], g_pair[1]))
         if step == 1:
             x_pair.append(send(x_own[3], "x"))
             g_pair.append(send(g_own[3], "x"))
@@ -880,7 +890,10 @@
         far, near, low, out_sums, flying_out, shared_grads, ed_grad, x_blocks, routed_sets)
 
     def panel_sum(panel, gives, step):
-        return pick(panel, slot(step, 0)).astype(F32) + send(gives[step], "x").astype(F32)
+        return [pick(panel, slot(step, 0)), send(gives[step], "x")]
+
+    def two(parts):
+        return parts[0].astype(F32) + parts[1].astype(F32)
 
     shared_grads = swap_core(shared_grads)
     flying_out = send((out_sums[3] + flying_out.astype(F32)).astype(BF), "z1")
@@ -898,26 +911,35 @@
     hidden_out = (after_attn + out_sums[0] + flying_out.astype(F32)).astype(BF)
     e_got = [send(ed_grad[1], "y")]
     shared_z = {2: send(shared_far, "z2")}
-    wo_sums = {step: panel_sum(wo_part, wo_gives, step) for step in (1, 2)}
+    def wo_pair(first, second):
+        arrived = send(jnp.stack([wo_gives[first], wo_gives[second]]), "x")
+        for k, step in enumerate((first, second)):
+            wo_sums[step] = [pick(wo_part, slot(step, 0)), arrived[k]]
+
+    wo_sums = {}
+    wo_pair(1, 2)
     behind_rows = 8
     panel_shape = (n_exp, n_fsdp * rows_w + behind_rows, 3 * wide)
-    grad_lin, grad_normed_one, panel = attend(
+    grad_lin, grad_normed_one, gain_one_part, panel = attend(
         normed_seq, wqkv, bias, tables, seq, (keep, arrived, qkv_seq), core_place, panel_shape)
     shared_far = {k: pick(shared_grads, lax.rem(z + k, 4)) for k in (1, 3)}
-    (grad_lin, grad_normed_one, panel, hidden_out, e_got, shared_z, shared_far, shared_grads, wo_part, wo_gives,
+    shared_z[0] = pick(shared_grads, z)
+    give_x = pick(shared_z[0], 1 - x)
+    (grad_lin, grad_normed_one, gain_one_part, panel, hidden_out, e_got, shared_z, shared_far, give_x, wo_part, wo_gives,
      wo_sums, ed_grad, x_blocks, routed_sets) = sync(
-        grad_lin, grad_normed_one, panel, hidden_out, e_got, shared_z, shared_far, shared_grads, wo_part, wo_gives,
+        grad_lin, grad_normed_one, gain_one_part, panel, hidden_out, e_got, shared_z, shared_far, give_x, wo_part, wo_gives,
         wo_sums, ed_grad, x_blocks, routed_sets)
     parts = grad_normed_one.reshape(micro, 2, 2, tok, width)
     parts = parts[:, :, 0] + send(parts[:, :, 1].astype(BF), "core").astype(F32)
     near, last = parts[:, 0], parts[:, 1].astype(BF)
     e_got.append(send(ed_grad[2], "y"))
-    eg_grad = weight_grads(y_place, x_blocks, [routed_sets[1]], width, e_parts)
+    rest = ex_cols // 16 * 5 // 16 * 16
+    g_parts, u_parts = (ex_cols, ex_cols - rest, rest), (ex_cols, rest, ex_cols - rest)
+    eg_grad = weight_grads(y_place, x_blocks, [routed_sets[1]], width, g_parts)
     for k in (1, 3):
         shared_z[k] = send(shared_far[k], f"z{k}")
-    for step in (3, 0):
-        wo_sums[step] = panel_sum(wo_part, wo_gives, step)
-    gain_one_part = jnp.sum(grad_normed_one * normed_seq.astype(F32), axis=0) / gain_one
+    wo_pair(3, 0)
+    gain_one_part = gain_one_part[0] / gain_one
     bias_place = put(jnp.zeros((n_fsdp, 1, 3 * wide), F32), jnp.sum(grad_lin.astype(F32), axis=0)[None], my_fsdp)
     bias_place = from_fsdp(bias_place)[:, 0]
     small_part = jnp.concatenate([router_part, gain_one_part[None], gain_two_part[None], bias_place], axis=0)
@@ -927,47 +949,55 @@
     panel = lax.dynamic_update_slice_in_dim(
         panel, small_part.reshape(n_exp, behind_rows, 3 * wide), n_fsdp * rows_w, 1)
     gives = [pick(panel, slot(step, 1)) for step in range(4)]
-    gives, panel, last, near, e_got, shared_z, shared_grads, wo_sums, eg_grad, x_blocks, routed_sets = sync(
-        gives, panel, last, near, e_got, shared_z, shared_grads, wo_sums, eg_grad, x_blocks, routed_sets)
+    (gives, panel, last, near, e_got, shared_z, give_x, wo_sums, wo_part, wo_gives, eg_grad, x_blocks,
+     routed_sets) = sync(gives, panel, last, near, e_got, shared_z, give_x, wo_sums, wo_part, wo_gives, eg_grad,
+                         x_blocks, routed_sets)
 
     far = send(last, "y")
-    eu_grad = weight_grads(y_place, x_blocks, [routed_sets[2]], width, e_parts)
+    eu_grad = weight_grads(y_place, x_blocks, [routed_sets[2]], width, u_parts)
     e_grads = (eg_grad, eu_grad, ed_grad)
-    for k in (1, 2, 3):
-        shared_grads = put(shared_grads, shared_z[k], lax.rem(z + 4 - k, 4))
-    shared_mine, shared_give = pick(shared_grads, x, 1), pick(shared_grads, 1 - x, 1)
     shared_x, sums = [], {}
 
     for turn, step in enumerate((1, 2, 3, 0)):
         sums[step] = panel_sum(panel, gives, step)
-        shared_x.append(send(shared_give[turn], "x"))
-        e_got.append(send(e_grads[turn // 2][1 + turn % 2], "y"))
+        shared_x.append(send(give_x, "x"))
+        if turn < 3:
+            give_x = pick(shared_z[turn + 1], 1 - x)
+        if turn:
+            e_got.append(send(e_gives[turn - 1], "y"))
         if turn == 0:
-            flying_wo = send(wo_sums[1].astype(BF), "z1")
-            (far, near, sums, e_got, shared_x, shared_give, shared_mine, e_grads, panel, gives, flying_wo,
-             wo_sums) = sync(far, near, sums, e_got, shared_x, shared_give, shared_mine, e_grads, panel, gives,
+            flying_wo = send(two(wo_sums[1]).astype(BF), "z1")
+            e_gives = [eg_grad[1], jnp.concatenate([eg_grad[2], eu_grad[1]]), eu_grad[2]]
+            (far, near, sums, e_got, shared_x, give_x, shared_z, e_grads, e_gives, panel, gives, flying_wo,
+             wo_sums) = sync(far, near, sums, e_got, shared_x, give_x, shared_z, e_grads, e_gives, panel, gives,
                              flying_wo, wo_sums)
             continue
         if turn == 1:
             routed_grads = {2: ed_grad[0].astype(F32) + jnp.concatenate(e_got[:2]).astype(F32)}
-            flying = send(sums[1].astype(BF), "z1")
+            flying = send(two(sums[1]).astype(BF), "z1")
             grad_normed_one = (near + far.astype(F32)).reshape(own, width)
             in_grad = grad_after + norm_back(grad_normed_one, scaled_one, inverse_one, gain_one)
         else:
-            flying = send((sums[turn] + flying.astype(F32)).astype(BF), "z1")
-        if turn == 2:
-            routed_grads[0] = (eg_grad[0].astype(F32) + jnp.concatenate(e_got[2:4]).astype(F32)).T
+            flying = send((two(sums[turn]) + flying.astype(F32)).astype(BF), "z1")
+        if turn == 3:
+            rest = eg_grad[2].shape[0]
+            got_g, got_u = e_got[3][:rest], e_got[3][rest:]
+            routed_grads[0] = (eg_grad[0].astype(F32) + jnp.concatenate([e_got[2], got_g]).astype(F32)).T
         if turn < 3:
-            flying_wo = send((wo_sums[turn + 1] + flying_wo.astype(F32)).astype(BF), "z1")
-            sums, e_got, shared_x, shared_give, flying, e_grads, panel, gives, flying_wo, in_grad, routed_grads = sync(
-                sums, e_got, shared_x, shared_give, flying, e_grads, panel, gives, flying_wo, in_grad, routed_grads)
+            flying_wo = send((two(wo_sums[turn + 1]) + flying_wo.astype(F32)).astype(BF), "z1")
+            (sums, e_got, shared_x, give_x, shared_z, flying, e_grads, e_gives, panel, gives, flying_wo, in_grad,
+             routed_grads, wo_part, wo_gives) = sync(
+                sums, e_got, shared_x, give_x, shared_z, flying, e_grads, e_gives, panel, gives, flying_wo, in_grad,
+                routed_grads, wo_part, wo_gives)
         else:
-            out_own = wo_sums[0] + flying_wo.astype(F32)
+            out_own = two(wo_sums[0]) + flying_wo.astype(F32)
             flying, sums, out_own, e_got, shared_x = sync(flying, sums, out_own, e_got, shared_x)
-    shared_grads = in_order(shared_mine, jnp.stack(shared_x), x, 1).reshape(16, rows_w, unit_cols)
-    shared_own = unpack_shared(shared_grads, full_cols, rest_cols)
-    routed_grads[1] = (eu_grad[0].astype(F32) + jnp.concatenate(e_got[4:6]).astype(F32)).T
-    total = (sums[0] + flying.astype(F32)).astype(BF)
+    shared_blocks = jnp.stack([in_order(pick(shared_z[k], x), shared_x[k], x, 0) for k in range(4)])
+    places = (lax.rem(z + 4 - jnp.arange(4), 4)[:, None] * 4 + jnp.arange(4)[None]).reshape(16)
+    shared_own = unpack_shared(
+        shared_blocks.reshape(16, rows_w, unit_cols), places.astype(jnp.int32), full_cols, rest_cols)
+    routed_grads[1] = (eu_grad[0].astype(F32) + jnp.concatenate([got_u, e_got[4]]).astype(F32)).T
+    total = (two(sums[0]) + flying.astype(F32)).astype(BF)
 
     count = n_fsdp * rows_w
     small_sum = total[count:].reshape(-1)[: n_fsdp * n_small * rows_w].reshape(n_fsdp, n_small * rows_w)
@@ -1138,8 +1168,8 @@
     gain_two_part = jnp.sum(grad_normed_two * scaled_two, axis=0)
 
     grad_attn = links.gather_seq(grad_after.astype(BF).reshape(micro, tok, width)).reshape(micro * seq, width)
-    grad_lin, grad_normed_one = attend(normed_seq, wqkv, bias, tables, seq, (grad_attn, wo, qkv_seq))
-    gain_one_part = jnp.sum(grad_normed_one * normed_seq.astype(F32), axis=0) / gain_one
+    grad_lin, grad_normed_one, gain_one_part = attend(normed_seq, wqkv, bias, tables, seq, (grad_attn, wo, qkv_seq))
+    gain_one_part = gain_one_part[0] / gain_one
     grad_normed_one = grad_normed_one.reshape(micro, n_fsdp, tok, width)
     grad_normed_one = links.sum_four([grad_normed_one[:, k] for k in range(4)]).reshape(own, width)
     in_grad = grad_after + norm_back(grad_normed_one, scaled_one, inverse_one, gain_one)

time: 769 us -> 718 us (0.934)
  waiting for transfers between devices: 261 us -> 214 us
  Pallas kernels: 166 us -> 186 us
  local copies, waits for them, and re-layouts: 115 us -> 104 us
  other arithmetic: 103 us -> 93.6 us
    ppermute x119 -> x117, waiting for transfers between devices: 261 us -> 214 us  [send(): return lax.ppermute(value, ALL, ring_perm(MOVES[link]))]
    unnamed x425 -> x291, local copies, waits for them, and re-layouts: 40.9 us -> 15.1 us
    pallas_call x5, Pallas kernels: 43.6 us -> 64 us  [weight_grads(): pl.pallas_call(functools.partial(weights_kernel, n_sets, split), grid=(n_...]
    squeeze x9 -> x21, local copies, waits for them, and re-layouts: 9.02 us -> 19.3 us  [pick(): return lax.dynamic_index_in_dim(value, place, axis, keepdims=False)]
    add x24 -> x18, other arithmetic: 21.7 us -> 14.5 us  [the longest x8 7.03 us: core_sums(): found[0].astype(F32) + arrived[:own].astype(F32)]
    ppermute x119 -> x117, starting transfers between devices: 101 us -> 98 us  [send(): return lax.ppermute(value, ALL, ring_perm(MOVES[link]))]
    dynamic_update_slice x20 -> x15, local copies, waits for them, and re-layouts: 17.8 us -> 20 us  [put(): return lax.dynamic_update_index_in_dim(value, block, place, axis)]
  transfers between devices with their start and end apart: 119 -> 117, of which waited for: 44 -> 38; matrix products, arithmetic and copies ran while one was open for 20% -> 22% of each run, Pallas kernels for 22% -> 26%
where the time goes in v4:
time: 718 us; the launch traced here: 709 us
  waiting for transfers between devices  214 us (30%)
  Pallas kernels  186 us (26%)
  local copies, waits for them, and re-layouts  104 us (14%)
  starting transfers between devices  98 us (14%)
  other arithmetic  93.6 us (13%)
  matrix products  8.6 us (1%)
    ppermute x117, waiting for transfers between devices, send(): return lax.ppermute(value, ALL, ring_perm(MOVES[link]))  214 us
    ppermute x117, starting transfers between devices, send(): return lax.ppermute(value, ALL, ring_perm(MOVES[link]))  98 us
    pallas_call x4, Pallas kernels, feed(): pl.pallas_call(functools.partial(feed_kernel, experts, shared), in_specs=...  88.3 us
    pallas_call x5, Pallas kernels, weight_grads(): pl.pallas_call(functools.partial(weights_kernel, n_sets, split), grid=(n_...  64 us
    dynamic_update_slice x15, local copies, waits for them, and re-layouts, put(): return lax.dynamic_update_index_in_dim(value, block, place, axis)  20 us
    squeeze x21, local copies, waits for them, and re-layouts, pick(): return lax.dynamic_index_in_dim(value, place, axis, keepdims=False)  19.3 us
    pallas_call x1, Pallas kernels, attend(): pl.pallas_call(functools.partial(attend_back_kernel, heads, seq, scale, s...  18.7 us
    unnamed x291, local copies, waits for them, and re-layouts  15.1 us
  transfers between devices with their start and end apart: 117, of which 38 were waited for; matrix products, arithmetic and copies ran while one was open for 22% of the time, Pallas kernels for 26%

profile of v4, /device:TPU:0, one launch (start us, length us, event | category | flops | bytes accessed | tf_op | source)
XLA Modules:
  0.0 708.8 jit_solution(1323259236855748028)
XLA Ops:
  39.8 17.9 %collective-permute-done.6 = bf16[256,2048]{1,0:T(8,128)(2,1)} collective-permute-done((bf16[256,2048]{1,0:T(8,128)(2,1)S(1)}, bf16[256,2048]{1,0:T(8,128)(2,1)}, u32[]{:S(2)}, u32[]{:S(2)}) %collective-permute-start.6) | collective-permute-done | bytes 1048608 | tf_op jit(solution)/shard_map/ppermute | solution.py:571
  71.1 11.0 %collective-permute-done.12 = bf16[256,2048]{1,0:T(8,128)(2,1)} collective-permute-done((bf16[256,2048]{1,0:T(8,128)(2,1)}, bf16[256,2048]{1,0:T(8,128)(2,1)}, u32[]{:S(2)}, u32[]{:S(2)}) %collective-permute-start.12) | collective-permute-done | bytes 1048608 | tf_op jit(solution)/shard_map/ppermute | solution.py:571
  116.5 7.4 %collective-permute-done.23 = bf16[2,2,64,1056]{3,2,1,0:T(8,128)(2,1)S(1)} collective-permute-done((bf16[2,2,64,1056]{3,2,1,0:T(8,128)(2,1)S(1)}, bf16[2,2,64,1056]{3,2,1,0:T(8,128)(2,1)S(1)}, u32[]{:S(2)}, u32[]{:S(2)}) %collective-permute-start.23) | collective-permute-done | bytes 540704 | tf_op jit(solution)/shard_map/ppermute | solution.py:571
  123.8 9.8 %collective-permute-done.24 = bf16[2,2,64,1056]{3,2,1,0:T(8,128)(2,1)S(1)} collective-permute-done((bf16[2,2,64,1056]{3,2,1,0:T(8,128)(2,1)S(1)}, bf16[2,2,64,1056]{3,2,1,0:T(8,128)(2,1)S(1)}, u32[]{:S(2)}, u32[]{:S(2)}) %collective-permute-start.24) | collective-permute-done | bytes 540704 | tf_op jit(solution)/shard_map/ppermute | solution.py:571
  142.5 8.9 %attend.1 = (bf16[512,1536]{1,0:T(8,128)(2,1)S(1)}, bf16[512,256]{1,0:T(8,128)(2,1)S(1)}, bf16[512,256]{1,0:T(8,128)(2,1)S(1)}) custom-call(bf16[512,2048]{1,0:T(8,128)(2,1)S(1)} %bitcast.329, bf16[2048,2048]{1,0:T(8,128)(2,1)} %bitcast.75.w_ref, f32[1,1536]{1,0:T(1,128)S(1)} %fusion.46.bias_ref, f32[256,128]{1,0:T(8,128)S(1)} %get-tuple-element.878.cos_ref, ...), custom_call_target="tpu_custom_call" | custom-call | flops 100000000 | bytes 1000000 | tf_op jit(solution)/shard_map/attend/pallas_call | solution.py:215
  157.9 7.3 %collective-permute-done.28.refs_4_.refs_1_ = bf16[128,2176]{1,0:T(8,128)(2,1)S(1)} collective-permute-done((bf16[128,2176]{1,0:T(8,128)(2,1)}, bf16[128,2176]{1,0:T(8,128)(2,1)S(1)}, u32[]{:S(2)}, u32[]{:S(2)}) %collective-permute-start.28) | collective-permute-done | bytes 557088 | tf_op jit(solution)/shard_map/ppermute | solution.py:571
  180.9 9.5 %collective-permute-done.31 = bf16[2,64,1056]{2,1,0:T(8,128)(2,1)S(1)} collective-permute-done((bf16[2,64,1056]{2,1,0:T(8,128)(2,1)S(1)}, bf16[2,64,1056]{2,1,0:T(8,128)(2,1)S(1)}, u32[]{:S(2)}, u32[]{:S(2)}) %collective-permute-start.31) | collective-permute-done | bytes 270368 | tf_op jit(solution)/shard_map/ppermute | solution.py:571
  190.3 12.9 %collective-permute-done.33.refs_2_ = bf16[1056,512]{1,0:T(8,128)(2,1)S(1)} collective-permute-done((bf16[1056,512]{1,0:T(8,128)(2,1)S(1)}, bf16[1056,512]{1,0:T(8,128)(2,1)S(1)}, u32[]{:S(2)}, u32[]{:S(2)}) %collective-permute-start.33) | collective-permute-done | bytes 1081376 | tf_op jit(solution)/shard_map/ppermute | solution.py:571
  240.1 8.6 %collective-permute-done.40.refs_3_.refs_6_ = bf16[128,2176]{1,0:T(8,128)(2,1)S(1)} collective-permute-done((bf16[128,2176]{1,0:T(8,128)(2,1)}, bf16[128,2176]{1,0:T(8,128)(2,1)S(1)}, u32[]{:S(2)}, u32[]{:S(2)}) %collective-permute-start.40) | collective-permute-done | bytes 557088 | tf_op jit(solution)/shard_map/ppermute | solution.py:571
  260.8 8.1 %collective-permute-done.45.refs_0_.refs_6_ = bf16[128,2048]{1,0:T(8,128)(2,1)} collective-permute-done((bf16[128,2048]{1,0:T(8,128)(2,1)S(1)}, bf16[128,2048]{1,0:T(8,128)(2,1)}, u32[]{:S(2)}, u32[]{:S(2)}) %collective-permute-start.45) | collective-permute-done | bytes 524320 | tf_op jit(solution)/shard_map/ppermute | solution.py:571
  276.9 22.0 %feed.4 = (bf16[512,384]{1,0:T(8,128)(2,1)}, bf16[512,384]{1,0:T(8,128)(2,1)}, bf16[512,384]{1,0:T(8,128)(2,1)}, bf16[512,768]{1,0:T(8,128)(2,1)}, bf16[512,768]...) custom-call(s32[1]{0:T(128)} %bitcast.117.expert_ref, ...), custom_call_target="tpu_custom_call" | custom-call | flops 16000000000 | bytes 30000000 | tf_op jit(solution)/shard_map/feed/pallas_call | solution.py:326
  303.8 22.0 %feed.5 = (bf16[512,384]{1,0:T(8,128)(2,1)}, bf16[512,384]{1,0:T(8,128)(2,1)}, bf16[512,384]{1,0:T(8,128)(2,1)}, bf16[512,768]{1,0:T(8,128)(2,1)}, bf16[512,768]...) custom-call(s32[1]{0:T(128)} %bitcast.117.expert_ref, ...), custom_call_target="tpu_custom_call" | custom-call | flops 16000000000 | bytes 30000000 | tf_op jit(solution)/shard_map/feed/pallas_call | solution.py:326
  331.6 22.3 %feed.6 = (bf16[512,384]{1,0:T(8,128)(2,1)}, bf16[512,384]{1,0:T(8,128)(2,1)}, bf16[512,384]{1,0:T(8,128)(2,1)}, bf16[512,768]{1,0:T(8,128)(2,1)}, bf16[512,768]...) custom-call(s32[1]{0:T(128)} %bitcast.117.expert_ref, ...), custom_call_target="tpu_custom_call" | custom-call | flops 16000000000 | bytes 30000000 | tf_op jit(solution)/shard_map/feed/pallas_call | solution.py:326
  359.3 22.0 %feed.7 = (bf16[512,384]{1,0:T(8,128)(2,1)}, bf16[512,384]{1,0:T(8,128)(2,1)}, bf16[512,384]{1,0:T(8,128)(2,1)}, bf16[512,768]{1,0:T(8,128)(2,1)}, bf16[512,768]...) custom-call(s32[1]{0:T(128)} %bitcast.117.expert_ref, ...), custom_call_target="tpu_custom_call" | custom-call | flops 16000000000 | bytes 30000000 | tf_op jit(solution)/shard_map/feed/pallas_call | solution.py:326
  391.3 13.3 %weight_grads.5 = (bf16[384,1024]{1,0:T(8,128)(2,1)}, bf16[384,1024]{1,0:T(8,128)(2,1)}, bf16[384,1024]{1,0:T(8,128)(2,1)}, bf16[384,1024]{1,0:T(8,128)(2,1)}) custom-call(s32[1]{0:T(128)} %bitcast.105.y_ref, bf16[128,2048]{1,0:T(8,128)(2,1)} %copy-done.34, bf16[128,2048]{1,0:T(8,128)(2,1)} %copy-done.112, ...), custom_call_target="tpu_custom_call" | custom-call | flops 8000000000 | bytes 20000000 | tf_op jit(solution)/shard_map/weight_grads/pallas_call | solution.py:502
  418.6 9.5 %weight_grads.6 = (bf16[384,1024]{1,0:T(8,128)(2,1)}, bf16[384,1024]{1,0:T(8,128)(2,1)}) custom-call(s32[1]{0:T(128)} %bitcast.105.y_ref, bf16[128,2176]{1,0:T(8,128)(2,1)} %fusion.26.refs_3_.refs_0_, bf16[128,2176]{1,0:T(8,128)(2,1)} %copy-done.91, bf16[256,2176]{1,0:T(8,128)(2,1)} %collective-permute-done.37.refs_5_.refs_2_, ...), custom_call_target="tpu_custom_call" | custom-call | flops 4000000000 | bytes 20000000 | tf_op jit(solution)/shard_map/weight_grads/pallas_call | solution.py:502
  441.0 13.8 %weight_grads.7 = (bf16[352,2048]{1,0:T(8,128)(2,1)}, bf16[176,2048]{1,0:T(8,128)(2,1)}, bf16[176,2048]{1,0:T(8,128)(2,1)}) custom-call(s32[1]{0:T(128)} %bitcast.105.y_ref, bf16[128,2176]{1,0:T(8,128)(2,1)} %fusion.26.refs_3_.refs_0_, bf16[128,2176]{1,0:T(8,128)(2,1)} %copy-done.91, bf16[256,2176]{1,0:T(8,128)(2,1)} %collective-permute-done.37.refs_5_.refs_2_, ...), custom_call_target="tpu_custom_call" | custom-call | flops 8000000000 | bytes 20000000 | tf_op jit(solution)/shard_map/weight_grads/pallas_call | solution.py:502
  507.7 9.6 %collective-permute-done.87 = bf16[128,2048]{1,0:T(8,128)(2,1)S(1)} collective-permute-done((bf16[128,2048]{1,0:T(8,128)(2,1)S(1)}, bf16[128,2048]{1,0:T(8,128)(2,1)S(1)}, u32[]{:S(2)}, u32[]{:S(2)}) %collective-permute-start.87) | collective-permute-done | bytes 524320 | tf_op jit(solution)/shard_map/ppermute | solution.py:571
  523.1 18.7 %attend_back.1 = (bf16[512,1536]{1,0:T(8,128)(2,1)S(1)}, f32[512,2048]{1,0:T(8,128)}, f32[1,2048]{1,0:T(1,128)S(1)}, bf16[8,264,1536]{2,1,0:T(8,128)(2,1)}) custom-call(bf16[512,256]{1,0:T(8,128)(2,1)S(1)} %get-tuple-element.1436.grad_ref, bf16[512,256]{1,0:T(8,128)(2,1)S(1)} %bitcast.338, bf16[512,1536]{1,0:T(8,128)(2,1)S(1)} %copy-done.7, ...), custom_call_target="tpu_custom_call" | custom-call | flops 100000000 | bytes 1000000 | tf_op jit(solution)/shard_map/attend_back/pallas_call | solution.py:231
  559.6 13.7 %weight_grads.8 = (bf16[352,2048]{1,0:T(8,128)(2,1)}, bf16[256,2048]{1,0:T(8,128)(2,1)}, bf16[96,2048]{1,0:T(8,128)(2,1)}) custom-call(s32[1]{0:T(128)} %bitcast.105.y_ref, bf16[128,2048]{1,0:T(8,128)(2,1)} %copy-done.34, bf16[128,2048]{1,0:T(8,128)(2,1)} %copy-done.112, bf16[256,2048]{1,0:T(8,128)(2,1)} %collective-permute-done.43.refs_2_, ...), custom_call_target="tpu_custom_call" | custom-call | flops 8000000000 | bytes 20000000 | tf_op jit(solution)/shard_map/weight_grads/pallas_call | solution.py:502
  585.2 13.7 %weight_grads.9 = (bf16[352,2048]{1,0:T(8,128)(2,1)}, bf16[96,2048]{1,0:T(8,128)(2,1)}, bf16[256,2048]{1,0:T(8,128)(2,1)}) custom-call(s32[1]{0:T(128)} %bitcast.105.y_ref, bf16[128,2048]{1,0:T(8,128)(2,1)} %copy-done.34, bf16[128,2048]{1,0:T(8,128)(2,1)} %copy-done.112, bf16[256,2048]{1,0:T(8,128)(2,1)} %collective-permute-done.43.refs_2_, ...), custom_call_target="tpu_custom_call" | custom-call | flops 8000000000 | bytes 20000000 | tf_op jit(solution)/shard_map/weight_grads/pallas_call | solution.py:502
  622.5 14.1 %collective-permute-done.104 = bf16[64,2048]{1,0:T(8,128)(2,1)} collective-permute-done((bf16[64,2048]{1,0:T(8,128)(2,1)}, bf16[64,2048]{1,0:T(8,128)(2,1)}, u32[]{:S(2)}, u32[]{:S(2)}) %collective-permute-start.104) | collective-permute-done | bytes 262176 | tf_op jit(solution)/shard_map/ppermute | solution.py:571
  645.0 19.7 %collective-permute-done.109 = bf16[64,2048]{1,0:T(8,128)(2,1)S(1)} collective-permute-done((bf16[64,2048]{1,0:T(8,128)(2,1)S(1)}, bf16[64,2048]{1,0:T(8,128)(2,1)S(1)}, u32[]{:S(2)}, u32[]{:S(2)}) %collective-permute-start.109) | collective-permute-done | bytes 262176 | tf_op jit(solution)/shard_map/ppermute | solution.py:571
  675.5 10.6 %collective-permute-done.113 = bf16[2,64,1056]{2,1,0:T(8,128)(2,1)S(1)} collective-permute-done((bf16[2,64,1056]{2,1,0:T(8,128)(2,1)S(1)}, bf16[2,64,1056]{2,1,0:T(8,128)(2,1)S(1)}, u32[]{:S(2)}, u32[]{:S(2)}) %collective-permute-start.113) | collective-permute-done | bytes 270368 | tf_op jit(solution)/shard_map/ppermute | solution.py:571
  (796 shorter events, 378.6 us)
Async XLA Ops:
  103.9 29.7 %collective-permute-start.21 = (bf16[256,2048]{1,0:T(8,128)(2,1)}, bf16[256,2048]{1,0:T(8,128)(2,1)S(1)}, u32[]{:S(2)}, u32[]{:S(2)}) collective-permute-start(bf16[256,2048]{1,0:T(8,128)(2,1)} %collective-permute-done.16), channel_id=1, source_target_pairs={{0,4},{1,5},{2,6},{3,7},{4,0},{5,1},{6,2},{7,3},{8,12},{9,13},{10,... | collective-permute-start | bytes 3145736 | tf_op jit(solution)/shard_map/ppermute | solution.py:571
  105.2 28.4 %collective-permute-start.22 = (bf16[264,2048]{1,0:T(8,128)(2,1)S(1)}, bf16[264,2048]{1,0:T(8,128)(2,1)S(1)}, u32[]{:S(2)}, u32[]{:S(2)}) collective-permute-start(bf16[264,2048]{1,0:T(8,128)(2,1)S(1)} %copy-done.63), channel_id=1, source_target_pairs={{0,2},{1,3},{2,0},{3,1},{4,6},{5,7},{6,4},{7,5},{8,10},{9,11},{10,... | collective-permute-start | bytes 3244040 | tf_op jit(solution)/shard_map/ppermute | solution.py:571
  133.7 31.5 %collective-permute-start.25 = (bf16[264,2048]{1,0:T(8,128)(2,1)}, bf16[264,2048]{1,0:T(8,128)(2,1)}, u32[]{:S(2)}, u32[]{:S(2)}) collective-permute-start(bf16[264,2048]{1,0:T(8,128)(2,1)} %get-tuple-element.869), channel_id=1, source_target_pairs={{0,2},{1,3},{2,0},{3,1},{4,6},{5,7},{6,4},{7,5},{8,10},{9,11},{10,... | collective-permute-start | bytes 3244040 | tf_op jit(solution)/shard_map/ppermute | solution.py:571
  269.3 29.6 %collective-permute-start.48 = (bf16[128,2048]{1,0:T(8,128)(2,1)}, bf16[128,2048]{1,0:T(8,128)(2,1)}, u32[]{:S(2)}, u32[]{:S(2)}) collective-permute-start(bf16[128,2048]{1,0:T(8,128)(2,1)} %collective-permute-done.45.refs_0_.refs_6_), channel_id=1, source_target_pairs={{0,8},{1,9},{2,10},{3,11},{4,12},{5,13},{6,14},{7,15},{8,16},{9,17... | collective-permute-start | bytes 1572872 | tf_op jit(solution)/shard_map/ppermute | solution.py:571
  270.7 28.2 %collective-permute-start.50 = (bf16[128,2048]{1,0:T(8,128)(2,1)}, bf16[128,2048]{1,0:T(8,128)(2,1)S(1)}, u32[]{:S(2)}, u32[]{:S(2)}) collective-permute-start(bf16[128,2048]{1,0:T(8,128)(2,1)} %collective-permute-done.45.refs_0_.refs_6_), channel_id=1, source_target_pairs={{0,4},{1,5},{2,6},{3,7},{4,0},{5,1},{6,2},{7,3},{8,12},{9,13},{10,... | collective-permute-start | bytes 1572872 | tf_op jit(solution)/shard_map/ppermute | solution.py:571
  271.9 27.1 %collective-permute-start.49 = (bf16[128,2176]{1,0:T(8,128)(2,1)}, bf16[128,2176]{1,0:T(8,128)(2,1)S(1)}, u32[]{:S(2)}, u32[]{:S(2)}) collective-permute-start(bf16[128,2176]{1,0:T(8,128)(2,1)} %copy-done.93), channel_id=1, source_target_pairs={{0,8},{1,9},{2,10},{3,11},{4,12},{5,13},{6,14},{7,15},{8,16},{9,17... | collective-permute-start | bytes 1671176 | tf_op jit(solution)/shard_map/ppermute | solution.py:571
  300.9 27.2 %collective-permute-start.52 = (bf16[256,2048]{1,0:T(8,128)(2,1)S(1)}, bf16[256,2048]{1,0:T(8,128)(2,1)}, u32[]{:S(2)}, u32[]{:S(2)}) collective-permute-start(bf16[256,2048]{1,0:T(8,128)(2,1)S(1)} %pad_maximum_fusion.15), channel_id=1, source_target_pairs={{0,1},{1,0},{2,3},{3,2},{4,5},{5,4},{6,7},{7,6},{8,9},{9,8},{10,11... | collective-permute-start | bytes 3145736 | tf_op jit(solution)/shard_map/ppermute | solution.py:571
  301.6 26.6 %collective-permute-start.53 = (bf16[256,2176]{1,0:T(8,128)(2,1)S(1)}, bf16[256,2176]{1,0:T(8,128)(2,1)}, u32[]{:S(2)}, u32[]{:S(2)}) collective-permute-start(bf16[256,2176]{1,0:T(8,128)(2,1)S(1)} %pad_maximum_fusion.11), channel_id=1, source_target_pairs={{0,1},{1,0},{2,3},{3,2},{4,5},{5,4},{6,7},{7,6},{8,9},{9,8},{10,11... | collective-permute-start | bytes 3342344 | tf_op jit(solution)/shard_map/ppermute | solution.py:571
  329.5 27.2 %collective-permute-start.57 = (bf16[256,2048]{1,0:T(8,128)(2,1)S(1)}, bf16[256,2048]{1,0:T(8,128)(2,1)}, u32[]{:S(2)}, u32[]{:S(2)}) collective-permute-start(bf16[256,2048]{1,0:T(8,128)(2,1)S(1)} %pad_maximum_fusion.16), channel_id=1, source_target_pairs={{0,1},{1,0},{2,3},{3,2},{4,5},{5,4},{6,7},{7,6},{8,9},{9,8},{10,11... | collective-permute-start | bytes 3145736 | tf_op jit(solution)/shard_map/ppermute | solution.py:571
  330.0 26.7 %collective-permute-start.58 = (bf16[256,2176]{1,0:T(8,128)(2,1)S(1)}, bf16[256,2176]{1,0:T(8,128)(2,1)}, u32[]{:S(2)}, u32[]{:S(2)}) collective-permute-start(bf16[256,2176]{1,0:T(8,128)(2,1)S(1)} %pad_maximum_fusion.12), channel_id=1, source_target_pairs={{0,1},{1,0},{2,3},{3,2},{4,5},{5,4},{6,7},{7,6},{8,9},{9,8},{10,11... | collective-permute-start | bytes 3342344 | tf_op jit(solution)/shard_map/ppermute | solution.py:571
  356.8 29.7 %collective-permute-start.62 = (bf16[256,2176]{1,0:T(8,128)(2,1)}, bf16[256,2176]{1,0:T(8,128)(2,1)S(1)}, u32[]{:S(2)}, u32[]{:S(2)}) collective-permute-start(bf16[256,2176]{1,0:T(8,128)(2,1)} %get-tuple-element.1096), channel_id=1, source_target_pairs={{0,1},{1,0},{2,3},{3,2},{4,5},{5,4},{6,7},{7,6},{8,9},{9,8},{10,11... | collective-permute-start | bytes 3342344 | tf_op jit(solution)/shard_map/ppermute | solution.py:571
  357.3 26.9 %collective-permute-start.63 = (bf16[128,2176]{1,0:T(8,128)(2,1)S(1)}, bf16[128,2176]{1,0:T(8,128)(2,1)S(1)}, u32[]{:S(2)}, u32[]{:S(2)}) collective-permute-start(bf16[128,2176]{1,0:T(8,128)(2,1)S(1)} %convert_add_fusion.10), channel_id=1, source_target_pairs={{0,4},{1,5},{2,6},{3,7},{4,0},{5,1},{6,2},{7,3},{8,12},{9,13},{10,... | collective-permute-start | bytes 1671176 | tf_op jit(solution)/shard_map/ppermute | solution.py:571
  358.3 26.9 %collective-permute-start.64 = (bf16[256,2048]{1,0:T(8,128)(2,1)}, bf16[256,2048]{1,0:T(8,128)(2,1)S(1)}, u32[]{:S(2)}, u32[]{:S(2)}) collective-permute-start(bf16[256,2048]{1,0:T(8,128)(2,1)} %get-tuple-element.1113), channel_id=1, source_target_pairs={{0,1},{1,0},{2,3},{3,2},{4,5},{5,4},{6,7},{7,6},{8,9},{9,8},{10,11... | collective-permute-start | bytes 3145736 | tf_op jit(solution)/shard_map/ppermute | solution.py:571
  517.3 30.6 %collective-permute-start.88 = (bf16[176,2048]{1,0:T(8,128)(2,1)S(1)}, bf16[176,2048]{1,0:T(8,128)(2,1)S(1)}, u32[]{:S(2)}, u32[]{:S(2)}) collective-permute-start(bf16[176,2048]{1,0:T(8,128)(2,1)S(1)} %copy-done.141), channel_id=1, source_target_pairs={{0,2},{1,3},{2,0},{3,1},{4,6},{5,7},{6,4},{7,5},{8,10},{9,11},{10,... | collective-permute-start | bytes 2162696 | tf_op jit(solution)/shard_map/ppermute | solution.py:571
  551.4 27.9 %collective-permute-start.91 = (bf16[2,2,64,2048]{3,2,0,1:T(8,128)(2,1)S(1)}, bf16[2,2,64,2048]{3,2,0,1:T(8,128)(2,1)S(1)}, u32[]{:S(2)}, u32[]{:S(2)}) collective-permute-start(bf16[2,2,64,2048]{3,2,0,1:T(8,128)(2,1)S(1)} %fusion.13), channel_id=1, source_target_pairs={{0,1},{1,0},{2,3},{3,2},{4,5},{5,4},{6,7},{7,6},{8,9},{9,8},{10,11... | collective-permute-start | bytes 3145736 | tf_op jit(solution)/shard_map/ppermute | solution.py:571
  551.5 29.5 %collective-permute-start.92 = (bf16[176,2048]{1,0:T(8,128)(2,1)}, bf16[176,2048]{1,0:T(8,128)(2,1)S(1)}, u32[]{:S(2)}, u32[]{:S(2)}) collective-permute-start(bf16[176,2048]{1,0:T(8,128)(2,1)} %get-tuple-element.1485), channel_id=1, source_target_pairs={{0,2},{1,3},{2,0},{3,1},{4,6},{5,7},{6,4},{7,5},{8,10},{9,11},{10,... | collective-permute-start | bytes 2162696 | tf_op jit(solution)/shard_map/ppermute | solution.py:571
  552.5 27.2 %collective-permute-start.93 = (bf16[2,2,64,1056]{3,2,1,0:T(8,128)(2,1)}, bf16[2,2,64,1056]{3,2,1,0:T(8,128)(2,1)S(1)}, u32[]{:S(2)}, u32[]{:S(2)}) collective-permute-start(bf16[2,2,64,1056]{3,2,1,0:T(8,128)(2,1)} %get-tuple-element.1487), channel_id=1, source_target_pairs={{0,8},{1,9},{2,10},{3,11},{4,12},{5,13},{6,14},{7,15},{8,16},{9,17... | collective-permute-start | bytes 1622024 | tf_op jit(solution)/shard_map/ppermute | solution.py:571
  552.6 28.4 %collective-permute-start.94 = (bf16[2,2,64,1056]{3,2,1,0:T(8,128)(2,1)}, bf16[2,2,64,1056]{3,2,1,0:T(8,128)(2,1)S(1)}, u32[]{:S(2)}, u32[]{:S(2)}) collective-permute-start(bf16[2,2,64,1056]{3,2,1,0:T(8,128)(2,1)} %get-tuple-element.1489), channel_id=1, source_target_pairs={{0,24},{1,25},{2,26},{3,27},{4,28},{5,29},{6,30},{7,31},{8,0},{9,1... | collective-permute-start | bytes 1622024 | tf_op jit(solution)/shard_map/ppermute | solution.py:571
  581.0 26.5 %collective-permute-start.96 = (bf16[2,64,2048]{2,1,0:T(8,128)(2,1)S(1)}, bf16[2,64,2048]{2,1,0:T(8,128)(2,1)}, u32[]{:S(2)}, u32[]{:S(2)}) collective-permute-start(bf16[2,64,2048]{2,1,0:T(8,128)(2,1)S(1)} %fusion.28), channel_id=1, source_target_pairs={{0,2},{1,3},{2,0},{3,1},{4,6},{5,7},{6,4},{7,5},{8,10},{9,11},{10,... | collective-permute-start | bytes 1572872 | tf_op jit(solution)/shard_map/ppermute | solution.py:571
  607.5 29.1 %collective-permute-start.100 = (bf16[264,1536]{1,0:T(8,128)(2,1)}, bf16[264,1536]{1,0:T(8,128)(2,1)}, u32[]{:S(2)}, u32[]{:S(2)}) collective-permute-start(bf16[264,1536]{1,0:T(8,128)(2,1)} %get-tuple-element.1569), channel_id=1, source_target_pairs={{0,4},{1,5},{2,6},{3,7},{4,0},{5,1},{6,2},{7,3},{8,12},{9,13},{10,... | collective-permute-start | bytes 2433032 | tf_op jit(solution)/shard_map/ppermute | solution.py:571
  608.4 28.2 %collective-permute-start.101 = (bf16[256,2048]{1,0:T(8,128)(2,1)}, bf16[256,2048]{1,0:T(8,128)(2,1)}, u32[]{:S(2)}, u32[]{:S(2)}) collective-permute-start(bf16[256,2048]{1,0:T(8,128)(2,1)} %get-tuple-element.1572), channel_id=1, source_target_pairs={{0,2},{1,3},{2,0},{3,1},{4,6},{5,7},{6,4},{7,5},{8,10},{9,11},{10,... | collective-permute-start | bytes 3145736 | tf_op jit(solution)/shard_map/ppermute | solution.py:571
  609.6 27.0 %collective-permute-start.102 = (bf16[2,64,1056]{2,1,0:T(8,128)(2,1)}, bf16[2,64,1056]{2,1,0:T(8,128)(2,1)}, u32[]{:S(2)}, u32[]{:S(2)}) collective-permute-start(bf16[2,64,1056]{2,1,0:T(8,128)(2,1)} %dynamic-slice_bitcast_fusion.24), channel_id=1, source_target_pairs={{0,4},{1,5},{2,6},{3,7},{4,0},{5,1},{6,2},{7,3},{8,12},{9,13},{10,... | collective-permute-start | bytes 811016 | tf_op jit(solution)/shard_map/ppermute | solution.py:571
  636.6 28.1 %collective-permute-start.105 = (bf16[264,1536]{1,0:T(8,128)(2,1)S(1)}, bf16[264,1536]{1,0:T(8,128)(2,1)S(1)}, u32[]{:S(2)}, u32[]{:S(2)}) collective-permute-start(bf16[264,1536]{1,0:T(8,128)(2,1)S(1)} %copy-done.79), channel_id=1, source_target_pairs={{0,4},{1,5},{2,6},{3,7},{4,0},{5,1},{6,2},{7,3},{8,12},{9,13},{10,... | collective-permute-start | bytes 2433032 | tf_op jit(solution)/shard_map/ppermute | solution.py:571
  637.9 26.9 %collective-permute-start.106 = (bf16[192,2048]{1,0:T(8,128)(2,1)S(1)}, bf16[192,2048]{1,0:T(8,128)(2,1)S(1)}, u32[]{:S(2)}, u32[]{:S(2)}) collective-permute-start(bf16[192,2048]{1,0:T(8,128)(2,1)S(1)} %copy-done.80), channel_id=1, source_target_pairs={{0,2},{1,3},{2,0},{3,1},{4,6},{5,7},{6,4},{7,5},{8,10},{9,11},{10,... | collective-permute-start | bytes 2359304 | tf_op jit(solution)/shard_map/ppermute | solution.py:571
  (238 other events, 2937.0 us)

commit v5 on v4

--- a/solution.py
+++ b/solution.py
@@ -918,7 +918,7 @@
 
     wo_sums = {}
     wo_pair(1, 2)
-    behind_rows = 8
+    behind_rows = 16
     panel_shape = (n_exp, n_fsdp * rows_w + behind_rows, 3 * wide)
     grad_lin, grad_normed_one, gain_one_part, panel = attend(
         normed_seq, wqkv, bias, tables, seq, (keep, arrived, qkv_seq), core_place, panel_shape)

time: 718 us -> 721 us (level)
    unnamed x291 -> x295, local copies, waits for them, and re-layouts: 15.1 us -> 15 us
where the time goes in v5:
time: 721 us; the launch traced here: 711 us
  waiting for transfers between devices  218 us (30%)
  Pallas kernels  186 us (26%)
  local copies, waits for them, and re-layouts  106 us (15%)
  starting transfers between devices  96.8 us (13%)
  other arithmetic  92.6 us (13%)
  matrix products  8.6 us (1%)
    ppermute x117, waiting for transfers between devices, send(): return lax.ppermute(value, ALL, ring_perm(MOVES[link]))  218 us
    ppermute x117, starting transfers between devices, send(): return lax.ppermute(value, ALL, ring_perm(MOVES[link]))  96.8 us
    pallas_call x4, Pallas kernels, feed(): pl.pallas_call(functools.partial(feed_kernel, experts, shared), in_specs=...  88.3 us
    pallas_call x5, Pallas kernels, weight_grads(): pl.pallas_call(functools.partial(weights_kernel, n_sets, split), grid=(n_...  64.1 us
    dynamic_update_slice x15, local copies, waits for them, and re-layouts, put(): return lax.dynamic_update_index_in_dim(value, block, place, axis)  20 us
    pallas_call x1, Pallas kernels, attend(): pl.pallas_call(functools.partial(attend_back_kernel, heads, seq, scale, s...  18.7 us
    squeeze x21, local copies, waits for them, and re-layouts, pick(): return lax.dynamic_index_in_dim(value, place, axis, keepdims=False)  18.5 us
    unnamed x295, local copies, waits for them, and re-layouts  15 us
  transfers between devices with their start and end apart: 117, of which 38 were waited for; matrix products, arithmetic and copies ran while one was open for 22% of the time, Pallas kernels for 26%

profile of v5, /device:TPU:0, one launch (start us, length us, event | category | flops | bytes accessed | tf_op | source)
XLA Modules:
  0.0 711.4 jit_solution(16471441566618657787)
XLA Ops:
  39.8 17.9 %collective-permute-done.6 = bf16[256,2048]{1,0:T(8,128)(2,1)} collective-permute-done((bf16[256,2048]{1,0:T(8,128)(2,1)S(1)}, bf16[256,2048]{1,0:T(8,128)(2,1)}, u32[]{:S(2)}, u32[]{:S(2)}) %collective-permute-start.6) | collective-permute-done | bytes 1048608 | tf_op jit(solution)/shard_map/ppermute | solution.py:571
  71.1 10.9 %collective-permute-done.12 = bf16[256,2048]{1,0:T(8,128)(2,1)} collective-permute-done((bf16[256,2048]{1,0:T(8,128)(2,1)}, bf16[256,2048]{1,0:T(8,128)(2,1)}, u32[]{:S(2)}, u32[]{:S(2)}) %collective-permute-start.12) | collective-permute-done | bytes 1048608 | tf_op jit(solution)/shard_map/ppermute | solution.py:571
  116.5 7.4 %collective-permute-done.23 = bf16[2,2,64,1056]{3,2,1,0:T(8,128)(2,1)S(1)} collective-permute-done((bf16[2,2,64,1056]{3,2,1,0:T(8,128)(2,1)S(1)}, bf16[2,2,64,1056]{3,2,1,0:T(8,128)(2,1)S(1)}, u32[]{:S(2)}, u32[]{:S(2)}) %collective-permute-start.23) | collective-permute-done | bytes 540704 | tf_op jit(solution)/shard_map/ppermute | solution.py:571
  123.8 9.8 %collective-permute-done.24 = bf16[2,2,64,1056]{3,2,1,0:T(8,128)(2,1)S(1)} collective-permute-done((bf16[2,2,64,1056]{3,2,1,0:T(8,128)(2,1)S(1)}, bf16[2,2,64,1056]{3,2,1,0:T(8,128)(2,1)S(1)}, u32[]{:S(2)}, u32[]{:S(2)}) %collective-permute-start.24) | collective-permute-done | bytes 540704 | tf_op jit(solution)/shard_map/ppermute | solution.py:571
  142.5 8.9 %attend.1 = (bf16[512,1536]{1,0:T(8,128)(2,1)S(1)}, bf16[512,256]{1,0:T(8,128)(2,1)S(1)}, bf16[512,256]{1,0:T(8,128)(2,1)S(1)}) custom-call(bf16[512,2048]{1,0:T(8,128)(2,1)S(1)} %bitcast.329, bf16[2048,2048]{1,0:T(8,128)(2,1)} %bitcast.75.w_ref, f32[1,1536]{1,0:T(1,128)S(1)} %fusion.46.bias_ref, f32[256,128]{1,0:T(8,128)S(1)} %get-tuple-element.878.cos_ref, ...), custom_call_target="tpu_custom_call" | custom-call | flops 100000000 | bytes 1000000 | tf_op jit(solution)/shard_map/attend/pallas_call | solution.py:215
  157.9 7.3 %collective-permute-done.28.refs_4_.refs_1_ = bf16[128,2176]{1,0:T(8,128)(2,1)S(1)} collective-permute-done((bf16[128,2176]{1,0:T(8,128)(2,1)}, bf16[128,2176]{1,0:T(8,128)(2,1)S(1)}, u32[]{:S(2)}, u32[]{:S(2)}) %collective-permute-start.28) | collective-permute-done | bytes 557088 | tf_op jit(solution)/shard_map/ppermute | solution.py:571
  180.9 9.5 %collective-permute-done.31 = bf16[2,64,1056]{2,1,0:T(8,128)(2,1)S(1)} collective-permute-done((bf16[2,64,1056]{2,1,0:T(8,128)(2,1)S(1)}, bf16[2,64,1056]{2,1,0:T(8,128)(2,1)S(1)}, u32[]{:S(2)}, u32[]{:S(2)}) %collective-permute-start.31) | collective-permute-done | bytes 270368 | tf_op jit(solution)/shard_map/ppermute | solution.py:571
  190.3 12.9 %collective-permute-done.33.refs_2_ = bf16[1056,512]{1,0:T(8,128)(2,1)S(1)} collective-permute-done((bf16[1056,512]{1,0:T(8,128)(2,1)S(1)}, bf16[1056,512]{1,0:T(8,128)(2,1)S(1)}, u32[]{:S(2)}, u32[]{:S(2)}) %collective-permute-start.33) | collective-permute-done | bytes 1081376 | tf_op jit(solution)/shard_map/ppermute | solution.py:571
  240.2 8.6 %collective-permute-done.40.refs_3_.refs_6_ = bf16[128,2176]{1,0:T(8,128)(2,1)S(1)} collective-permute-done((bf16[128,2176]{1,0:T(8,128)(2,1)}, bf16[128,2176]{1,0:T(8,128)(2,1)S(1)}, u32[]{:S(2)}, u32[]{:S(2)}) %collective-permute-start.40) | collective-permute-done | bytes 557088 | tf_op jit(solution)/shard_map/ppermute | solution.py:571
  260.8 8.1 %collective-permute-done.45.refs_0_.refs_6_ = bf16[128,2048]{1,0:T(8,128)(2,1)} collective-permute-done((bf16[128,2048]{1,0:T(8,128)(2,1)S(1)}, bf16[128,2048]{1,0:T(8,128)(2,1)}, u32[]{:S(2)}, u32[]{:S(2)}) %collective-permute-start.45) | collective-permute-done | bytes 524320 | tf_op jit(solution)/shard_map/ppermute | solution.py:571
  277.0 22.0 %feed.4 = (bf16[512,384]{1,0:T(8,128)(2,1)}, bf16[512,384]{1,0:T(8,128)(2,1)}, bf16[512,384]{1,0:T(8,128)(2,1)}, bf16[512,768]{1,0:T(8,128)(2,1)}, bf16[512,768]...) custom-call(s32[1]{0:T(128)} %bitcast.117.expert_ref, ...), custom_call_target="tpu_custom_call" | custom-call | flops 16000000000 | bytes 30000000 | tf_op jit(solution)/shard_map/feed/pallas_call | solution.py:326
  303.8 22.0 %feed.5 = (bf16[512,384]{1,0:T(8,128)(2,1)}, bf16[512,384]{1,0:T(8,128)(2,1)}, bf16[512,384]{1,0:T(8,128)(2,1)}, bf16[512,768]{1,0:T(8,128)(2,1)}, bf16[512,768]...) custom-call(s32[1]{0:T(128)} %bitcast.117.expert_ref, ...), custom_call_target="tpu_custom_call" | custom-call | flops 16000000000 | bytes 30000000 | tf_op jit(solution)/shard_map/feed/pallas_call | solution.py:326
  331.8 22.2 %feed.6 = (bf16[512,384]{1,0:T(8,128)(2,1)}, bf16[512,384]{1,0:T(8,128)(2,1)}, bf16[512,384]{1,0:T(8,128)(2,1)}, bf16[512,768]{1,0:T(8,128)(2,1)}, bf16[512,768]...) custom-call(s32[1]{0:T(128)} %bitcast.117.expert_ref, ...), custom_call_target="tpu_custom_call" | custom-call | flops 16000000000 | bytes 30000000 | tf_op jit(solution)/shard_map/feed/pallas_call | solution.py:326
  359.5 22.0 %feed.7 = (bf16[512,384]{1,0:T(8,128)(2,1)}, bf16[512,384]{1,0:T(8,128)(2,1)}, bf16[512,384]{1,0:T(8,128)(2,1)}, bf16[512,768]{1,0:T(8,128)(2,1)}, bf16[512,768]...) custom-call(s32[1]{0:T(128)} %bitcast.117.expert_ref, ...), custom_call_target="tpu_custom_call" | custom-call | flops 16000000000 | bytes 30000000 | tf_op jit(solution)/shard_map/feed/pallas_call | solution.py:326
  391.4 13.3 %weight_grads.5 = (bf16[384,1024]{1,0:T(8,128)(2,1)}, bf16[384,1024]{1,0:T(8,128)(2,1)}, bf16[384,1024]{1,0:T(8,128)(2,1)}, bf16[384,1024]{1,0:T(8,128)(2,1)}) custom-call(s32[1]{0:T(128)} %bitcast.105.y_ref, bf16[128,2048]{1,0:T(8,128)(2,1)} %copy-done.34, bf16[128,2048]{1,0:T(8,128)(2,1)} %copy-done.111, ...), custom_call_target="tpu_custom_call" | custom-call | flops 8000000000 | bytes 20000000 | tf_op jit(solution)/shard_map/weight_grads/pallas_call | solution.py:502
  418.7 9.5 %weight_grads.6 = (bf16[384,1024]{1,0:T(8,128)(2,1)}, bf16[384,1024]{1,0:T(8,128)(2,1)}) custom-call(s32[1]{0:T(128)} %bitcast.105.y_ref, bf16[128,2176]{1,0:T(8,128)(2,1)} %fusion.26.refs_3_.refs_0_, bf16[128,2176]{1,0:T(8,128)(2,1)} %copy-done.90, bf16[256,2176]{1,0:T(8,128)(2,1)} %collective-permute-done.37.refs_5_.refs_2_, ...), custom_call_target="tpu_custom_call" | custom-call | flops 4000000000 | bytes 20000000 | tf_op jit(solution)/shard_map/weight_grads/pallas_call | solution.py:502
  441.0 13.8 %weight_grads.7 = (bf16[352,2048]{1,0:T(8,128)(2,1)}, bf16[176,2048]{1,0:T(8,128)(2,1)}, bf16[176,2048]{1,0:T(8,128)(2,1)}) custom-call(s32[1]{0:T(128)} %bitcast.105.y_ref, bf16[128,2176]{1,0:T(8,128)(2,1)} %fusion.26.refs_3_.refs_0_, bf16[128,2176]{1,0:T(8,128)(2,1)} %copy-done.90, bf16[256,2176]{1,0:T(8,128)(2,1)} %collective-permute-done.37.refs_5_.refs_2_, ...), custom_call_target="tpu_custom_call" | custom-call | flops 8000000000 | bytes 20000000 | tf_op jit(solution)/shard_map/weight_grads/pallas_call | solution.py:502
  507.8 9.6 %collective-permute-done.87 = bf16[128,2048]{1,0:T(8,128)(2,1)S(1)} collective-permute-done((bf16[128,2048]{1,0:T(8,128)(2,1)S(1)}, bf16[128,2048]{1,0:T(8,128)(2,1)S(1)}, u32[]{:S(2)}, u32[]{:S(2)}) %collective-permute-start.87) | collective-permute-done | bytes 524320 | tf_op jit(solution)/shard_map/ppermute | solution.py:571
  522.5 18.7 %attend_back.1 = (bf16[512,1536]{1,0:T(8,128)(2,1)S(1)}, f32[512,2048]{1,0:T(8,128)}, f32[1,2048]{1,0:T(1,128)S(1)}, bf16[8,272,1536]{2,1,0:T(8,128)(2,1)}) custom-call(bf16[512,256]{1,0:T(8,128)(2,1)S(1)} %get-tuple-element.1436.grad_ref, bf16[512,256]{1,0:T(8,128)(2,1)S(1)} %bitcast.338, bf16[512,1536]{1,0:T(8,128)(2,1)S(1)} %copy-done.7, ...), custom_call_target="tpu_custom_call" | custom-call | flops 100000000 | bytes 1000000 | tf_op jit(solution)/shard_map/attend_back/pallas_call | solution.py:231
  559.6 13.7 %weight_grads.8 = (bf16[352,2048]{1,0:T(8,128)(2,1)}, bf16[256,2048]{1,0:T(8,128)(2,1)}, bf16[96,2048]{1,0:T(8,128)(2,1)}) custom-call(s32[1]{0:T(128)} %bitcast.105.y_ref, bf16[128,2048]{1,0:T(8,128)(2,1)} %copy-done.34, bf16[128,2048]{1,0:T(8,128)(2,1)} %copy-done.111, bf16[256,2048]{1,0:T(8,128)(2,1)} %collective-permute-done.43.refs_2_, ...), custom_call_target="tpu_custom_call" | custom-call | flops 8000000000 | bytes 20000000 | tf_op jit(solution)/shard_map/weight_grads/pallas_call | solution.py:502
  585.4 13.8 %weight_grads.9 = (bf16[352,2048]{1,0:T(8,128)(2,1)}, bf16[96,2048]{1,0:T(8,128)(2,1)}, bf16[256,2048]{1,0:T(8,128)(2,1)}) custom-call(s32[1]{0:T(128)} %bitcast.105.y_ref, bf16[128,2048]{1,0:T(8,128)(2,1)} %copy-done.34, bf16[128,2048]{1,0:T(8,128)(2,1)} %copy-done.111, bf16[256,2048]{1,0:T(8,128)(2,1)} %collective-permute-done.43.refs_2_, ...), custom_call_target="tpu_custom_call" | custom-call | flops 8000000000 | bytes 20000000 | tf_op jit(solution)/shard_map/weight_grads/pallas_call | solution.py:502
  622.1 16.3 %collective-permute-done.104 = bf16[64,2048]{1,0:T(8,128)(2,1)} collective-permute-done((bf16[64,2048]{1,0:T(8,128)(2,1)}, bf16[64,2048]{1,0:T(8,128)(2,1)}, u32[]{:S(2)}, u32[]{:S(2)}) %collective-permute-start.104) | collective-permute-done | bytes 262176 | tf_op jit(solution)/shard_map/ppermute | solution.py:571
  647.2 19.6 %collective-permute-done.109 = bf16[64,2048]{1,0:T(8,128)(2,1)S(1)} collective-permute-done((bf16[64,2048]{1,0:T(8,128)(2,1)S(1)}, bf16[64,2048]{1,0:T(8,128)(2,1)S(1)}, u32[]{:S(2)}, u32[]{:S(2)}) %collective-permute-start.109) | collective-permute-done | bytes 262176 | tf_op jit(solution)/shard_map/ppermute | solution.py:571
  678.2 10.5 %collective-permute-done.113 = bf16[2,64,1056]{2,1,0:T(8,128)(2,1)S(1)} collective-permute-done((bf16[2,64,1056]{2,1,0:T(8,128)(2,1)S(1)}, bf16[2,64,1056]{2,1,0:T(8,128)(2,1)S(1)}, u32[]{:S(2)}, u32[]{:S(2)}) %collective-permute-start.113) | collective-permute-done | bytes 270368 | tf_op jit(solution)/shard_map/ppermute | solution.py:571
  (800 shorter events, 379.2 us)
Async XLA Ops:
  103.9 29.7 %collective-permute-start.21 = (bf16[256,2048]{1,0:T(8,128)(2,1)}, bf16[256,2048]{1,0:T(8,128)(2,1)S(1)}, u32[]{:S(2)}, u32[]{:S(2)}) collective-permute-start(bf16[256,2048]{1,0:T(8,128)(2,1)} %collective-permute-done.16), channel_id=1, source_target_pairs={{0,4},{1,5},{2,6},{3,7},{4,0},{5,1},{6,2},{7,3},{8,12},{9,13},{10,... | collective-permute-start | bytes 3145736 | tf_op jit(solution)/shard_map/ppermute | solution.py:571
  105.2 28.4 %collective-permute-start.22 = (bf16[264,2048]{1,0:T(8,128)(2,1)S(1)}, bf16[264,2048]{1,0:T(8,128)(2,1)S(1)}, u32[]{:S(2)}, u32[]{:S(2)}) collective-permute-start(bf16[264,2048]{1,0:T(8,128)(2,1)S(1)} %copy-done.63), channel_id=1, source_target_pairs={{0,2},{1,3},{2,0},{3,1},{4,6},{5,7},{6,4},{7,5},{8,10},{9,11},{10,... | collective-permute-start | bytes 3244040 | tf_op jit(solution)/shard_map/ppermute | solution.py:571
  133.7 31.5 %collective-permute-start.25 = (bf16[264,2048]{1,0:T(8,128)(2,1)}, bf16[264,2048]{1,0:T(8,128)(2,1)}, u32[]{:S(2)}, u32[]{:S(2)}) collective-permute-start(bf16[264,2048]{1,0:T(8,128)(2,1)} %get-tuple-element.869), channel_id=1, source_target_pairs={{0,2},{1,3},{2,0},{3,1},{4,6},{5,7},{6,4},{7,5},{8,10},{9,11},{10,... | collective-permute-start | bytes 3244040 | tf_op jit(solution)/shard_map/ppermute | solution.py:571
  269.4 29.6 %collective-permute-start.48 = (bf16[128,2048]{1,0:T(8,128)(2,1)}, bf16[128,2048]{1,0:T(8,128)(2,1)}, u32[]{:S(2)}, u32[]{:S(2)}) collective-permute-start(bf16[128,2048]{1,0:T(8,128)(2,1)} %collective-permute-done.45.refs_0_.refs_6_), channel_id=1, source_target_pairs={{0,8},{1,9},{2,10},{3,11},{4,12},{5,13},{6,14},{7,15},{8,16},{9,17... | collective-permute-start | bytes 1572872 | tf_op jit(solution)/shard_map/ppermute | solution.py:571
  270.8 28.2 %collective-permute-start.50 = (bf16[128,2048]{1,0:T(8,128)(2,1)}, bf16[128,2048]{1,0:T(8,128)(2,1)S(1)}, u32[]{:S(2)}, u32[]{:S(2)}) collective-permute-start(bf16[128,2048]{1,0:T(8,128)(2,1)} %collective-permute-done.45.refs_0_.refs_6_), channel_id=1, source_target_pairs={{0,4},{1,5},{2,6},{3,7},{4,0},{5,1},{6,2},{7,3},{8,12},{9,13},{10,... | collective-permute-start | bytes 1572872 | tf_op jit(solution)/shard_map/ppermute | solution.py:571
  271.9 27.1 %collective-permute-start.49 = (bf16[128,2176]{1,0:T(8,128)(2,1)}, bf16[128,2176]{1,0:T(8,128)(2,1)S(1)}, u32[]{:S(2)}, u32[]{:S(2)}) collective-permute-start(bf16[128,2176]{1,0:T(8,128)(2,1)} %copy-done.92), channel_id=1, source_target_pairs={{0,8},{1,9},{2,10},{3,11},{4,12},{5,13},{6,14},{7,15},{8,16},{9,17... | collective-permute-start | bytes 1671176 | tf_op jit(solution)/shard_map/ppermute | solution.py:571
  301.0 27.2 %collective-permute-start.52 = (bf16[256,2048]{1,0:T(8,128)(2,1)S(1)}, bf16[256,2048]{1,0:T(8,128)(2,1)}, u32[]{:S(2)}, u32[]{:S(2)}) collective-permute-start(bf16[256,2048]{1,0:T(8,128)(2,1)S(1)} %pad_maximum_fusion.15), channel_id=1, source_target_pairs={{0,1},{1,0},{2,3},{3,2},{4,5},{5,4},{6,7},{7,6},{8,9},{9,8},{10,11... | collective-permute-start | bytes 3145736 | tf_op jit(solution)/shard_map/ppermute | solution.py:571
  301.6 26.6 %collective-permute-start.53 = (bf16[256,2176]{1,0:T(8,128)(2,1)S(1)}, bf16[256,2176]{1,0:T(8,128)(2,1)}, u32[]{:S(2)}, u32[]{:S(2)}) collective-permute-start(bf16[256,2176]{1,0:T(8,128)(2,1)S(1)} %pad_maximum_fusion.11), channel_id=1, source_target_pairs={{0,1},{1,0},{2,3},{3,2},{4,5},{5,4},{6,7},{7,6},{8,9},{9,8},{10,11... | collective-permute-start | bytes 3342344 | tf_op jit(solution)/shard_map/ppermute | solution.py:571
  329.5 27.3 %collective-permute-start.57 = (bf16[256,2048]{1,0:T(8,128)(2,1)S(1)}, bf16[256,2048]{1,0:T(8,128)(2,1)}, u32[]{:S(2)}, u32[]{:S(2)}) collective-permute-start(bf16[256,2048]{1,0:T(8,128)(2,1)S(1)} %pad_maximum_fusion.16), channel_id=1, source_target_pairs={{0,1},{1,0},{2,3},{3,2},{4,5},{5,4},{6,7},{7,6},{8,9},{9,8},{10,11... | collective-permute-start | bytes 3145736 | tf_op jit(solution)/shard_map/ppermute | solution.py:571
  330.1 26.8 %collective-permute-start.58 = (bf16[256,2176]{1,0:T(8,128)(2,1)S(1)}, bf16[256,2176]{1,0:T(8,128)(2,1)}, u32[]{:S(2)}, u32[]{:S(2)}) collective-permute-start(bf16[256,2176]{1,0:T(8,128)(2,1)S(1)} %pad_maximum_fusion.12), channel_id=1, source_target_pairs={{0,1},{1,0},{2,3},{3,2},{4,5},{5,4},{6,7},{7,6},{8,9},{9,8},{10,11... | collective-permute-start | bytes 3342344 | tf_op jit(solution)/shard_map/ppermute | solution.py:571
  356.8 29.7 %collective-permute-start.62 = (bf16[256,2176]{1,0:T(8,128)(2,1)}, bf16[256,2176]{1,0:T(8,128)(2,1)S(1)}, u32[]{:S(2)}, u32[]{:S(2)}) collective-permute-start(bf16[256,2176]{1,0:T(8,128)(2,1)} %get-tuple-element.1096), channel_id=1, source_target_pairs={{0,1},{1,0},{2,3},{3,2},{4,5},{5,4},{6,7},{7,6},{8,9},{9,8},{10,11... | collective-permute-start | bytes 3342344 | tf_op jit(solution)/shard_map/ppermute | solution.py:571
  357.4 26.9 %collective-permute-start.63 = (bf16[128,2176]{1,0:T(8,128)(2,1)S(1)}, bf16[128,2176]{1,0:T(8,128)(2,1)S(1)}, u32[]{:S(2)}, u32[]{:S(2)}) collective-permute-start(bf16[128,2176]{1,0:T(8,128)(2,1)S(1)} %convert_add_fusion.10), channel_id=1, source_target_pairs={{0,4},{1,5},{2,6},{3,7},{4,0},{5,1},{6,2},{7,3},{8,12},{9,13},{10,... | collective-permute-start | bytes 1671176 | tf_op jit(solution)/shard_map/ppermute | solution.py:571
  358.3 26.9 %collective-permute-start.64 = (bf16[256,2048]{1,0:T(8,128)(2,1)}, bf16[256,2048]{1,0:T(8,128)(2,1)S(1)}, u32[]{:S(2)}, u32[]{:S(2)}) collective-permute-start(bf16[256,2048]{1,0:T(8,128)(2,1)} %get-tuple-element.1113), channel_id=1, source_target_pairs={{0,1},{1,0},{2,3},{3,2},{4,5},{5,4},{6,7},{7,6},{8,9},{9,8},{10,11... | collective-permute-start | bytes 3145736 | tf_op jit(solution)/shard_map/ppermute | solution.py:571
  517.4 30.7 %collective-permute-start.88 = (bf16[176,2048]{1,0:T(8,128)(2,1)S(1)}, bf16[176,2048]{1,0:T(8,128)(2,1)S(1)}, u32[]{:S(2)}, u32[]{:S(2)}) collective-permute-start(bf16[176,2048]{1,0:T(8,128)(2,1)S(1)} %copy-done.143), channel_id=1, source_target_pairs={{0,2},{1,3},{2,0},{3,1},{4,6},{5,7},{6,4},{7,5},{8,10},{9,11},{10,... | collective-permute-start | bytes 2162696 | tf_op jit(solution)/shard_map/ppermute | solution.py:571
  551.5 28.9 %collective-permute-start.91 = (bf16[2,2,64,2048]{3,2,0,1:T(8,128)(2,1)S(1)}, bf16[2,2,64,2048]{3,2,0,1:T(8,128)(2,1)S(1)}, u32[]{:S(2)}, u32[]{:S(2)}) collective-permute-start(bf16[2,2,64,2048]{3,2,0,1:T(8,128)(2,1)S(1)} %fusion.13), channel_id=1, source_target_pairs={{0,1},{1,0},{2,3},{3,2},{4,5},{5,4},{6,7},{7,6},{8,9},{9,8},{10,11... | collective-permute-start | bytes 3145736 | tf_op jit(solution)/shard_map/ppermute | solution.py:571
  551.6 29.6 %collective-permute-start.92 = (bf16[176,2048]{1,0:T(8,128)(2,1)}, bf16[176,2048]{1,0:T(8,128)(2,1)S(1)}, u32[]{:S(2)}, u32[]{:S(2)}) collective-permute-start(bf16[176,2048]{1,0:T(8,128)(2,1)} %get-tuple-element.1485), channel_id=1, source_target_pairs={{0,2},{1,3},{2,0},{3,1},{4,6},{5,7},{6,4},{7,5},{8,10},{9,11},{10,... | collective-permute-start | bytes 2162696 | tf_op jit(solution)/shard_map/ppermute | solution.py:571
  552.6 28.2 %collective-permute-start.93 = (bf16[2,2,64,1056]{3,2,1,0:T(8,128)(2,1)}, bf16[2,2,64,1056]{3,2,1,0:T(8,128)(2,1)S(1)}, u32[]{:S(2)}, u32[]{:S(2)}) collective-permute-start(bf16[2,2,64,1056]{3,2,1,0:T(8,128)(2,1)} %get-tuple-element.1487), channel_id=1, source_target_pairs={{0,8},{1,9},{2,10},{3,11},{4,12},{5,13},{6,14},{7,15},{8,16},{9,17... | collective-permute-start | bytes 1622024 | tf_op jit(solution)/shard_map/ppermute | solution.py:571
  552.6 28.5 %collective-permute-start.94 = (bf16[2,2,64,1056]{3,2,1,0:T(8,128)(2,1)}, bf16[2,2,64,1056]{3,2,1,0:T(8,128)(2,1)}, u32[]{:S(2)}, u32[]{:S(2)}) collective-permute-start(bf16[2,2,64,1056]{3,2,1,0:T(8,128)(2,1)} %get-tuple-element.1489), channel_id=1, source_target_pairs={{0,24},{1,25},{2,26},{3,27},{4,28},{5,29},{6,30},{7,31},{8,0},{9,1... | collective-permute-start | bytes 1622024 | tf_op jit(solution)/shard_map/ppermute | solution.py:571
  581.7 26.7 %collective-permute-start.96 = (bf16[2,64,2048]{2,1,0:T(8,128)(2,1)S(1)}, bf16[2,64,2048]{2,1,0:T(8,128)(2,1)S(1)}, u32[]{:S(2)}, u32[]{:S(2)}) collective-permute-start(bf16[2,64,2048]{2,1,0:T(8,128)(2,1)S(1)} %fusion.28), channel_id=1, source_target_pairs={{0,2},{1,3},{2,0},{3,1},{4,6},{5,7},{6,4},{7,5},{8,10},{9,11},{10,... | collective-permute-start | bytes 1572872 | tf_op jit(solution)/shard_map/ppermute | solution.py:571
  608.4 29.9 %collective-permute-start.100 = (bf16[272,1536]{1,0:T(8,128)(2,1)}, bf16[272,1536]{1,0:T(8,128)(2,1)}, u32[]{:S(2)}, u32[]{:S(2)}) collective-permute-start(bf16[272,1536]{1,0:T(8,128)(2,1)} %get-tuple-element.1569), channel_id=1, source_target_pairs={{0,4},{1,5},{2,6},{3,7},{4,0},{5,1},{6,2},{7,3},{8,12},{9,13},{10,... | collective-permute-start | bytes 2506760 | tf_op jit(solution)/shard_map/ppermute | solution.py:571
  609.6 28.8 %collective-permute-start.101 = (bf16[256,2048]{1,0:T(8,128)(2,1)}, bf16[256,2048]{1,0:T(8,128)(2,1)}, u32[]{:S(2)}, u32[]{:S(2)}) collective-permute-start(bf16[256,2048]{1,0:T(8,128)(2,1)} %get-tuple-element.1572), channel_id=1, source_target_pairs={{0,2},{1,3},{2,0},{3,1},{4,6},{5,7},{6,4},{7,5},{8,10},{9,11},{10,... | collective-permute-start | bytes 3145736 | tf_op jit(solution)/shard_map/ppermute | solution.py:571
  610.6 27.8 %collective-permute-start.102 = (bf16[2,64,1056]{2,1,0:T(8,128)(2,1)}, bf16[2,64,1056]{2,1,0:T(8,128)(2,1)}, u32[]{:S(2)}, u32[]{:S(2)}) collective-permute-start(bf16[2,64,1056]{2,1,0:T(8,128)(2,1)} %dynamic-slice_bitcast_fusion.24), channel_id=1, source_target_pairs={{0,4},{1,5},{2,6},{3,7},{4,0},{5,1},{6,2},{7,3},{8,12},{9,13},{10,... | collective-permute-start | bytes 811016 | tf_op jit(solution)/shard_map/ppermute | solution.py:571
  638.4 28.4 %collective-permute-start.105 = (bf16[272,1536]{1,0:T(8,128)(2,1)S(1)}, bf16[272,1536]{1,0:T(8,128)(2,1)S(1)}, u32[]{:S(2)}, u32[]{:S(2)}) collective-permute-start(bf16[272,1536]{1,0:T(8,128)(2,1)S(1)} %copy-done.78), channel_id=1, source_target_pairs={{0,4},{1,5},{2,6},{3,7},{4,0},{5,1},{6,2},{7,3},{8,12},{9,13},{10,... | collective-permute-start | bytes 2506760 | tf_op jit(solution)/shard_map/ppermute | solution.py:571
  639.4 27.4 %collective-permute-start.106 = (bf16[192,2048]{1,0:T(8,128)(2,1)S(1)}, bf16[192,2048]{1,0:T(8,128)(2,1)S(1)}, u32[]{:S(2)}, u32[]{:S(2)}) collective-permute-start(bf16[192,2048]{1,0:T(8,128)(2,1)S(1)} %copy-done.79), channel_id=1, source_target_pairs={{0,2},{1,3},{2,0},{3,1},{4,6},{5,7},{6,4},{7,5},{8,10},{9,11},{10,... | collective-permute-start | bytes 2359304 | tf_op jit(solution)/shard_map/ppermute | solution.py:571
  (240 other events, 2920.5 us)
